TPU v7x, 32 devices: a whole 2x2x4 slice. The times are simulated.
32 devices in a mesh: band: 8 (over y, x, core), samp: 4 (over z).
Axes of the slice: x: 2, y: 2, z: 4, core: 2. Of those that a mesh axis runs over, the one named last changes fastest.
Arguments:
- tokens: bfloat16 [4, 1024, 1024], P('samp', 'band'), may hold values from -6 to 6
- cotangent: bfloat16 [4, 1024, 1024], P('samp', 'band'), may hold values from -6 to 6
- w_qkv: bfloat16 [1024, 3072], P(('band', 'samp')), may hold values from -0.25 to 0.25
- w_out: bfloat16 [1024, 1024], P(('band', 'samp')), may hold values from -0.375 to 0.375
- w_up: bfloat16 [1024, 4096], P(('band', 'samp')), may hold values from -0.1875 to 0.1875
- w_down: bfloat16 [4096, 1024], P(('band', 'samp')), may hold values from -0.1875 to 0.1875
- up_bias: bfloat16 [4096], P(('band', 'samp')), may hold values from -3 to 3
- norm_gains: bfloat16 [2, 1024], P(None, ('band', 'samp')), may hold values from 0.099609375 to 1.8984375
- shift_rows: bfloat16 [6, 1024], P(None, ('band', 'samp')), may hold values from -3 to 3
- lead_weight: bfloat16 [2, 1024], P(None, ('band', 'samp')), may hold values from -3 to 3
- lead_steps: int32 [4], P('samp'), may hold values from 0 to 28
- valid_cells: int32 [4, 1024], P('samp', 'band'), may hold values from 0 to 4, as said below
Outputs:
- output: bfloat16 [4, 1024, 1024], P('samp', 'band')
- input_grad: bfloat16 [4, 1024, 1024], P('samp', 'band')
- grad_qkv: float32 [1024, 3072], P(('band', 'samp'))
- grad_out: float32 [1024, 1024], P(('band', 'samp'))
- grad_up: float32 [1024, 4096], P(('band', 'samp'))
- grad_down: float32 [4096, 1024], P(('band', 'samp'))
- grad_up_bias: float32 [4096], P(('band', 'samp'))
- grad_gains: float32 [2, 1024], P(None, ('band', 'samp'))
- grad_shifts: float32 [6, 1024], P(None, ('band', 'samp'))
- grad_lead: float32 [2, 1024], P(None, ('band', 'samp'))
Inputs may be any that keep to these rules, and one draw needn't show every extreme that they name: `valid_cells`: each entry counts the valid cells among a patch's 4 cells; a patch with none is masked as a key. Each sample's first and last patches are valid.
All inputs are finite; a program needn't handle non-finite values.
Results may differ from a plain program's by a relative error of at most 0.015.
Values may be sent and summed in bfloat16 or wider, within the bound.
A program may use at most 320 MiB of HBM per device.

v0:
```python
import jax
import jax.numpy as jnp
from jax import lax
from jax.sharding import PartitionSpec as P

HEADS = 16


eps = 1e-05
masked = 10000.0


def layer_norm(values, gain_row, shift_row):
    centered = values - jnp.mean(values, axis=-1, keepdims=True)
    variance = jnp.mean(centered * centered, axis=-1, keepdims=True)
    return centered * lax.rsqrt(variance + eps) * gain_row + shift_row


def gelu_exact(values):
    return jax.nn.gelu(values, approximate=False)


def body(
    tokens,
    cotangent,
    w_qkv,
    w_out,
    w_up,
    w_down,
    up_bias,
    norm_gains,
    shift_rows,
    lead_weight,
    lead_steps,
    valid_cells,
):
    whole = (
        lax.all_gather(w_qkv, ("band", "samp"), axis=0, tiled=True),
        lax.all_gather(w_out, ("band", "samp"), axis=0, tiled=True),
        lax.all_gather(w_up, ("band", "samp"), axis=0, tiled=True),
        lax.all_gather(w_down, ("band", "samp"), axis=0, tiled=True),
        lax.all_gather(up_bias, ("band", "samp"), axis=0, tiled=True),
        lax.all_gather(norm_gains, ("band", "samp"), axis=1, tiled=True),
        lax.all_gather(shift_rows, ("band", "samp"), axis=1, tiled=True),
        lax.all_gather(lead_weight, ("band", "samp"), axis=1, tiled=True),
    )
    qkv_full = whole[0]
    out_full = whole[1]
    up_full = whole[2]
    down_full = whole[3]
    up_shift = whole[4].astype(jnp.float32)
    gain_all = whole[5].astype(jnp.float32)
    shift_all = whole[6].astype(jnp.float32)
    lead_all = whole[7].astype(jnp.float32)
    row_count = tokens.shape[1]
    width = tokens.shape[2]
    head_count = HEADS
    head_size = width // head_count
    score_scale = head_size ** (-0.5)
    lead_days = lead_steps[0].astype(jnp.float32) * 0.25
    entering = tokens[0].astype(jnp.float32) + lead_days * lead_all[0] + lead_all[1]
    normed, norm_first_back = jax.vjp(layer_norm, entering, gain_all[0], shift_all[0])
    normed_low = normed.astype(jnp.bfloat16)
    project = jnp.dot(normed_low, qkv_full, preferred_element_type=jnp.float32)
    queries = (project[:, :width] + shift_all[1]).astype(jnp.bfloat16)
    key_rows = project[:, width : 2 * width].astype(jnp.bfloat16)
    value_rows = (project[:, 2 * width :] + shift_all[2]).astype(jnp.bfloat16)
    key_open = (valid_cells[0] > 0).astype(jnp.bfloat16)
    keys_all, values_all, open_all = (
        lax.all_gather(key_rows, "band", axis=0, tiled=True),
        lax.all_gather(value_rows, "band", axis=0, tiled=True),
        lax.all_gather(key_open, "band", axis=0, tiled=True),
    )
    seq_total = keys_all.shape[0]
    block_rows = min(512, seq_total)
    block_count = seq_total // block_rows
    block_ids = jnp.arange(block_count)
    bias_all = (open_all.astype(jnp.float32) - 1.0) * masked
    query_heads = queries.reshape(row_count, head_count, head_size)

    def block_keys(step_index):
        first_row = step_index * block_rows
        key_block = lax.dynamic_slice_in_dim(keys_all, first_row, block_rows, 0).reshape(
            block_rows, head_count, head_size
        )
        value_block = lax.dynamic_slice_in_dim(values_all, first_row, block_rows, 0).reshape(
            block_rows, head_count, head_size
        )
        bias_block = lax.dynamic_slice_in_dim(bias_all, first_row, block_rows, 0)
        scores = (
            jnp.einsum("qhe,khe->hqk", query_heads, key_block, preferred_element_type=jnp.float32)
            * score_scale
            + bias_block
        )
        return (scores, key_block, value_block)

    def max_step(running, step_index):
        row_max, exp_total = running
        scores = block_keys(step_index)[0]
        new_max = jnp.maximum(row_max, jnp.max(scores, axis=-1))
        exp_total = exp_total * jnp.exp(row_max - new_max) + jnp.sum(
            jnp.exp(scores - new_max[..., None]), axis=-1
        )
        return ((new_max, exp_total), None)

    start_max = jnp.full((head_count, row_count), -jnp.inf, jnp.float32)
    start_total = jnp.zeros((head_count, row_count), jnp.float32)
    row_max, exp_total = lax.scan(max_step, (start_max, start_total), block_ids)[0]
    log_total = row_max + jnp.log(exp_total)

    def out_step(running, step_index):
        scores, key_block, value_block = block_keys(step_index)
        weights_low = jnp.exp(scores - log_total[..., None]).astype(jnp.bfloat16)
        return (
            running
            + jnp.einsum(
                "hqk,khe->qhe", weights_low, value_block, preferred_element_type=jnp.float32
            ),
            None,
        )

    attended_heads = lax.scan(
        out_step, jnp.zeros((row_count, head_count, head_size), jnp.float32), block_ids
    )[0]
    attended_low = attended_heads.reshape(row_count, width).astype(jnp.bfloat16)
    middle = (
        entering
        + jnp.dot(attended_low, out_full, preferred_element_type=jnp.float32)
        + shift_all[3]
    )
    second, norm_second_back = jax.vjp(layer_norm, middle, gain_all[1], shift_all[4])
    second_low = second.astype(jnp.bfloat16)
    hidden_pre = jnp.dot(second_low, up_full, preferred_element_type=jnp.float32) + up_shift
    hidden, gelu_back = jax.vjp(gelu_exact, hidden_pre)
    hidden_low = hidden.astype(jnp.bfloat16)
    result = (
        middle + jnp.dot(hidden_low, down_full, preferred_element_type=jnp.float32) + shift_all[5]
    )
    output = result.astype(jnp.bfloat16)
    grad_result = cotangent[0]
    grad_result_f = grad_result.astype(jnp.float32)
    grad_down_w = jnp.einsum(
        "tf,td->fd", hidden_low, grad_result, preferred_element_type=jnp.float32
    )
    grad_shift_down = jnp.sum(grad_result_f, axis=0)
    grad_hidden = jnp.einsum(
        "td,fd->tf", grad_result, down_full, preferred_element_type=jnp.float32
    )
    grad_pre_low = gelu_back(grad_hidden)[0].astype(jnp.bfloat16)
    grad_up_w = jnp.einsum(
        "td,tf->df", second_low, grad_pre_low, preferred_element_type=jnp.float32
    )
    grad_up_shift = jnp.sum(grad_pre_low.astype(jnp.float32), axis=0)
    grad_second = jnp.einsum("tf,df->td", grad_pre_low, up_full, preferred_element_type=jnp.float32)
    grad_middle_norm, grad_gain_second, grad_shift_second = norm_second_back(grad_second)
    grad_middle = grad_result_f + grad_middle_norm
    ffn_sums = (
        lax.psum_scatter(grad_up_w, ("band", "samp"), scatter_dimension=0, tiled=True),
        lax.psum_scatter(grad_down_w, ("band", "samp"), scatter_dimension=0, tiled=True),
        lax.psum_scatter(grad_up_shift, ("band", "samp"), scatter_dimension=0, tiled=True),
    )
    grad_branch = grad_middle.astype(jnp.bfloat16)
    grad_shift_out = jnp.sum(grad_branch.astype(jnp.float32), axis=0)
    grad_out_w = jnp.einsum(
        "td,te->de", attended_low, grad_branch, preferred_element_type=jnp.float32
    )
    grad_attended = jnp.einsum(
        "te,de->td", grad_branch, out_full, preferred_element_type=jnp.float32
    ).astype(jnp.bfloat16)
    grad_heads = grad_attended.reshape(row_count, head_count, head_size)
    delta = jnp.einsum("qhe,qhe->hq", grad_heads.astype(jnp.float32), attended_heads)
    zero_heads = jnp.zeros((row_count, head_count, head_size), jnp.float32)

    def key_grad_step(g_queries, step_index):
        scores, key_block, value_block = block_keys(step_index)
        weights_full = jnp.exp(scores - log_total[..., None])
        g_weights = jnp.einsum(
            "qhe,khe->hqk", grad_heads, value_block, preferred_element_type=jnp.float32
        )
        g_scores = (weights_full * (g_weights - delta[..., None])).astype(jnp.bfloat16)
        g_queries = (
            g_queries
            + jnp.einsum("hqk,khe->qhe", g_scores, key_block, preferred_element_type=jnp.float32)
            * score_scale
        )
        key_term = (
            jnp.einsum("hqk,qhe->khe", g_scores, query_heads, preferred_element_type=jnp.float32)
            * score_scale
        )
        value_term = jnp.einsum(
            "hqk,qhe->khe",
            weights_full.astype(jnp.bfloat16),
            grad_heads,
            preferred_element_type=jnp.float32,
        )
        return (
            g_queries,
            (key_term.reshape(block_rows, width), value_term.reshape(block_rows, width)),
        )

    grad_query_heads, block_terms = lax.scan(key_grad_step, zero_heads, block_ids)
    grad_query_f = grad_query_heads.reshape(row_count, width)
    key_sum, value_sum = (
        lax.psum_scatter(
            block_terms[0].reshape(seq_total, width), "band", scatter_dimension=0, tiled=True
        ),
        lax.psum_scatter(
            block_terms[1].reshape(seq_total, width), "band", scatter_dimension=0, tiled=True
        ),
    )
    grad_query_low = grad_query_f.astype(jnp.bfloat16)
    grad_key_low = key_sum.astype(jnp.bfloat16)
    grad_value_low = value_sum.astype(jnp.bfloat16)
    grad_project = jnp.concatenate([grad_query_low, grad_key_low, grad_value_low], axis=-1)
    grad_qkv_w = jnp.einsum(
        "td,te->de", normed_low, grad_project, preferred_element_type=jnp.float32
    )
    grad_shift_query = jnp.sum(grad_query_low.astype(jnp.float32), axis=0)
    grad_shift_value = jnp.sum(grad_value_low.astype(jnp.float32), axis=0)
    grad_normed = jnp.einsum(
        "te,de->td", grad_project, qkv_full, preferred_element_type=jnp.float32
    )
    grad_entering_norm, grad_gain_first, grad_shift_first = norm_first_back(grad_normed)
    grad_entering = grad_middle + grad_entering_norm
    input_grad = grad_entering.astype(jnp.bfloat16)
    entering_sum = jnp.sum(grad_entering, axis=0)
    grad_lead_rows = jnp.stack([lead_days * entering_sum, entering_sum])
    grad_gain_rows = jnp.stack([grad_gain_first, grad_gain_second])
    grad_shift_stack = jnp.stack(
        [
            grad_shift_first,
            grad_shift_query,
            grad_shift_value,
            grad_shift_out,
            grad_shift_second,
            grad_shift_down,
        ]
    )
    attention_sums = (
        lax.psum_scatter(grad_qkv_w, ("band", "samp"), scatter_dimension=0, tiled=True),
        lax.psum_scatter(grad_out_w, ("band", "samp"), scatter_dimension=0, tiled=True),
        lax.psum_scatter(grad_gain_rows, ("band", "samp"), scatter_dimension=1, tiled=True),
        lax.psum_scatter(grad_shift_stack, ("band", "samp"), scatter_dimension=1, tiled=True),
        lax.psum_scatter(grad_lead_rows, ("band", "samp"), scatter_dimension=1, tiled=True),
    )
    return (
        output[None],
        input_grad[None],
        attention_sums[0],
        attention_sums[1],
        ffn_sums[0],
        ffn_sums[1],
        ffn_sums[2],
        attention_sums[2],
        attention_sums[3],
        attention_sums[4],
    )


def solution(mesh):
    return jax.shard_map(
        body,
        mesh=mesh,
        in_specs=(
            P("samp", "band", None),
            P("samp", "band", None),
            P(("band", "samp"), None),
            P(("band", "samp"), None),
            P(("band", "samp"), None),
            P(("band", "samp"), None),
            P(("band", "samp")),
            P(None, ("band", "samp")),
            P(None, ("band", "samp")),
            P(None, ("band", "samp")),
            P("samp"),
            P("samp", "band"),
        ),
        out_specs=(
            P("samp", "band", None),
            P("samp", "band", None),
            P(("band", "samp"), None),
            P(("band", "samp"), None),
            P(("band", "samp"), None),
            P(("band", "samp"), None),
            P(("band", "samp")),
            P(None, ("band", "samp")),
            P(None, ("band", "samp")),
            P(None, ("band", "samp")),
        ),
        check_vma=False,
    )
```

profile of v0, /device:TPU:0, one launch (start us, length us, event | category | flops | bytes accessed | tf_op | source)
XLA Modules:
  0.0 2110.7 jit_solution(3205998705367314178)
XLA Ops:
  8.6 69.7 %all-gather.2 = bf16[32,32,2]{1,2,0:T(2,128)(2,1)S(1)} all-gather(bf16[1,32,2]{1,2,0:T(2,128)(2,1)} %bitcast.278), channel_id=1, replica_groups=mesh['band'=8,'samp'=4] {'band','samp'}, dimensions={0}, use_global_device_ids=true | all-gather | bytes 4224 | tf_op jit(solution)/shard_map/all_gather | solution.py:43
  78.4 63.2 %all-gather.1 = bf16[32,32,2]{1,2,0:T(2,128)(2,1)S(1)} all-gather(bf16[1,32,2]{1,2,0:T(2,128)(2,1)} %bitcast.279), channel_id=1, replica_groups=mesh['band'=8,'samp'=4] {'band','samp'}, dimensions={0}, use_global_device_ids=true | all-gather | bytes 4224 | tf_op jit(solution)/shard_map/all_gather | solution.py:45
  141.7 66.2 %all-gather.3 = bf16[32,32,6]{1,2,0:T(8,128)(2,1)S(1)} all-gather(bf16[1,32,6]{1,2,0:T(8,128)(2,1)} %bitcast.277), channel_id=1, replica_groups=mesh['band'=8,'samp'=4] {'band','samp'}, dimensions={0}, use_global_device_ids=true | all-gather | bytes 12672 | tf_op jit(solution)/shard_map/all_gather | solution.py:44
  209.1 1.2 fusion.40
  210.9 4.0 fusion.57
  218.4 63.0 %all-gather.4 = bf16[32,1,128]{2,1,0:T(2,128)(2,1)S(1)} all-gather(bf16[1,1,128]{2,1,0:T(2,128)(2,1)S(1)} %bitcast.280), channel_id=1, replica_groups=mesh['band'=8,'samp'=4] {'band','samp'}, dimensions={0}, use_global_device_ids=true | all-gather | bytes 8448 | tf_op jit(solution)/shard_map/all_gather | solution.py:42
  281.5 8.2 all-gather
  290.0 3.9 copy.76
  293.9 2.9 copy.77
  296.8 6.9 while.39
  303.7 14.7 while.40
  305.1 2.4 constant_dynamic-slice_fusion.10
  307.5 3.5 fusion.126
  312.3 2.4 constant_dynamic-slice_fusion.10
  314.8 3.7 fusion.126
  319.5 10.3 all-gather.18.cloned.1.call-done
  329.8 2.1 fusion.67
  332.2 76.7 %all-gather.20.cloned.1.call-done = bf16[1024,4096]{1,0:T(8,128)(2,1)} async-done(((bf16[32,4096]{1,0:T(8,128)(2,1)}), bf16[1024,4096]{1,0:T(8,128)(2,1)}) %all-gather.20.cloned.1.call-update) | async-done | bytes 8388624 | tf_op jit(solution)/shard_map/all_gather | solution.py:40
  408.9 6.1 convolution_add_fusion
  415.0 72.7 %all-gather.22.cloned.1.call-done = bf16[4096,1024]{1,0:T(8,128)(2,1)} async-done(((bf16[128,1024]{1,0:T(8,128)(2,1)}), bf16[4096,1024]{1,0:T(8,128)(2,1)}) %all-gather.22.cloned.1.call-update) | async-done | bytes 8388624 | tf_op jit(solution)/shard_map/all_gather | solution.py:41
  487.7 10.1 convert_reduce_fusion
  497.8 3.0 multiply_reduce_fusion
  502.7 1.6 convolution_convert_fusion
  504.2 1.1 copy.78
  505.3 1.1 fusion.42
  506.5 38.1 %while.41 = (s32[]{:T(128)}, f32[128,16,64]{0,2,1:T(8,128)}, f32[2,512,1024]{2,1,0:T(8,128)}, f32[2,512,1024]{2,1,0:T(8,128)}, s32[2]{0:T(128)S(1)}, /*index=5*/...) while((s32[]{:T(128)}, f32[128,16,64]{0,2,1:T(8,128)}, ...), condition=%wide.region_13.14_spmd.clone, body=%wide.region_12.13_spmd.clone.sunk | while | flops 682491904 | bytes 70287712 | solution.py:201
  507.9 1.3 constant_dynamic-slice_fusion.12
  510.2 1.6 multiply_convert_fusion.5
  511.8 1.2 fusion.139
  513.7 2.1 convolution_multiply_fusion.3
  515.8 2.9 copy.128
  518.8 1.8 copy.127
  520.6 4.9 constant_dynamic-update-slice_fusion.3
  527.0 1.3 constant_dynamic-slice_fusion.12
  529.2 1.6 multiply_convert_fusion.5
  530.8 1.2 fusion.139
  532.7 2.1 convolution_multiply_fusion.3
  534.8 2.9 copy.128
  537.8 1.8 copy.127
  539.6 4.9 constant_dynamic-update-slice_fusion.3
  544.5 5.3 copy.84
  550.0 5.4 copy.82
  556.6 43.3 %reduce-scatter.18.cloned.1.call-done = f32[128,1024]{0,1:T(8,128)} async-done(((f32[1024,1024]{0,1:T(8,128)}), f32[128,1024]{0,1:T(8,128)}) %reduce-scatter.18.cloned.1.call-update) | async-done | bytes 524304 | tf_op jit(solution)/shard_map/reduce_scatter | solution.py:207
  600.0 1.2 convert_reduce_fusion.3
  601.2 53.8 %reduce-scatter.16.cloned.1.call-done = f32[128,1024]{0,1:T(8,128)} async-done(((f32[1024,1024]{0,1:T(8,128)}), f32[128,1024]{0,1:T(8,128)}) %reduce-scatter.16.cloned.1.call-update) | async-done | bytes 524304 | tf_op jit(solution)/shard_map/reduce_scatter | solution.py:204
  656.2 5.1 fusion.61
  666.3 2.6 fusion.69
  669.0 6.4 fusion.44
  675.5 1.5 copy-done.14
  677.0 9.7 fusion.46
  686.8 1.2 copy-done.11
  688.0 8.2 fusion.60
  696.2 39.9 %all-reduce = f32[4096]{0:T(1024)S(1)} all-reduce(f32[4096]{0:T(1024)S(1)} %get-tuple-element.479), channel_id=9, replica_groups=mesh['band'=8,'samp'=4] {'band','samp'}, use_global_device_ids=true, to_apply=%region_23.24.clone | all-reduce | flops 4096 | bytes 32768
  736.6 8.6 fusion.25
  745.3 53.3 %reduce-scatter.32.cloned.1.call-done = f32[32,2]{1,0:T(8,128)} async-done(((f32[1024,2]{1,0:T(8,128)}), f32[32,2]{1,0:T(8,128)}) %reduce-scatter.32.cloned.1.call-update) | async-done | bytes 272
  798.5 1.4 copy.98
  799.9 131.6 %reduce-scatter.28.cloned.1.call-done = f32[32,2]{1,0:T(8,128)} async-done(((f32[1024,2]{1,0:T(8,128)}), f32[32,2]{1,0:T(8,128)}) %reduce-scatter.28.cloned.1.call-update) | async-done | bytes 272
  931.5 1.4 copy.94
  932.9 131.7 %reduce-scatter.30.cloned.1.call-done = f32[32,6]{1,0:T(8,128)} async-done(((f32[1024,6]{1,0:T(8,128)}), f32[32,6]{1,0:T(8,128)}) %reduce-scatter.30.cloned.1.call-update) | async-done | bytes 784
  1064.5 1.4 copy.96
  1065.9 144.9 %reduce-scatter.22.cloned.1.call-done = f32[32,1024]{1,0:T(8,128)} async-done(((f32[1024,1024]{1,0:T(8,128)}), f32[32,1024]{1,0:T(8,128)}) %reduce-scatter.22.cloned.1.call-update) | async-done | bytes 131088 | tf_op jit(solution)/shard_map/reduce_scatter | solution.py:241
  1210.8 162.1 %reduce-scatter.20.cloned.1.call-done = f32[32,3072]{1,0:T(8,128)} async-done(((f32[1024,3072]{1,0:T(8,128)}), f32[32,3072]{1,0:T(8,128)}) %reduce-scatter.20.cloned.1.call-update) | async-done | bytes 393232 | tf_op jit(solution)/shard_map/reduce_scatter | solution.py:240
  1372.9 366.1 %reduce-scatter.26.cloned.1.call-done = f32[128,1024]{1,0:T(8,128)} async-done(((f32[4096,1024]{1,0:T(8,128)}), f32[128,1024]{1,0:T(8,128)}) %reduce-scatter.26.cloned.1.call-update) | async-done | bytes 524304 | tf_op jit(solution)/shard_map/reduce_scatter | solution.py:159
  1739.0 364.9 %reduce-scatter.24.cloned.1.call-done = f32[32,4096]{1,0:T(8,128)} async-done(((f32[1024,4096]{1,0:T(8,128)}), f32[32,4096]{1,0:T(8,128)}) %reduce-scatter.24.cloned.1.call-update) | async-done | bytes 524304 | tf_op jit(solution)/shard_map/reduce_scatter | solution.py:158
  (164 shorter events, 29.1 us)
Async XLA Ops:
  7.2 203.7 %all-gather.12.cloned.1.call-start = ((), (), s32[]{:S(2)}) async-start(), calls=%async_computation.9 | async-start | bytes 6488064 | tf_op jit(solution)/shard_map/all_gather | solution.py:38
  7.9 282.0 %all-gather.14.cloned.1.call-start = ((), (), s32[]{:S(2)}) async-start(), calls=%async_computation.10 | async-start | bytes 2359296 | tf_op jit(solution)/shard_map/all_gather | solution.py:71
  214.9 3.5 copy-start.20
  214.9 66.6 %copy-start.21 = (s32[1,128]{1,0:T(1,128)S(1)}, s32[1,128]{1,0:T(1,128)}, u32[]{:S(2)}) copy-start(s32[1,128]{1,0:T(1,128)} %param.29) | copy-start | bytes 1540
  215.8 78.1 %all-gather.16.cloned.1.call-start = ((), (), s32[]{:S(2)}) async-start(), calls=%async_computation.11 | async-start | bytes 2359296 | tf_op jit(solution)/shard_map/all_gather | solution.py:70
  216.6 113.2 %all-gather.18.cloned.1.call-start = ((), (), s32[]{:S(2)}) async-start(), calls=%async_computation.12 | async-start | bytes 2162688 | tf_op jit(solution)/shard_map/all_gather | solution.py:39
  217.1 191.7 %all-gather.20.cloned.1.call-start = ((), (), s32[]{:S(2)}) async-start(), calls=%async_computation.13 | async-start | bytes 8650752 | tf_op jit(solution)/shard_map/all_gather | solution.py:40
  217.7 270.0 %all-gather.22.cloned.1.call-start = ((), (), s32[]{:S(2)}) async-start(), calls=%async_computation.14 | async-start | bytes 8650752 | tf_op jit(solution)/shard_map/all_gather | solution.py:41
  218.3 381.7 %reduce-scatter.18.cloned.1.call-start = ((), (), s32[]{:S(2)}) async-start(), calls=%async_computation.16 | async-start | bytes 4718592 | tf_op jit(solution)/shard_map/reduce_scatter | solution.py:207
  319.5 95.5 %copy-start.12 = (bf16[128,16,64]{0,2,1:T(8,128)(2,1)}, bf16[128,16,64]{0,2,1:T(8,128)(2,1)S(1)}, u32[]{:S(2)}) copy-start(bf16[128,16,64]{0,2,1:T(8,128)(2,1)S(1)} %convert_element_type.117) | copy-start | bytes 786436
  408.9 78.8 %copy-start.16 = (bf16[1,128,1024]{2,1,0:T(8,128)(2,1)S(1)}, bf16[1,128,1024]{2,1,0:T(8,128)(2,1)}, u32[]{:S(2)}) copy-start(bf16[1,128,1024]{2,1,0:T(8,128)(2,1)} %param.19) | copy-start | bytes 786436
  487.7 10.1 copy-start.2
  497.8 3.1 copy-start.10
  497.8 4.2 copy-start.17
  500.9 1.8 copy-start.7
  501.2 0.8 copy-start.8
  506.5 2.9 copy-start
  511.8 1.2 copy-start.3
  513.7 2.2 copy-start.4
  520.6 4.9 copy-start.1
  525.5 2.9 copy-start
  530.8 1.2 copy-start.3
  532.7 2.2 copy-start.4
  539.6 4.9 copy-start.1
  549.9 105.2 %reduce-scatter.16.cloned.1.call-start = ((), (), s32[]{:S(2)}) async-start(), calls=%async_computation.15 | async-start | bytes 4718592 | tf_op jit(solution)/shard_map/reduce_scatter | solution.py:204
  555.3 1.1 copy-start.5
  555.4 100.8 %copy-start.6 = (bf16[1,128,1024]{2,1,0:T(8,128)(2,1)S(1)}, bf16[1,128,1024]{2,1,0:T(8,128)(2,1)}, u32[]{:S(2)}) copy-start(bf16[1,128,1024]{2,1,0:T(8,128)(2,1)} %param.18) | copy-start | bytes 786436
  555.4 243.1 %reduce-scatter.32.cloned.1.call-start = ((), (), s32[]{:S(2)}) async-start(), calls=%async_computation.23 | async-start | bytes 540672
  656.2 5.6 copy-start.9
  656.2 5.6 copy-start.18
  662.8 3.5 copy-start.13
  663.9 267.6 %reduce-scatter.28.cloned.1.call-start = ((), (), s32[]{:S(2)}) async-start(), calls=%async_computation.21 | async-start | bytes 540672
  665.0 399.5 %reduce-scatter.30.cloned.1.call-start = ((), (), s32[]{:S(2)}) async-start(), calls=%async_computation.22 | async-start | bytes 540672
  666.2 544.6 %reduce-scatter.22.cloned.1.call-start = ((), (), s32[]{:S(2)}) async-start(), calls=%async_computation.18 | async-start | bytes 4325376 | tf_op jit(solution)/shard_map/reduce_scatter | solution.py:241
  668.9 704.0 %reduce-scatter.20.cloned.1.call-start = ((), (), s32[]{:S(2)}) async-start(), calls=%async_computation.17 | async-start | bytes 12976128 | tf_op jit(solution)/shard_map/reduce_scatter | solution.py:240
  675.4 1.6 copy-start.14
  675.5 1063.5 %reduce-scatter.26.cloned.1.call-start = ((), (), s32[]{:S(2)}) async-start(), calls=%async_computation.20 | async-start | bytes 17301504 | tf_op jit(solution)/shard_map/reduce_scatter | solution.py:159
  686.7 1.2 copy-start.11
  686.8 1417.1 %reduce-scatter.24.cloned.1.call-start = ((), (), s32[]{:S(2)}) async-start(), calls=%async_computation.19 | async-start | bytes 17301504 | tf_op jit(solution)/shard_map/reduce_scatter | solution.py:158
  696.1 40.5 %copy-start.15 = (f32[128,4096]{1,0:T(8,128)S(1)}, f32[128,4096]{1,0:T(8,128)}, u32[]{:S(2)}) copy-start(f32[128,4096]{1,0:T(8,128)} %convolution_add_fusion) | copy-start | bytes 6291460
  696.2 40.5 %copy-start.19 = (f32[1,1024]{1,0:T(1,128)S(1)}, f32[1,1024]{1,0:T(1,128)}, u32[]{:S(2)}) copy-start(f32[1,1024]{1,0:T(1,128)} %get-tuple-element.466) | copy-start | bytes 12292
Sparse Core Ops, SparseCore 0:
  10.9 72.2 all-gather.11
  215.9 24.1 all-gather.13
  242.5 27.8 all-gather.15
  273.3 56.5 all-gather.17
  332.6 76.2 all-gather.19
  411.7 75.9 all-gather.21
  550.0 49.9 reduce-scatter.17
  603.7 51.3 reduce-scatter.15
  664.0 134.4 reduce-scatter.31
  800.7 130.7 reduce-scatter.27
  933.7 130.7 reduce-scatter.29
  1067.3 143.4 reduce-scatter.21
  1218.4 154.4 reduce-scatter.19
  1375.7 363.2 reduce-scatter.25
  1741.7 362.1 reduce-scatter.23
where the time goes:
time: 2110 us
  waiting for transfers between devices  1610 us (76%)
  blocking collectives  310 us (15%)
  matrix products  89.8 us (4%)
  local copies, waits for them, and re-layouts  64.7 us (3%)
    reduce_scatter x1, waiting for transfers between devices, body(): lax.psum_scatter(grad_down_w, ('band', 'samp'), scatter_dimension=0, tile...  366 us
    reduce_scatter x1, waiting for transfers between devices, body(): lax.psum_scatter(grad_up_w, ('band', 'samp'), scatter_dimension=0, tiled=...  365 us
    unnamed x18, waiting for transfers between devices  319 us
    reduce_scatter x1, waiting for transfers between devices, body(): lax.psum_scatter(grad_qkv_w, ('band', 'samp'), scatter_dimension=0, tiled...  162 us
    reduce_scatter x1, waiting for transfers between devices, body(): lax.psum_scatter(grad_out_w, ('band', 'samp'), scatter_dimension=0, tiled...  145 us
    all_gather x1, waiting for transfers between devices, body(): lax.all_gather(w_up, ('band', 'samp'), axis=0, tiled=True)  76.7 us
    all_gather x1, waiting for transfers between devices, body(): lax.all_gather(w_down, ('band', 'samp'), axis=0, tiled=True)  72.7 us
    all_gather x1, blocking collectives, body(): lax.all_gather(norm_gains, ('band', 'samp'), axis=1, tiled=True)  69.7 us
  transfers between devices with their start and end apart: 15, of which 12 were waited for; matrix products, arithmetic and copies ran while one was open for 4% of the time, Pallas kernels for 0%

commit v1 on v0

--- a/solution.py
+++ b/solution.py
@@ -1,6 +1,8 @@
 import jax
 import jax.numpy as jnp
 from jax import lax
+from jax.experimental import pallas as pl
+from jax.experimental.pallas import tpu as pltpu
 from jax.sharding import PartitionSpec as P
 
 HEADS = 16
@@ -257,9 +259,727 @@
     )
 
 
+MESH = pl.DeviceIdType.MESH
+F32 = jnp.float32
+BF16 = jnp.bfloat16
+PLANE = 8
+DEPTH = 4
+ROWS = 128
+BLOCK = 256
+CHIPS = 4
+NN = (((1,), (0,)), ((), ()))
+NT = (((1,), (1,)), ((), ()))
+TN = (((0,), (0,)), ((), ()))
+INNER = 32
+
+
+def mm(left, right, dims=NN):
+    return lax.dot_general(left, right, dims, preferred_element_type=F32)
+
+
+def plane_kernel(
+    lead_ref, tok, cot, wqkv, wout, wup, wdown, vec_in,
+    out_o, ig_o, gqkv_o, gout_o, gup_o, gdown_o, vec_o,
+    agf, wq, wo, wu, wd, sq, su, ztr, vt, vecf, vrow,
+    normed, qaug, kaug, kt, vv, vt2, pst, ot, invl, att, gproj, dk, dv,
+    hid, gder, gpre, mid, gmid,
+    part, pr, cs, rr,
+    gds, gus, gqs, gos, gdr, gur, gqr, gor_, gu2, gq2, gua, gqa, goa,
+    acc, gub, vs, vsr, vz, vzr,
+    ag_s, ag_r, fw_s, fw_r, aq_s, aq_r, v_s, v_r, z_s, z_r, p_s, p_r, c_s, c_r,
+):
+    b = lax.axis_index("band")
+    s = lax.axis_index("samp")
+    c = b % 2
+    x = (b // 2) % 2
+    y = b // 4
+    mate = b + 1 - 2 * c
+    own = b // 2
+
+    def chip(r):
+        dx = r % 2
+        dy = r // 2
+        xx = x + dx * (1 - 2 * x)
+        yy = y + dy * (1 - 2 * y)
+        return yy * 2 + xx
+
+    def peer(k):
+        return (b + k) % PLANE
+
+    def level(k):
+        return (s + k) % DEPTH
+
+    barrier = pltpu.get_barrier_semaphore()
+    for k in range(1, PLANE):
+        pl.semaphore_signal(barrier, inc=1, device_id=(peer(k), s), device_id_type=MESH)
+    for k in range(1, DEPTH):
+        pl.semaphore_signal(barrier, inc=1, device_id=(b, level(k)), device_id_type=MESH)
+    pl.semaphore_wait(barrier, PLANE - 1 + DEPTH - 1)
+
+    def rc(src, dst, ss, rs, band, samp):
+        return pltpu.make_async_remote_copy(
+            src_ref=src, dst_ref=dst, send_sem=ss, recv_sem=rs,
+            device_id=(band, samp), device_id_type=MESH,
+        )
+
+    def zc(kind, k, src, dst):
+        return rc(src, dst, z_s.at[kind, k - 1], z_r.at[kind, k - 1], b, level(k))
+
+    def gather(op, r):
+        dst = mate if r == 0 else chip(r) * 2 + c
+        src = tok if op == 0 else (cot if op == 1 else agf.at[op, b])
+        return rc(src, agf.at[op, b], ag_s.at[op, r], ag_r.at[op, r], dst, s)
+
+    def forward(op, r):
+        blk = chip(r) * 2 + c
+        return rc(agf.at[op, blk], agf.at[op, blk], fw_s.at[op, r], fw_r.at[op, r], mate, s)
+
+    def start_gather(op):
+        for r in (1, 2, 3, 0):
+            gather(op, r).start()
+
+    def pass_on(op, rs):
+        for r in rs:
+            gather(op, r).wait_recv()
+            forward(op, r).start()
+
+    def block(op, q):
+        return agf[op, pl.ds(2 * q, 2)].reshape(BLOCK, -1)
+
+    def swap(kind, k, src, dst):
+        return rc(src, dst, aq_s.at[kind, k - 1], aq_r.at[kind, k - 1], peer(k), s)
+
+    start_gather(0)
+    for k in range(1, DEPTH):
+        zc(0, k, vec_in.at[0], ztr.at[k - 1]).start()
+    agf[0, b] = tok[...]
+    agf[1, b] = cot[...]
+    width = tok.shape[1]
+    for d in range(PLANE):
+        for j in range(3):
+            sq[d, :, j * 128:(j + 1) * 128] = wqkv[:, j * width + d * 128:j * width + (d + 1) * 128]
+    for k in range(1, PLANE):
+        swap(0, k, sq.at[peer(k)], wq.at[b, s]).start()
+    wq[b, s] = sq[b]
+    wo[s] = wout[...]
+    for k in range(1, DEPTH):
+        zc(1, k, wo.at[s], wo.at[s]).start()
+    for d in range(PLANE):
+        su[d] = wup[:, d * 512:(d + 1) * 512]
+    wu[b, s] = su[b]
+    wd[s] = wdown[...]
+
+    for k in range(1, DEPTH):
+        zc(0, k, vec_in.at[0], ztr.at[k - 1]).wait_recv()
+    vt[...] = (
+        vec_in[0].astype(F32) + vec_in[1].astype(F32)
+        + ztr[0].astype(F32) + ztr[1].astype(F32) + ztr[2].astype(F32)
+    ).astype(BF16)
+
+    def spread(k):
+        return rc(vt, vecf.at[b], v_s.at[0, k - 1], v_r.at[0, k - 1], peer(k), s)
+
+    for k in range(1, PLANE):
+        spread(k).start()
+    vecf[b] = vt[...]
+    for k in range(1, PLANE):
+        swap(0, k, sq.at[peer(k)], wq.at[b, s]).wait_recv()
+    for k in range(1, DEPTH):
+        zc(2, k, wq.at[:, s], wq.at[:, s]).start()
+    for k in range(1, PLANE):
+        swap(1, k, su.at[peer(k)], wu.at[b, s]).start()
+    for k in range(1, PLANE):
+        spread(k).wait_recv()
+    for d in range(PLANE):
+        vrow[:, d * 128:(d + 1) * 128] = vecf[d].astype(F32)
+    lead_days = lead_ref[0].astype(F32) * 0.25
+    lane = lax.broadcasted_iota(jnp.int32, (1, 128), 1)
+    head_lane = [(lane < 64).astype(F32), (lane >= 64).astype(F32)]
+    ones_lane = jnp.where(lane < 2, 1.0, 0.0).astype(F32)
+    ends_lane = jnp.where(lane == 0, 9984.0, jnp.where(lane == 1, 16.0, 0.0)).astype(F32)
+    gain1, gain2 = vrow[0:1, :], vrow[1:2, :]
+    shift1, shift_out, shift2, shift_down = vrow[2:3, :], vrow[5:6, :], vrow[6:7, :], vrow[7:8, :]
+    lead_row = lead_days * vrow[8:9, :] + vrow[9:10, :]
+    mine = vecf[b].astype(F32)
+
+    def stats(v):
+        mean = jnp.mean(v, axis=-1, keepdims=True)
+        centered = v - mean
+        variance = jnp.mean(centered * centered, axis=-1, keepdims=True)
+        rstd = lax.rsqrt(variance + eps)
+        return centered * rstd, rstd
+
+    for d in range(PLANE):
+        row = jnp.broadcast_to(vecf[d].astype(F32)[10:11, :], (128, 128))
+        column = row.T - 1.0
+        kaug[d * 128:(d + 1) * 128, 128:256] = (column * ends_lane).astype(BF16)
+    for h in range(2):
+        for q in range(CHIPS):
+            qaug[h, q, :, 128:256] = jnp.broadcast_to(ones_lane, (BLOCK, 128)).astype(BF16)
+
+    def norm_block(d):
+        def chunk(j, _):
+            rows = pl.ds(pl.multiple_of(j * INNER, INNER), INNER)
+            ent = agf[0, d, rows, :].astype(F32) + lead_row
+            xhat = stats(ent)[0]
+            normed[d, rows, :] = (xhat * gain1 + shift1).astype(BF16)
+            return 0
+
+        lax.fori_loop(0, ROWS // INNER, chunk, 0)
+
+    norm_block(b)
+    gather(0, 0).wait_recv()
+    norm_block(mate)
+    pass_on(0, (1, 2))
+    for r in (1, 2):
+        norm_block(chip(r) * 2 + c)
+        forward(0, r).wait_recv()
+        norm_block(chip(r) * 2 + 1 - c)
+    pass_on(0, (3,))
+    start_gather(1)
+    norm_block(chip(3) * 2 + c)
+    forward(0, 3).wait_recv()
+    norm_block(chip(3) * 2 + 1 - c)
+
+    for k in range(1, DEPTH):
+        zc(2, k, wq.at[:, s], wq.at[:, s]).wait_recv()
+    for k in range(1, PLANE):
+        swap(1, k, su.at[peer(k)], wu.at[b, s]).wait_recv()
+    for k in range(1, DEPTH):
+        zc(3, k, wu.at[:, s], wu.at[:, s]).start()
+    for k in range(1, DEPTH):
+        zc(4, k, wd.at[s], wd.at[s]).start()
+
+    def project_block(q, _):
+        rows = pl.ds(pl.multiple_of(q * BLOCK, BLOCK), BLOCK)
+        pj = mm(normed[pl.ds(2 * q, 2)].reshape(BLOCK, width), wq[...].reshape(width, 384))
+        qv = (pj[:, 0:128] + mine[3:4, :]).astype(BF16).astype(F32) * 0.125
+        for h in range(2):
+            qaug[h, q, :, 0:128] = (qv * head_lane[h]).astype(BF16)
+        kv = pj[:, 128:256].astype(BF16)
+        kaug[rows, 0:128] = kv
+        kt[:, rows] = kv.T
+        vb = (pj[:, 256:384] + mine[4:5, :]).astype(BF16)
+        vv[rows, :] = vb
+        vt2[:, rows] = vb.T
+        return 0
+
+    lax.fori_loop(0, CHIPS, project_block, 0)
+    for k in range(1, DEPTH):
+        zc(1, k, wo.at[s], wo.at[s]).wait_recv()
+
+    def mate_copy(op, slot, r):
+        return rc(part.at[slot, r, 1 - c], pr.at[op, r], p_s.at[op, r], p_r.at[op, r], mate, s)
+
+    def chip_copy(op, slot, r):
+        return rc(cs.at[slot, r], rr.at[op, r], c_s.at[op, r], c_r.at[op, r], chip(r) * 2 + c, s)
+
+    def put_part(op, slot, r, blk):
+        part[slot, r] = blk.astype(BF16).reshape(2, ROWS, width)
+        mate_copy(op, slot, r).start()
+
+    def fold(op, slot, r, send=True):
+        mate_copy(op, slot, r).wait_recv()
+
+        def chunk(j, _):
+            rows = pl.ds(pl.multiple_of(j * INNER, INNER), INNER)
+            cs[slot, r, rows, :] = (
+                part[slot, r, c, rows, :].astype(F32) + pr[op, r, rows, :].astype(F32)
+            ).astype(BF16)
+            return 0
+
+        lax.fori_loop(0, ROWS // INNER, chunk, 0)
+
+        if send:
+            @pl.when(r > 0)
+            def _():
+                chip_copy(op, slot, r).start()
+
+    def plane_total(op, slot, rows):
+        total = cs[slot, 0, rows, :].astype(F32)
+        for r in (1, 2, 3):
+            total = total + rr[op, r, rows, :].astype(F32)
+        return total
+
+    def end_sums(op, slot):
+        for r in range(CHIPS):
+            mate_copy(op, slot, r).wait_send()
+        for r in (1, 2, 3):
+            chip_copy(op, slot, r).wait_send()
+
+    def attend_block(i, _):
+        r = 3 - i
+        q = chip(r)
+
+        def head(h, _):
+            top = pl.ds(pl.multiple_of(h * 64, 64), 64)
+            st = mm(kaug[...], qaug[h, q], NT)
+            p = jnp.exp(st - jnp.max(st, axis=0, keepdims=True))
+            inverse = 1.0 / jnp.sum(p, axis=0, keepdims=True)
+            pb = p.astype(BF16)
+            pst[h, q] = pb
+            ot[q, top, :] = mm(vt2[top, :], pb) * inverse
+            invl[q, h] = jnp.broadcast_to(inverse, (8, BLOCK))
+            return 0
+
+        lax.fori_loop(0, 2, head, 0)
+        low = ot[q].T.astype(BF16)
+        att[q] = low
+        put_part(0, 0, r, mm(low, wo[...].reshape(128, width)))
+
+        @pl.when(i > 0)
+        def _():
+            fold(0, 0, r + 1)
+
+        return 0
+
+    lax.fori_loop(0, CHIPS, attend_block, 0)
+    fold(0, 0, 0)
+    pass_on(1, (1, 2, 3))
+    for r in (1, 2, 3):
+        chip_copy(0, 0, r).wait_recv()
+
+    def middle_chunk(j, _):
+        rows = pl.ds(pl.multiple_of(j * INNER, INNER), INNER)
+        ent = tok[rows, :].astype(F32) + lead_row
+        m = ent + plane_total(0, 0, rows) + shift_out
+        mid[rows, :] = m
+        agf[2, b, rows, :] = (stats(m)[0] * gain2 + shift2).astype(BF16)
+        return 0
+
+    lax.fori_loop(0, ROWS // INNER, middle_chunk, 0)
+    start_gather(2)
+    end_sums(0, 0)
+
+    for k in range(1, DEPTH):
+        zc(3, k, wu.at[:, s], wu.at[:, s]).wait_recv()
+    bias = jnp.concatenate([mine[11 + j:12 + j, :] for j in range(4)], axis=1)
+
+    def arrivals(op, i):
+        @pl.when(i == 0)
+        def _():
+            gather(op, 0).wait_recv()
+
+        @pl.when(i == 1)
+        def _():
+            pass_on(op, (1, 2))
+            forward(op, 1).wait_recv()
+
+        @pl.when(i == 2)
+        def _():
+            forward(op, 2).wait_recv()
+
+        @pl.when(i == 3)
+        def _():
+            pass_on(op, (3,))
+            forward(op, 3).wait_recv()
+
+    def up_block(i, _):
+        arrivals(2, i)
+        q = chip(i)
+        hp = mm(block(2, q), wu[...].reshape(width, 512)) + bias
+        phi = 0.5 + 0.5 * lax.erf(hp * 0.7071067811865476)
+        hid[pl.ds(pl.multiple_of(q * BLOCK, BLOCK), BLOCK), :] = (hp * phi).astype(BF16)
+        gder[q] = phi + hp * jnp.exp(hp * hp * -0.5) * 0.3989422804014327
+        return 0
+
+    lax.fori_loop(0, CHIPS, up_block, 0)
+    gather(1, 0).wait_recv()
+    for r in (1, 2, 3):
+        forward(1, r).wait_recv()
+
+    def down_grad(f, _):
+        cols = pl.ds(pl.multiple_of(f * BLOCK, BLOCK), BLOCK)
+        g = mm(hid[:, cols], agf[1].reshape(PLANE * ROWS, width), TN)
+        gds[pl.ds(2 * f, 2)] = g.astype(BF16).reshape(2, 128, width)
+        return 0
+
+    lax.fori_loop(0, 2, down_grad, 0)
+    for k in range(1, DEPTH):
+        zc(4, k, wd.at[s], wd.at[s]).wait_recv()
+    for k in range(1, DEPTH):
+        zc(5, k, gds.at[level(k)], gdr.at[k - 1]).start()
+    gub[...] = jnp.zeros_like(gub)
+
+    def back_block(i, _):
+        r = 3 - i
+        q = chip(r)
+        rows = pl.ds(pl.multiple_of(q * BLOCK, BLOCK), BLOCK)
+        gh = mm(block(1, q), wd[...].reshape(512, width), NT)
+        gp = (gder[q] * gh).astype(BF16)
+        gpre[rows, :] = gp
+        gub[...] += jnp.sum(gp.astype(F32).reshape(BLOCK // 8, 8, 512), axis=0)
+        put_part(1, 1, r, mm(gp, wu[...].reshape(width, 512), NT))
+
+        @pl.when(i > 0)
+        def _():
+            fold(1, 1, r + 1)
+
+        return 0
+
+    lax.fori_loop(0, CHIPS, back_block, 0)
+    fold(1, 1, 0)
+
+    def up_grad(f, _):
+        cols = pl.ds(pl.multiple_of(f * BLOCK, BLOCK), BLOCK)
+        g = mm(agf[2, :, :, cols].reshape(PLANE * ROWS, BLOCK), gpre[...], TN)
+        gus[pl.ds(2 * f, 2)] = g.astype(BF16).reshape(2, 4, 32, 512)
+        return 0
+
+    lax.fori_loop(0, CHIPS, up_grad, 0)
+    for k in range(1, DEPTH):
+        zc(6, k, gus.at[:, level(k)], gur.at[k - 1]).start()
+
+    def out_block(i, _):
+        r = 3 - i
+        q = chip(r)
+        rows = pl.ds(pl.multiple_of(q * BLOCK, BLOCK), BLOCK)
+        put_part(2, 2, r, mm(hid[rows, :], wd[...].reshape(512, width)))
+
+        @pl.when(i > 0)
+        def _():
+            fold(2, 2, r + 1, send=False)
+
+        return 0
+
+    lax.fori_loop(0, CHIPS, out_block, 0)
+    fold(2, 2, 0, send=False)
+
+    for r in (1, 2, 3):
+        chip_copy(1, 1, r).wait_recv()
+    acc[...] = jnp.zeros_like(acc)
+
+    def add_row(n, v):
+        acc[n] += jnp.sum(v.reshape(INNER // 8, 8, width), axis=0)
+
+    def norm_back(v, grad, gain):
+        xhat, rstd = stats(v)
+        d = grad * gain
+        mean_d = jnp.mean(d, axis=-1, keepdims=True)
+        mean_dx = jnp.mean(d * xhat, axis=-1, keepdims=True)
+        return rstd * (d - mean_d - xhat * mean_dx), xhat
+
+    def second_chunk(j, _):
+        rows = pl.ds(pl.multiple_of(j * INNER, INNER), INNER)
+        gs = plane_total(1, 1, rows)
+        g, xhat = norm_back(mid[rows, :], gs, gain2)
+        ct = cot[rows, :].astype(F32)
+        gm = ct + g
+        gmid[rows, :] = gm
+        gb = gm.astype(BF16)
+        agf[3, b, rows, :] = gb
+        add_row(1, gs * xhat)
+        add_row(6, gs)
+        add_row(5, gb.astype(F32))
+        add_row(7, ct)
+        return 0
+
+    lax.fori_loop(0, ROWS // INNER, second_chunk, 0)
+    start_gather(3)
+
+    dk[...] = jnp.zeros_like(dk)
+    dv[...] = jnp.zeros_like(dv)
+    goa[...] = jnp.zeros_like(goa)
+
+    def attend_back(i, _):
+        arrivals(3, i)
+        q = chip(i)
+        gbk = block(3, q)
+        wo_all = wo[...].reshape(128, width)
+        dot_t = mm(wo_all, gbk, NT)
+        inv = jnp.concatenate(
+            [jnp.broadcast_to(invl[q, h, 0:1, :], (64, BLOCK)) for h in range(2)], axis=0
+        )
+        dos = dot_t * inv
+        prod = dos * ot[q]
+        deltas = [jnp.sum(prod[h * 64:(h + 1) * 64], axis=0, keepdims=True) for h in range(2)]
+        do_rows = dos.T
+        zero = jnp.zeros((64, BLOCK), F32)
+        dq_parts = []
+        for h in range(2):
+            halves = [dos[0:64], zero] if h == 0 else [zero, dos[64:128]]
+            dp = mm(vv[...], jnp.concatenate(halves, axis=0).astype(BF16))
+            pb = pst[h, q]
+            ds = (pb.astype(F32) * (dp - deltas[h])).astype(BF16)
+            dv[...] += mm(pb, (do_rows * head_lane[h]).astype(BF16))
+            dk[...] += mm(ds, qaug[h, q, :, 0:128])
+            dq_parts.append(mm(kt[h * 64:(h + 1) * 64, :], ds))
+        dq = jnp.concatenate(dq_parts, axis=0).T * 0.125
+        gproj[pl.ds(pl.multiple_of(q * BLOCK, BLOCK), BLOCK), 0:128] = dq.astype(BF16)
+        goa[...] += mm(att[q], gbk, TN)
+        return 0
+
+    lax.fori_loop(0, CHIPS, attend_back, 0)
+    for r in (1, 2, 3):
+        chip_copy(2, 2, r).start()
+    gproj[:, 128:256] = dk[...].astype(BF16)
+    gproj[:, 256:384] = dv[...].astype(BF16)
+
+    def project_back(i, _):
+        r = 3 - i
+        q = chip(r)
+        rows = pl.ds(pl.multiple_of(q * BLOCK, BLOCK), BLOCK)
+        put_part(3, 0, r, mm(gproj[rows, :], wq[...].reshape(width, 384), NT))
+
+        @pl.when(i > 0)
+        def _():
+            fold(3, 0, r + 1)
+
+        return 0
+
+    lax.fori_loop(0, CHIPS, project_back, 0)
+    fold(3, 0, 0)
+
+    def qkv_grad(f, _):
+        cols = pl.ds(pl.multiple_of(f * BLOCK, BLOCK), BLOCK)
+        g = mm(normed[:, :, cols].reshape(PLANE * ROWS, BLOCK), gproj[...], TN)
+        gqs[pl.ds(2 * f, 2)] = g.astype(BF16).reshape(2, 4, 32, 384)
+        return 0
+
+    lax.fori_loop(0, CHIPS, qkv_grad, 0)
+    gos[...] = goa[...].astype(BF16).reshape(4, 32, width)
+    for k in range(1, DEPTH):
+        zc(7, k, gqs.at[:, level(k)], gqr.at[k - 1]).start()
+    for k in range(1, DEPTH):
+        zc(8, k, gos.at[level(k)], gor_.at[k - 1]).start()
+
+    for k in range(1, DEPTH):
+        zc(5, k, gds.at[level(k)], gdr.at[k - 1]).wait_recv()
+    gdown_o[...] = (
+        gds[s].astype(F32) + gdr[0].astype(F32) + gdr[1].astype(F32) + gdr[2].astype(F32)
+    )
+    for k in range(1, DEPTH):
+        zc(6, k, gus.at[:, level(k)], gur.at[k - 1]).wait_recv()
+    for d in range(PLANE):
+        gu2[d] = (
+            gus[d, s].astype(F32) + gur[0, d].astype(F32)
+            + gur[1, d].astype(F32) + gur[2, d].astype(F32)
+        ).astype(BF16)
+    for k in range(1, PLANE):
+        swap(2, k, gu2.at[peer(k)], gua.at[b]).start()
+    gua[b] = gu2[b]
+
+    for r in (1, 2, 3):
+        chip_copy(2, 2, r).wait_recv()
+
+    def output_chunk(j, _):
+        rows = pl.ds(pl.multiple_of(j * INNER, INNER), INNER)
+        out_o[rows, :] = (mid[rows, :] + plane_total(2, 2, rows) + shift_down).astype(BF16)
+        return 0
+
+    lax.fori_loop(0, ROWS // INNER, output_chunk, 0)
+
+    for r in (1, 2, 3):
+        chip_copy(3, 0, r).wait_recv()
+
+    def first_chunk(j, _):
+        rows = pl.ds(pl.multiple_of(j * INNER, INNER), INNER)
+        gn = plane_total(3, 0, rows)
+        g, xhat = norm_back(tok[rows, :].astype(F32) + lead_row, gn, gain1)
+        ge = gmid[rows, :] + g
+        ig_o[rows, :] = ge.astype(BF16)
+        add_row(0, gn * xhat)
+        add_row(2, gn)
+        add_row(9, ge)
+        return 0
+
+    lax.fori_loop(0, ROWS // INNER, first_chunk, 0)
+    acc[8] = acc[9] * lead_days
+
+    sums = [jnp.sum(acc[n], axis=0, keepdims=True) for n in range(10)]
+    packed = jnp.concatenate(sums + [jnp.zeros((6, width), F32)], axis=0)
+    for d in range(PLANE):
+        vs[d] = packed[:, d * 128:(d + 1) * 128]
+
+    def vec_swap(k):
+        return rc(vs.at[peer(k)], vsr.at[k - 1], v_s.at[1, k - 1], v_r.at[1, k - 1], peer(k), s)
+
+    for k in range(1, PLANE):
+        vec_swap(k).start()
+    gq_cols = jnp.sum(gproj[:, 0:128].astype(F32), axis=0, keepdims=True)
+    gv_cols = jnp.sum(gproj[:, 256:384].astype(F32), axis=0, keepdims=True)
+    gub_row = jnp.sum(gub[...], axis=0, keepdims=True)
+    extra = jnp.concatenate(
+        [jnp.zeros((3, 128), F32), gq_cols, gv_cols, jnp.zeros((6, 128), F32)]
+        + [gub_row[:, j * 128:(j + 1) * 128] for j in range(4)]
+        + [jnp.zeros((1, 128), F32)],
+        axis=0,
+    )
+    for k in range(1, PLANE):
+        vec_swap(k).wait_recv()
+    total = vs[b] + extra
+    for k in range(PLANE - 1):
+        total = total + vsr[k]
+    vz[...] = total
+    for k in range(1, DEPTH):
+        zc(9, k, vz, vzr.at[k - 1]).start()
+
+    for k in range(1, DEPTH):
+        zc(8, k, gos.at[level(k)], gor_.at[k - 1]).wait_recv()
+    gout_o[...] = (
+        gos[s].astype(F32) + gor_[0].astype(F32) + gor_[1].astype(F32) + gor_[2].astype(F32)
+    )
+    for k in range(1, DEPTH):
+        zc(7, k, gqs.at[:, level(k)], gqr.at[k - 1]).wait_recv()
+    for d in range(PLANE):
+        gq2[d] = (
+            gqs[d, s].astype(F32) + gqr[0, d].astype(F32)
+            + gqr[1, d].astype(F32) + gqr[2, d].astype(F32)
+        ).astype(BF16)
+    for k in range(1, PLANE):
+        swap(3, k, gq2.at[peer(k)], gqa.at[b]).start()
+    gqa[b] = gq2[b]
+    for k in range(1, PLANE):
+        swap(2, k, gu2.at[peer(k)], gua.at[b]).wait_recv()
+    for d in range(PLANE):
+        gup_o[:, d * 512:(d + 1) * 512] = gua[d].astype(F32)
+    for k in range(1, DEPTH):
+        zc(9, k, vz, vzr.at[k - 1]).wait_recv()
+    vec_o[...] = vz[...] + vzr[0] + vzr[1] + vzr[2]
+    for k in range(1, PLANE):
+        swap(3, k, gq2.at[peer(k)], gqa.at[b]).wait_recv()
+    for d in range(PLANE):
+        for j in range(3):
+            gqkv_o[:, j * width + d * 128:j * width + (d + 1) * 128] = (
+                gqa[d, :, j * 128:(j + 1) * 128].astype(F32)
+            )
+
+    for op in range(4):
+        for r in range(CHIPS):
+            gather(op, r).wait_send()
+        for r in (1, 2, 3):
+            forward(op, r).wait_send()
+    for op, slot in ((1, 1), (2, 2), (3, 0)):
+        end_sums(op, slot)
+    for k in range(1, PLANE):
+        swap(0, k, sq.at[peer(k)], wq.at[b, s]).wait_send()
+        swap(1, k, su.at[peer(k)], wu.at[b, s]).wait_send()
+        swap(2, k, gu2.at[peer(k)], gua.at[b]).wait_send()
+        swap(3, k, gq2.at[peer(k)], gqa.at[b]).wait_send()
+        spread(k).wait_send()
+        vec_swap(k).wait_send()
+    for k in range(1, DEPTH):
+        zc(0, k, vec_in.at[0], ztr.at[k - 1]).wait_send()
+        zc(1, k, wo.at[s], wo.at[s]).wait_send()
+        zc(2, k, wq.at[:, s], wq.at[:, s]).wait_send()
+        zc(3, k, wu.at[:, s], wu.at[:, s]).wait_send()
+        zc(4, k, wd.at[s], wd.at[s]).wait_send()
+        zc(5, k, gds.at[level(k)], gdr.at[k - 1]).wait_send()
+        zc(6, k, gus.at[:, level(k)], gur.at[k - 1]).wait_send()
+        zc(7, k, gqs.at[:, level(k)], gqr.at[k - 1]).wait_send()
+        zc(8, k, gos.at[level(k)], gor_.at[k - 1]).wait_send()
+        zc(9, k, vz, vzr.at[k - 1]).wait_send()
+
+
+def plane_body(
+    tokens, cotangent, w_qkv, w_out, w_up, w_down,
+    up_bias, norm_gains, shift_rows, lead_weight, lead_steps, valid_cells,
+):
+    s = lax.axis_index("samp")
+    width = tokens.shape[2]
+    columns = jnp.concatenate([norm_gains, shift_rows, lead_weight], axis=0)
+    tile = jnp.zeros((16, 128), BF16)
+    tile = lax.dynamic_update_slice(tile, columns, (0, s * 32))
+    tile = lax.dynamic_update_slice(tile, up_bias[None], (11 + s, 0))
+    flags = jnp.zeros((16, 128), BF16)
+    flags = lax.dynamic_update_slice(flags, (valid_cells > 0).astype(BF16), (10, 0))
+    vectors = jnp.stack([tile, flags])
+    vmem = pl.BlockSpec(memory_space=pltpu.VMEM)
+    dma = pltpu.SemaphoreType.DMA
+    V = pltpu.VMEM
+    out_shape = (
+        jax.ShapeDtypeStruct((ROWS, width), BF16),
+        jax.ShapeDtypeStruct((ROWS, width), BF16),
+        jax.ShapeDtypeStruct((32, 3 * width), F32),
+        jax.ShapeDtypeStruct((32, width), F32),
+        jax.ShapeDtypeStruct((32, 4 * width), F32),
+        jax.ShapeDtypeStruct((128, width), F32),
+        jax.ShapeDtypeStruct((16, 128), F32),
+    )
+    scratch = [
+        V((4, PLANE, ROWS, width), BF16),
+        V((PLANE, DEPTH, 32, 384), BF16),
+        V((DEPTH, 32, width), BF16),
+        V((PLANE, DEPTH, 32, 512), BF16),
+        V((DEPTH, 128, width), BF16),
+        V((PLANE, 32, 384), BF16),
+        V((PLANE, 32, 512), BF16),
+        V((3, 16, 128), BF16),
+        V((16, 128), BF16),
+        V((PLANE, 16, 128), BF16),
+        V((16, width), F32),
+        V((PLANE, ROWS, width), BF16),
+        V((2, CHIPS, BLOCK, 256), BF16),
+        V((1024, 256), BF16),
+        V((128, 1024), BF16),
+        V((1024, 128), BF16),
+        V((128, 1024), BF16),
+        V((2, CHIPS, 1024, BLOCK), BF16),
+        V((CHIPS, 128, BLOCK), F32),
+        V((CHIPS, 2, 8, BLOCK), F32),
+        V((CHIPS, BLOCK, 128), BF16),
+        V((1024, 384), BF16),
+        V((1024, 128), F32),
+        V((1024, 128), F32),
+        V((1024, 512), BF16),
+        V((CHIPS, BLOCK, 512), F32),
+        V((1024, 512), BF16),
+        V((ROWS, width), F32),
+        V((ROWS, width), F32),
+        V((3, CHIPS, 2, ROWS, width), BF16),
+        V((4, CHIPS, ROWS, width), BF16),
+        V((3, CHIPS, ROWS, width), BF16),
+        V((4, CHIPS, ROWS, width), BF16),
+        V((DEPTH, 128, width), BF16),
+        V((PLANE, DEPTH, 32, 512), BF16),
+        V((PLANE, DEPTH, 32, 384), BF16),
+        V((DEPTH, 32, width), BF16),
+        V((3, 128, width), BF16),
+        V((3, PLANE, 32, 512), BF16),
+        V((3, PLANE, 32, 384), BF16),
+        V((3, 32, width), BF16),
+        V((PLANE, 32, 512), BF16),
+        V((PLANE, 32, 384), BF16),
+        V((PLANE, 32, 512), BF16),
+        V((PLANE, 32, 384), BF16),
+        V((128, width), F32),
+        V((10, 8, width), F32),
+        V((8, 512), F32),
+        V((PLANE, 16, 128), F32),
+        V((PLANE - 1, 16, 128), F32),
+        V((16, 128), F32),
+        V((3, 16, 128), F32),
+        dma((4, 4)), dma((4, 4)), dma((4, 4)), dma((4, 4)),
+        dma((4, 7)), dma((4, 7)), dma((2, 7)), dma((2, 7)),
+        dma((10, 3)), dma((10, 3)),
+        dma((4, 4)), dma((4, 4)), dma((4, 4)), dma((4, 4)),
+    ]
+    results = pl.pallas_call(
+        plane_kernel,
+        out_shape=out_shape,
+        in_specs=[pl.BlockSpec(memory_space=pltpu.SMEM)] + [vmem] * 7,
+        out_specs=tuple([vmem] * 7),
+        scratch_shapes=scratch,
+        compiler_params=pltpu.CompilerParams(
+            collective_id=0, has_side_effects=True, vmem_limit_bytes=63 * 2**20
+        ),
+    )(lead_steps, tokens[0], cotangent[0], w_qkv, w_out, w_up, w_down, vectors)
+    output, input_grad, g_qkv, g_out, g_up, g_down, vec = results
+    rows = lax.dynamic_slice(vec, (0, s * 32), (10, 32))
+    g_bias = lax.dynamic_slice(vec, (11 + s, 0), (1, 128))[0]
+    return (
+        output[None], input_grad[None], g_qkv, g_out, g_up, g_down, g_bias,
+        rows[0:2], rows[2:8], rows[8:10],
+    )
+
+
+def plane_fits(mesh):
+    return mesh.shape["band"] == PLANE and mesh.shape["samp"] == DEPTH
+
+
 def solution(mesh):
     return jax.shard_map(
-        body,
+        plane_body if plane_fits(mesh) else body,
         mesh=mesh,
         in_specs=(
             P("samp", "band", None),

time: 2110 us -> 177 us (0.08)
  waiting for transfers between devices: 1610 us -> 0 us
  blocking collectives: 310 us -> 0 us
  Pallas kernels: 0 us -> 163 us
  matrix products: 89.8 us -> 0 us
  local copies, waits for them, and re-layouts: 64.7 us -> 11.3 us
    reduce_scatter x6 -> x0, waiting for transfers between devices: 1140 us -> none  [the longest x1 366 us: body(): lax.psum_scatter(grad_down_w, ('band', 'samp'), scatter_dimension=0, tile...]
    unnamed x18 -> x0, waiting for transfers between devices: 319 us -> none
    all_gather x5 -> x0, blocking collectives: 270 us -> none  [the longest x1 69.7 us: body(): lax.all_gather(norm_gains, ('band', 'samp'), axis=1, tiled=True)]
    pallas_call x0 -> x1, Pallas kernels: none -> 163 us  [plane_body(): pl.pallas_call(plane_kernel, out_shape=out_shape, in_specs=[pl.BlockSpec(...]
    all_gather x6 -> x0, waiting for transfers between devices: 160 us -> none  [the longest x1 76.7 us: body(): lax.all_gather(w_up, ('band', 'samp'), axis=0, tiled=True)]
    dot_general x26 -> x0, matrix products: 89.8 us -> none  [the longest x1 10.1 us: body(): jnp.einsum('td,fd->tf', grad_result, down_full, preferred_element_type=jn...]
    unnamed x1 -> x0, blocking collectives: 39.9 us -> none
  transfers between devices with their start and end apart: 15 -> 0, of which waited for: 12 -> 0; matrix products, arithmetic and copies ran while one was open for 4% -> 0% of each run, Pallas kernels for 0% -> 0%
where the time goes in v1:
time: 177 us; the launch traced here: 176 us
  Pallas kernels  163 us (92%)
  local copies, waits for them, and re-layouts  11.3 us (6%)
    pallas_call x1, Pallas kernels, plane_body(): pl.pallas_call(plane_kernel, out_shape=out_shape, in_specs=[pl.BlockSpec(...  163 us
    unnamed x28, local copies, waits for them, and re-layouts  8.41 us

profile of v1, /device:TPU:0, one launch (start us, length us, event | category | flops | bytes accessed | tf_op | source)
XLA Modules:
  0.0 176.3 jit_solution(14617259666063010165)
XLA Ops:
  1.3 0.0 copy-start.10
  1.3 0.6 copy-done.10
  2.0 0.0 copy-start.6
  2.0 0.0 copy-start.7
  2.0 0.0 copy-start.8
  2.0 0.6 copy-done.6
  2.6 0.0 copy-done.7
  2.6 0.0 copy-done.8
  2.7 0.0 copy-start.9
  2.7 0.3 dynamic_update_slice.11
  3.0 0.3 copy-done.9
  3.4 0.6 pad_maximum_fusion.vec_in
  4.0 163.1 %shard_map.195 = (bf16[128,1024]{1,0:T(8,128)(2,1)}, bf16[128,1024]{1,0:T(8,128)(2,1)}, f32[32,3072]{1,0:T(8,128)}, f32[32,1024]{1,0:T(8,128)}, f32[32,4096]{1,0...) custom-call(s32[1]{0:T(128)S(6)} %copy.30.lead_ref, bf16[128,1024]{1,0:T(8,128)(2,1)} %bitcast.11, ...), custom_call_target="tpu_custom_call" | custom-call | tf_op jit(solution)/shard_map/pallas_call | solution.py:957
  167.0 1.2 dynamic-slice_bitcast_fusion
  168.2 0.0 copy-start.5
  168.2 0.7 copy-done.5
  168.9 0.6 fusion.1
  169.6 0.0 copy-start.3
  169.6 0.7 dynamic-slice.1
  170.2 0.0 copy-start.2
  170.2 1.7 copy.31
  172.0 0.0 copy-done.3
  172.0 0.7 copy.32
  172.7 0.0 copy-done.2
  172.7 0.0 copy-start.4
  172.7 0.0 copy-start.1
  172.7 0.7 copy.33
  173.4 0.2 copy-done.4
  173.7 0.7 copy.34
  174.3 0.0 copy-done.1
  174.3 0.0 copy-start
  174.3 0.8 copy.35
  175.1 0.4 copy-done
  175.6 0.8 copy.36
  (5 shorter events, 0.1 us)
Async XLA Ops:
  1.3 0.7 copy-start.10
  2.0 0.7 copy-start.6
  2.0 0.7 copy-start.7
  2.0 0.7 copy-start.8
  2.7 0.7 copy-start.9
  168.2 0.7 copy-start.5
  169.6 2.4 %copy-start.3 = (bf16[128,1024]{1,0:T(8,128)(2,1)S(1)}, bf16[128,1024]{1,0:T(8,128)(2,1)}, u32[]{:S(2)}) copy-start(bf16[128,1024]{1,0:T(8,128)(2,1)} %get-tuple-element.18) | copy-start | bytes 786436
  170.2 2.4 %copy-start.2 = (f32[32,3072]{1,0:T(8,128)S(1)}, f32[32,3072]{1,0:T(8,128)}, u32[]{:S(2)}) copy-start(f32[32,3072]{1,0:T(8,128)} %get-tuple-element.38) | copy-start | bytes 1179652
  172.7 1.0 copy-start.4
  172.7 1.7 copy-start.1
  174.3 1.2 copy-start

commit v2 on v1

--- a/solution.py
+++ b/solution.py
@@ -265,6 +265,7 @@
 PLANE = 8
 DEPTH = 4
 ROWS = 128
+HALF = 64
 BLOCK = 256
 CHIPS = 4
 NN = (((1,), (0,)), ((), ()))
@@ -278,15 +279,19 @@
 
 
 def plane_kernel(
-    lead_ref, tok, cot, wqkv, wout, wup, wdown, vec_in,
-    out_o, ig_o, gqkv_o, gout_o, gup_o, gdown_o, vec_o,
+    lead_ref, gain_in, shift_in, leadw_in, bias_in, valid_in,
+    tok_in, cot_in, wqkv_in, wout_in, wup_in, wdown_in,
+    out_h, ig_h, gqkv_h, gout_h, gup_h, gdown_h, gain_o, shift_o, lead_o, bias_o,
+    out_o, ig_o, gqkv_o, gout_o, gup_o, gdown_o,
+    wqkv, wup, vcol, vec_in,
     agf, wq, wo, wu, wd, sq, su, ztr, vt, vecf, vrow,
     normed, qaug, kaug, kt, vv, vt2, pst, ot, invl, att, gproj, dk, dv,
     hid, gder, gpre, mid, gmid,
     part, pr, cs, rr,
-    gds, gus, gqs, gos, gdr, gur, gqr, gor_, gu2, gq2, gua, gqa, goa,
+    gds, gus, gqs, gos, gdr, gur, gqr, gor_, gda, guc, gqc, goc, gu2, gq2, gua, gqa, goa,
     acc, gub, vs, vsr, vz, vzr,
-    ag_s, ag_r, fw_s, fw_r, aq_s, aq_r, v_s, v_r, z_s, z_r, p_s, p_r, c_s, c_r,
+    in_s, out_s, ag_s, ag_r, ac_s, ac_r, fw_s, fw_r, aq_s, aq_r, v_s, v_r, y_s, y_r, z_s, z_r, za_r,
+    p_s, p_r, c_s, c_r,
 ):
     b = lax.axis_index("band")
     s = lax.axis_index("samp")
@@ -314,6 +319,41 @@
         pl.semaphore_signal(barrier, inc=1, device_id=(peer(k), s), device_id_type=MESH)
     for k in range(1, DEPTH):
         pl.semaphore_signal(barrier, inc=1, device_id=(b, level(k)), device_id_type=MESH)
+
+    width = tok_in.shape[1]
+    fetches = [
+        pltpu.make_async_copy(src, dst, in_s.at[n])
+        for n, (src, dst) in enumerate((
+            (wqkv_in, wqkv), (wout_in, wo.at[s]), (tok_in, agf.at[0, b]),
+            (wup_in, wup), (wdown_in, wd.at[s]), (cot_in, agf.at[1, b]),
+        ))
+    ]
+    for fetch in fetches:
+        fetch.start()
+    vcol[...] = jnp.zeros_like(vcol)
+    vcol[0:2, 0:32] = gain_in[...].astype(F32)
+    vcol[2:8, 0:32] = shift_in[...].astype(F32)
+    vcol[8:10, 0:32] = leadw_in[...].astype(F32)
+    line = lax.broadcasted_iota(jnp.int32, (16, 128), 0)
+    tile = pltpu.roll(vcol[...], s * 32, 1)
+    tile = jnp.where(line == 11 + s, bias_in[...].astype(F32), tile)
+    vec_in[0] = tile.astype(BF16)
+    opened = jnp.where(valid_in[...] > 0, 1.0, 0.0)
+    vec_in[1] = jnp.where(line == 10, opened, 0.0).astype(BF16)
+    far = (s + 2) % DEPTH
+    ends = (s == 0) | (s == DEPTH - 1)
+    inner = (s > 0) & (s < DEPTH - 1)
+
+    @pl.when(ends)
+    def _():
+        for kept in (gdr, gur, gqr, gor_):
+            kept[DEPTH - 1 - s] = jnp.zeros(kept.shape[1:], BF16)
+
+    fetches[0].wait()
+    for d in range(PLANE):
+        for j in range(3):
+            sq[d, :, j * 128:(j + 1) * 128] = wqkv[:, j * width + d * 128:j * width + (d + 1) * 128]
+    fetches[1].wait()
     pl.semaphore_wait(barrier, PLANE - 1 + DEPTH - 1)
 
     def rc(src, dst, ss, rs, band, samp):
@@ -322,26 +362,190 @@
             device_id=(band, samp), device_id_type=MESH,
         )
 
-    def zc(kind, k, src, dst):
-        return rc(src, dst, z_s.at[kind, k - 1], z_r.at[kind, k - 1], b, level(k))
-
-    def gather(op, r):
-        dst = mate if r == 0 else chip(r) * 2 + c
-        src = tok if op == 0 else (cot if op == 1 else agf.at[op, b])
-        return rc(src, agf.at[op, b], ag_s.at[op, r], ag_r.at[op, r], dst, s)
-
-    def forward(op, r):
+    def yc(kind, k, src, dst):
+        return rc(src, dst, y_s.at[kind, k - 1], y_r.at[kind, k - 1], b, level(k))
+
+    def weight_copy(kind, region, role, to):
+        return rc(region(s), region(s), z_s.at[kind, role], z_r.at[kind, s], b, to)
+
+    def weight_hand(kind, region):
+        return rc(region(far), region(far), z_s.at[kind, 3], z_r.at[kind, far], b, 3 * (s - 1))
+
+    def weight_from(kind, region, t):
+        rc(region(t), region(t), z_s.at[kind, 3], z_r.at[kind, t], b, t).wait_recv()
+
+    def weight_start(kind, region):
+        @pl.when(s == 1)
+        def _():
+            weight_copy(kind, region, 2, s - 1).start()
+
+        weight_copy(kind, region, 0, far).start()
+
+        @pl.when(s < DEPTH - 1)
+        def _():
+            weight_copy(kind, region, 1, s + 1).start()
+
+        @pl.when(s > 1)
+        def _():
+            weight_copy(kind, region, 2, s - 1).start()
+
+    def weight_pass(kind, region):
+        @pl.when(inner)
+        def _():
+            weight_from(kind, region, far)
+            weight_hand(kind, region).start()
+
+    def weight_finish(kind, region):
+        @pl.when(s < DEPTH - 1)
+        def _():
+            weight_from(kind, region, s + 1)
+
+        @pl.when(s > 0)
+        def _():
+            weight_from(kind, region, s - 1)
+
+        @pl.when(ends)
+        def _():
+            weight_from(kind, region, far)
+            weight_from(kind, region, DEPTH - 1 - s)
+
+    def weight_sent(kind, region):
+        weight_copy(kind, region, 0, far).wait_send()
+
+        @pl.when(s < DEPTH - 1)
+        def _():
+            weight_copy(kind, region, 1, s + 1).wait_send()
+
+        @pl.when(s > 0)
+        def _():
+            weight_copy(kind, region, 2, s - 1).wait_send()
+
+        @pl.when(inner)
+        def _():
+            weight_hand(kind, region).wait_send()
+
+    def grad_copy(kind, stage, got, role, to):
+        return rc(stage(to), got(s), z_s.at[kind, role], z_r.at[kind, s], b, to)
+
+    def grad_via(kind, stage, via):
+        return rc(stage(DEPTH - 1 - s), via, z_s.at[kind, 3], za_r.at[kind - 5], b, 1 + s // 3)
+
+    def grad_start(kind, stage, got, via):
+        @pl.when(ends)
+        def _():
+            grad_via(kind, stage, via).start()
+            grad_copy(kind, stage, got, 0, far).start()
+
+        @pl.when(s < DEPTH - 1)
+        def _():
+            grad_copy(kind, stage, got, 1, s + 1).start()
+
+        @pl.when(s > 0)
+        def _():
+            grad_copy(kind, stage, got, 2, s - 1).start()
+
+    def grad_pass(kind, stage, got, via):
+        @pl.when(inner)
+        def _():
+            rc(via, via, z_s.at[kind, 3], za_r.at[kind - 5], b, far).wait_recv()
+            term = stage(far)
+            count = via.shape[0]
+
+            def add(j, _):
+                term[j] = (term[j].astype(F32) + via[j].astype(F32)).astype(BF16)
+                return 0
+
+            if len(via.shape) == 3:
+                lax.fori_loop(0, count, add, 0)
+            else:
+                def add_rows(j, _):
+                    rows = pl.ds(pl.multiple_of(j * INNER, INNER), INNER)
+                    term[rows, :] = (term[rows, :].astype(F32) + via[rows, :].astype(F32)).astype(BF16)
+                    return 0
+
+                lax.fori_loop(0, count // INNER, add_rows, 0)
+            grad_copy(kind, stage, got, 0, far).start()
+
+    def grad_finish(kind, stage, got, via):
+        rc(got(far), got(far), z_s.at[kind, 0], z_r.at[kind, far], b, far).wait_recv()
+
+        @pl.when(s < DEPTH - 1)
+        def _():
+            rc(got(s + 1), got(s + 1), z_s.at[kind, 1], z_r.at[kind, s + 1], b, s + 1).wait_recv()
+
+        @pl.when(s > 0)
+        def _():
+            rc(got(s - 1), got(s - 1), z_s.at[kind, 2], z_r.at[kind, s - 1], b, s - 1).wait_recv()
+
+    def grad_sent(kind, stage, got, via):
+        grad_copy(kind, stage, got, 0, far).wait_send()
+
+        @pl.when(s < DEPTH - 1)
+        def _():
+            grad_copy(kind, stage, got, 1, s + 1).wait_send()
+
+        @pl.when(s > 0)
+        def _():
+            grad_copy(kind, stage, got, 2, s - 1).wait_send()
+
+        @pl.when(ends)
+        def _():
+            grad_via(kind, stage, via).wait_send()
+
+    results = ((out_o, out_h), (ig_o, ig_h), (gqkv_o, gqkv_h), (gout_o, gout_h), (gup_o, gup_h), (gdown_o, gdown_h))
+
+    def deliver(n):
+        return pltpu.make_async_copy(results[n][0], results[n][1], out_s.at[n])
+
+    w_out_z = (1, lambda t: wo.at[t])
+    w_qkv_z = (2, lambda t: wq.at[:, t])
+    w_up_z = (3, lambda t: wu.at[:, t])
+    w_down_z = (4, lambda t: wd.at[t])
+    g_down_z = (5, lambda t: gds.at[t], lambda t: gdr.at[t], gda)
+    g_up_z = (6, lambda t: gus.at[:, t], lambda t: gur.at[t], guc)
+    g_qkv_z = (7, lambda t: gqs.at[:, t], lambda t: gqr.at[t], gqc)
+    g_out_z = (8, lambda t: gos.at[t], lambda t: gor_.at[t], goc)
+
+    def gather(op, r, half):
+        dst = chip(r) * 2 + c
+        rows = pl.ds(HALF * ((half + r) % 2), HALF)
+        return rc(
+            agf.at[op, b, rows], agf.at[op, b, rows],
+            ag_s.at[op, r - 1, half], ag_r.at[op, r - 1, half], dst, s,
+        )
+
+    def across(op, r):
+        blk = chip(r) * 2 + c
+        rows = pl.ds(HALF * (r % 2), HALF)
+        return rc(
+            agf.at[op, blk, rows], agf.at[op, blk, rows],
+            ac_s.at[op, r - 1], ac_r.at[op, r - 1], chip(3 - r) * 2 + c, s,
+        )
+
+    def share(op, r):
         blk = chip(r) * 2 + c
         return rc(agf.at[op, blk], agf.at[op, blk], fw_s.at[op, r], fw_r.at[op, r], mate, s)
 
     def start_gather(op):
-        for r in (1, 2, 3, 0):
-            gather(op, r).start()
-
-    def pass_on(op, rs):
-        for r in rs:
-            gather(op, r).wait_recv()
-            forward(op, r).start()
+        for half in (0, 1):
+            for r in (1, 2):
+                gather(op, r, half).start()
+        share(op, 0).start()
+
+    def pass_first(op):
+        for r in (1, 2):
+            gather(op, r, 0).wait_recv()
+            across(op, r).start()
+
+    def pass_second(op):
+        for r in (1, 2):
+            gather(op, r, 1).wait_recv()
+            share(op, r).start()
+
+    def pass_far(op):
+        across(op, 1).wait_recv()
+        across(op, 2).wait_recv()
+        share(op, 3).start()
 
     def block(op, q):
         return agf[op, pl.ds(2 * q, 2)].reshape(BLOCK, -1)
@@ -349,28 +553,22 @@
     def swap(kind, k, src, dst):
         return rc(src, dst, aq_s.at[kind, k - 1], aq_r.at[kind, k - 1], peer(k), s)
 
-    start_gather(0)
     for k in range(1, DEPTH):
-        zc(0, k, vec_in.at[0], ztr.at[k - 1]).start()
-    agf[0, b] = tok[...]
-    agf[1, b] = cot[...]
-    width = tok.shape[1]
-    for d in range(PLANE):
-        for j in range(3):
-            sq[d, :, j * 128:(j + 1) * 128] = wqkv[:, j * width + d * 128:j * width + (d + 1) * 128]
+        yc(0, k, vec_in.at[0], ztr.at[k - 1]).start()
     for k in range(1, PLANE):
         swap(0, k, sq.at[peer(k)], wq.at[b, s]).start()
+    weight_start(*w_out_z)
+    fetches[2].wait()
+    for r in (1, 2):
+        gather(0, r, 0).start()
     wq[b, s] = sq[b]
-    wo[s] = wout[...]
-    for k in range(1, DEPTH):
-        zc(1, k, wo.at[s], wo.at[s]).start()
+    fetches[3].wait()
     for d in range(PLANE):
         su[d] = wup[:, d * 512:(d + 1) * 512]
     wu[b, s] = su[b]
-    wd[s] = wdown[...]
 
     for k in range(1, DEPTH):
-        zc(0, k, vec_in.at[0], ztr.at[k - 1]).wait_recv()
+        yc(0, k, vec_in.at[0], ztr.at[k - 1]).wait_recv()
     vt[...] = (
         vec_in[0].astype(F32) + vec_in[1].astype(F32)
         + ztr[0].astype(F32) + ztr[1].astype(F32) + ztr[2].astype(F32)
@@ -381,13 +579,16 @@
 
     for k in range(1, PLANE):
         spread(k).start()
+    for r in (1, 2):
+        gather(0, r, 1).start()
+    share(0, 0).start()
     vecf[b] = vt[...]
     for k in range(1, PLANE):
         swap(0, k, sq.at[peer(k)], wq.at[b, s]).wait_recv()
-    for k in range(1, DEPTH):
-        zc(2, k, wq.at[:, s], wq.at[:, s]).start()
+    weight_start(*w_qkv_z)
     for k in range(1, PLANE):
         swap(1, k, su.at[peer(k)], wu.at[b, s]).start()
+    pass_first(0)
     for k in range(1, PLANE):
         spread(k).wait_recv()
     for d in range(PLANE):
@@ -428,27 +629,26 @@
         lax.fori_loop(0, ROWS // INNER, chunk, 0)
 
     norm_block(b)
-    gather(0, 0).wait_recv()
+    share(0, 0).wait_recv()
     norm_block(mate)
-    pass_on(0, (1, 2))
+    pass_second(0)
     for r in (1, 2):
         norm_block(chip(r) * 2 + c)
-        forward(0, r).wait_recv()
+        share(0, r).wait_recv()
         norm_block(chip(r) * 2 + 1 - c)
-    pass_on(0, (3,))
+    weight_pass(*w_qkv_z)
+    pass_far(0)
+    fetches[5].wait()
     start_gather(1)
     norm_block(chip(3) * 2 + c)
-    forward(0, 3).wait_recv()
+    share(0, 3).wait_recv()
     norm_block(chip(3) * 2 + 1 - c)
 
-    for k in range(1, DEPTH):
-        zc(2, k, wq.at[:, s], wq.at[:, s]).wait_recv()
     for k in range(1, PLANE):
         swap(1, k, su.at[peer(k)], wu.at[b, s]).wait_recv()
-    for k in range(1, DEPTH):
-        zc(3, k, wu.at[:, s], wu.at[:, s]).start()
-    for k in range(1, DEPTH):
-        zc(4, k, wd.at[s], wd.at[s]).start()
+    weight_pass(*w_out_z)
+    weight_finish(*w_qkv_z)
+    weight_start(*w_up_z)
 
     def project_block(q, _):
         rows = pl.ds(pl.multiple_of(q * BLOCK, BLOCK), BLOCK)
@@ -465,8 +665,7 @@
         return 0
 
     lax.fori_loop(0, CHIPS, project_block, 0)
-    for k in range(1, DEPTH):
-        zc(1, k, wo.at[s], wo.at[s]).wait_recv()
+    weight_finish(*w_out_z)
 
     def mate_copy(op, slot, r):
         return rc(part.at[slot, r, 1 - c], pr.at[op, r], p_s.at[op, r], p_r.at[op, r], mate, s)
@@ -510,6 +709,11 @@
     def attend_block(i, _):
         r = 3 - i
         q = chip(r)
+
+        @pl.when(i == 1)
+        def _():
+            pass_first(1)
+            pass_second(1)
 
         def head(h, _):
             top = pl.ds(pl.multiple_of(h * 64, 64), 64)
@@ -535,13 +739,15 @@
 
     lax.fori_loop(0, CHIPS, attend_block, 0)
     fold(0, 0, 0)
-    pass_on(1, (1, 2, 3))
+    weight_pass(*w_up_z)
+    fetches[4].wait()
+    weight_start(*w_down_z)
     for r in (1, 2, 3):
         chip_copy(0, 0, r).wait_recv()
 
     def middle_chunk(j, _):
         rows = pl.ds(pl.multiple_of(j * INNER, INNER), INNER)
-        ent = tok[rows, :].astype(F32) + lead_row
+        ent = agf[0, b, rows, :].astype(F32) + lead_row
         m = ent + plane_total(0, 0, rows) + shift_out
         mid[rows, :] = m
         agf[2, b, rows, :] = (stats(m)[0] * gain2 + shift2).astype(BF16)
@@ -549,34 +755,40 @@
 
     lax.fori_loop(0, ROWS // INNER, middle_chunk, 0)
     start_gather(2)
+    pass_far(1)
     end_sums(0, 0)
 
-    for k in range(1, DEPTH):
-        zc(3, k, wu.at[:, s], wu.at[:, s]).wait_recv()
+    weight_finish(*w_up_z)
     bias = jnp.concatenate([mine[11 + j:12 + j, :] for j in range(4)], axis=1)
 
     def arrivals(op, i):
         @pl.when(i == 0)
         def _():
-            gather(op, 0).wait_recv()
+            share(op, 0).wait_recv()
 
         @pl.when(i == 1)
         def _():
-            pass_on(op, (1, 2))
-            forward(op, 1).wait_recv()
+            pass_first(op)
+            pass_second(op)
+            share(op, 1).wait_recv()
 
         @pl.when(i == 2)
         def _():
-            forward(op, 2).wait_recv()
+            share(op, 2).wait_recv()
 
         @pl.when(i == 3)
         def _():
-            pass_on(op, (3,))
-            forward(op, 3).wait_recv()
+            pass_far(op)
+            share(op, 3).wait_recv()
 
     def up_block(i, _):
         arrivals(2, i)
         q = chip(i)
+
+        @pl.when(i == 2)
+        def _():
+            weight_pass(*w_down_z)
+
         hp = mm(block(2, q), wu[...].reshape(width, 512)) + bias
         phi = 0.5 + 0.5 * lax.erf(hp * 0.7071067811865476)
         hid[pl.ds(pl.multiple_of(q * BLOCK, BLOCK), BLOCK), :] = (hp * phi).astype(BF16)
@@ -584,9 +796,8 @@
         return 0
 
     lax.fori_loop(0, CHIPS, up_block, 0)
-    gather(1, 0).wait_recv()
-    for r in (1, 2, 3):
-        forward(1, r).wait_recv()
+    for r in range(CHIPS):
+        share(1, r).wait_recv()
 
     def down_grad(f, _):
         cols = pl.ds(pl.multiple_of(f * BLOCK, BLOCK), BLOCK)
@@ -595,10 +806,8 @@
         return 0
 
     lax.fori_loop(0, 2, down_grad, 0)
-    for k in range(1, DEPTH):
-        zc(4, k, wd.at[s], wd.at[s]).wait_recv()
-    for k in range(1, DEPTH):
-        zc(5, k, gds.at[level(k)], gdr.at[k - 1]).start()
+    grad_start(*g_down_z)
+    weight_finish(*w_down_z)
     gub[...] = jnp.zeros_like(gub)
 
     def back_block(i, _):
@@ -627,8 +836,7 @@
         return 0
 
     lax.fori_loop(0, CHIPS, up_grad, 0)
-    for k in range(1, DEPTH):
-        zc(6, k, gus.at[:, level(k)], gur.at[k - 1]).start()
+    grad_start(*g_up_z)
 
     def out_block(i, _):
         r = 3 - i
@@ -645,6 +853,7 @@
     lax.fori_loop(0, CHIPS, out_block, 0)
     fold(2, 2, 0, send=False)
 
+    grad_pass(*g_down_z)
     for r in (1, 2, 3):
         chip_copy(1, 1, r).wait_recv()
     acc[...] = jnp.zeros_like(acc)
@@ -663,7 +872,7 @@
         rows = pl.ds(pl.multiple_of(j * INNER, INNER), INNER)
         gs = plane_total(1, 1, rows)
         g, xhat = norm_back(mid[rows, :], gs, gain2)
-        ct = cot[rows, :].astype(F32)
+        ct = agf[1, b, rows, :].astype(F32)
         gm = ct + g
         gmid[rows, :] = gm
         gb = gm.astype(BF16)
@@ -683,6 +892,16 @@
 
     def attend_back(i, _):
         arrivals(3, i)
+
+        @pl.when(i == 2)
+        def _():
+            for r in (3, 2, 1):
+                chip_copy(2, 2, r).start()
+
+        @pl.when(i == 3)
+        def _():
+            grad_pass(*g_up_z)
+
         q = chip(i)
         gbk = block(3, q)
         wo_all = wo[...].reshape(128, width)
@@ -710,10 +929,19 @@
         return 0
 
     lax.fori_loop(0, CHIPS, attend_back, 0)
-    for r in (1, 2, 3):
-        chip_copy(2, 2, r).start()
     gproj[:, 128:256] = dk[...].astype(BF16)
     gproj[:, 256:384] = dv[...].astype(BF16)
+
+    def qkv_grad(f, _):
+        cols = pl.ds(pl.multiple_of(f * BLOCK, BLOCK), BLOCK)
+        g = mm(normed[:, :, cols].reshape(PLANE * ROWS, BLOCK), gproj[...], TN)
+        gqs[pl.ds(2 * f, 2)] = g.astype(BF16).reshape(2, 4, 32, 384)
+        return 0
+
+    lax.fori_loop(0, CHIPS, qkv_grad, 0)
+    gos[...] = goa[...].astype(BF16).reshape(4, 32, width)
+    grad_start(*g_out_z)
+    grad_start(*g_qkv_z)
 
     def project_back(i, _):
         r = 3 - i
@@ -730,35 +958,12 @@
     lax.fori_loop(0, CHIPS, project_back, 0)
     fold(3, 0, 0)
 
-    def qkv_grad(f, _):
-        cols = pl.ds(pl.multiple_of(f * BLOCK, BLOCK), BLOCK)
-        g = mm(normed[:, :, cols].reshape(PLANE * ROWS, BLOCK), gproj[...], TN)
-        gqs[pl.ds(2 * f, 2)] = g.astype(BF16).reshape(2, 4, 32, 384)
-        return 0
-
-    lax.fori_loop(0, CHIPS, qkv_grad, 0)
-    gos[...] = goa[...].astype(BF16).reshape(4, 32, width)
-    for k in range(1, DEPTH):
-        zc(7, k, gqs.at[:, level(k)], gqr.at[k - 1]).start()
-    for k in range(1, DEPTH):
-        zc(8, k, gos.at[level(k)], gor_.at[k - 1]).start()
-
-    for k in range(1, DEPTH):
-        zc(5, k, gds.at[level(k)], gdr.at[k - 1]).wait_recv()
-    gdown_o[...] = (
-        gds[s].astype(F32) + gdr[0].astype(F32) + gdr[1].astype(F32) + gdr[2].astype(F32)
-    )
-    for k in range(1, DEPTH):
-        zc(6, k, gus.at[:, level(k)], gur.at[k - 1]).wait_recv()
-    for d in range(PLANE):
-        gu2[d] = (
-            gus[d, s].astype(F32) + gur[0, d].astype(F32)
-            + gur[1, d].astype(F32) + gur[2, d].astype(F32)
-        ).astype(BF16)
-    for k in range(1, PLANE):
-        swap(2, k, gu2.at[peer(k)], gua.at[b]).start()
-    gua[b] = gu2[b]
-
+    def others(got):
+        return [got(level(k)) for k in range(1, DEPTH)]
+
+    grad_finish(*g_down_z)
+    gdown_o[...] = sum([t[...].astype(F32) for t in others(g_down_z[2])], gds[s].astype(F32))
+    deliver(5).start()
     for r in (1, 2, 3):
         chip_copy(2, 2, r).wait_recv()
 
@@ -768,14 +973,25 @@
         return 0
 
     lax.fori_loop(0, ROWS // INNER, output_chunk, 0)
-
+    deliver(0).start()
+
+    grad_pass(*g_out_z)
+    grad_pass(*g_qkv_z)
+    grad_finish(*g_up_z)
+    for d in range(PLANE):
+        gu2[d] = sum(
+            [t[d].astype(F32) for t in others(g_up_z[2])], gus[d, s].astype(F32)
+        ).astype(BF16)
+    for k in range(1, PLANE):
+        swap(2, k, gu2.at[peer(k)], gua.at[b]).start()
+    gua[b] = gu2[b]
     for r in (1, 2, 3):
         chip_copy(3, 0, r).wait_recv()
 
     def first_chunk(j, _):
         rows = pl.ds(pl.multiple_of(j * INNER, INNER), INNER)
         gn = plane_total(3, 0, rows)
-        g, xhat = norm_back(tok[rows, :].astype(F32) + lead_row, gn, gain1)
+        g, xhat = norm_back(agf[0, b, rows, :].astype(F32) + lead_row, gn, gain1)
         ge = gmid[rows, :] + g
         ig_o[rows, :] = ge.astype(BF16)
         add_row(0, gn * xhat)
@@ -784,6 +1000,7 @@
         return 0
 
     lax.fori_loop(0, ROWS // INNER, first_chunk, 0)
+    deliver(1).start()
     acc[8] = acc[9] * lead_days
 
     sums = [jnp.sum(acc[n], axis=0, keepdims=True) for n in range(10)]
@@ -812,19 +1029,15 @@
         total = total + vsr[k]
     vz[...] = total
     for k in range(1, DEPTH):
-        zc(9, k, vz, vzr.at[k - 1]).start()
-
-    for k in range(1, DEPTH):
-        zc(8, k, gos.at[level(k)], gor_.at[k - 1]).wait_recv()
-    gout_o[...] = (
-        gos[s].astype(F32) + gor_[0].astype(F32) + gor_[1].astype(F32) + gor_[2].astype(F32)
-    )
-    for k in range(1, DEPTH):
-        zc(7, k, gqs.at[:, level(k)], gqr.at[k - 1]).wait_recv()
+        yc(1, k, vz, vzr.at[k - 1]).start()
+
+    grad_finish(*g_out_z)
+    gout_o[...] = sum([t[...].astype(F32) for t in others(g_out_z[2])], gos[s].astype(F32))
+    deliver(3).start()
+    grad_finish(*g_qkv_z)
     for d in range(PLANE):
-        gq2[d] = (
-            gqs[d, s].astype(F32) + gqr[0, d].astype(F32)
-            + gqr[1, d].astype(F32) + gqr[2, d].astype(F32)
+        gq2[d] = sum(
+            [t[d].astype(F32) for t in others(g_qkv_z[2])], gqs[d, s].astype(F32)
         ).astype(BF16)
     for k in range(1, PLANE):
         swap(3, k, gq2.at[peer(k)], gqa.at[b]).start()
@@ -833,9 +1046,15 @@
         swap(2, k, gu2.at[peer(k)], gua.at[b]).wait_recv()
     for d in range(PLANE):
         gup_o[:, d * 512:(d + 1) * 512] = gua[d].astype(F32)
+    deliver(4).start()
     for k in range(1, DEPTH):
-        zc(9, k, vz, vzr.at[k - 1]).wait_recv()
-    vec_o[...] = vz[...] + vzr[0] + vzr[1] + vzr[2]
+        yc(1, k, vz, vzr.at[k - 1]).wait_recv()
+    vz_sum = vz[...] + vzr[0] + vzr[1] + vzr[2]
+    columns = pltpu.roll(vz_sum, (128 - 32 * s) % 128, 1)
+    gain_o[...] = columns[0:2, 0:32]
+    shift_o[...] = columns[2:8, 0:32]
+    lead_o[...] = columns[8:10, 0:32]
+    bias_o[...] = jnp.sum(jnp.where(line == 11 + s, vz_sum, 0.0), axis=0, keepdims=True)
     for k in range(1, PLANE):
         swap(3, k, gq2.at[peer(k)], gqa.at[b]).wait_recv()
     for d in range(PLANE):
@@ -844,11 +1063,14 @@
                 gqa[d, :, j * 128:(j + 1) * 128].astype(F32)
             )
 
+    deliver(2).start()
     for op in range(4):
+        for r in (1, 2):
+            gather(op, r, 0).wait_send()
+            gather(op, r, 1).wait_send()
+            across(op, r).wait_send()
         for r in range(CHIPS):
-            gather(op, r).wait_send()
-        for r in (1, 2, 3):
-            forward(op, r).wait_send()
+            share(op, r).wait_send()
     for op, slot in ((1, 1), (2, 2), (3, 0)):
         end_sums(op, slot)
     for k in range(1, PLANE):
@@ -859,32 +1081,33 @@
         spread(k).wait_send()
         vec_swap(k).wait_send()
     for k in range(1, DEPTH):
-        zc(0, k, vec_in.at[0], ztr.at[k - 1]).wait_send()
-        zc(1, k, wo.at[s], wo.at[s]).wait_send()
-        zc(2, k, wq.at[:, s], wq.at[:, s]).wait_send()
-        zc(3, k, wu.at[:, s], wu.at[:, s]).wait_send()
-        zc(4, k, wd.at[s], wd.at[s]).wait_send()
-        zc(5, k, gds.at[level(k)], gdr.at[k - 1]).wait_send()
-        zc(6, k, gus.at[:, level(k)], gur.at[k - 1]).wait_send()
-        zc(7, k, gqs.at[:, level(k)], gqr.at[k - 1]).wait_send()
-        zc(8, k, gos.at[level(k)], gor_.at[k - 1]).wait_send()
-        zc(9, k, vz, vzr.at[k - 1]).wait_send()
+        yc(0, k, vec_in.at[0], ztr.at[k - 1]).wait_send()
+        yc(1, k, vz, vzr.at[k - 1]).wait_send()
+    for moved in (w_out_z, w_qkv_z, w_up_z, w_down_z):
+        weight_sent(*moved)
+    for moved in (g_down_z, g_up_z, g_qkv_z, g_out_z):
+        grad_sent(*moved)
+    for n in range(6):
+        deliver(n).wait()
+
+
+def hand_over(*refs):
+    count = len(refs) // 2
+    sems = refs[-1]
+    copies = [pltpu.make_async_copy(refs[n], refs[count + n], sems.at[n]) for n in range(count)]
+    for copy in copies:
+        copy.start()
+    for copy in copies:
+        copy.wait()
 
 
 def plane_body(
     tokens, cotangent, w_qkv, w_out, w_up, w_down,
     up_bias, norm_gains, shift_rows, lead_weight, lead_steps, valid_cells,
 ):
-    s = lax.axis_index("samp")
     width = tokens.shape[2]
-    columns = jnp.concatenate([norm_gains, shift_rows, lead_weight], axis=0)
-    tile = jnp.zeros((16, 128), BF16)
-    tile = lax.dynamic_update_slice(tile, columns, (0, s * 32))
-    tile = lax.dynamic_update_slice(tile, up_bias[None], (11 + s, 0))
-    flags = jnp.zeros((16, 128), BF16)
-    flags = lax.dynamic_update_slice(flags, (valid_cells > 0).astype(BF16), (10, 0))
-    vectors = jnp.stack([tile, flags])
     vmem = pl.BlockSpec(memory_space=pltpu.VMEM)
+    anywhere = pl.BlockSpec(memory_space=pl.ANY)
     dma = pltpu.SemaphoreType.DMA
     V = pltpu.VMEM
     out_shape = (
@@ -894,9 +1117,17 @@
         jax.ShapeDtypeStruct((32, width), F32),
         jax.ShapeDtypeStruct((32, 4 * width), F32),
         jax.ShapeDtypeStruct((128, width), F32),
-        jax.ShapeDtypeStruct((16, 128), F32),
+        jax.ShapeDtypeStruct((2, 32), F32),
+        jax.ShapeDtypeStruct((6, 32), F32),
+        jax.ShapeDtypeStruct((2, 32), F32),
+        jax.ShapeDtypeStruct((1, 128), F32),
     )
     scratch = [
+        V((ROWS, width), BF16), V((ROWS, width), BF16),
+        V((32, 3 * width), F32), V((32, width), F32),
+        V((32, 4 * width), F32), V((128, width), F32),
+        V((32, 3 * width), BF16), V((32, 4 * width), BF16),
+        V((16, 128), F32), V((2, 16, 128), BF16),
         V((4, PLANE, ROWS, width), BF16),
         V((PLANE, DEPTH, 32, 384), BF16),
         V((DEPTH, 32, width), BF16),
@@ -934,10 +1165,14 @@
         V((PLANE, DEPTH, 32, 512), BF16),
         V((PLANE, DEPTH, 32, 384), BF16),
         V((DEPTH, 32, width), BF16),
-        V((3, 128, width), BF16),
-        V((3, PLANE, 32, 512), BF16),
-        V((3, PLANE, 32, 384), BF16),
-        V((3, 32, width), BF16),
+        V((DEPTH, 128, width), BF16),
+        V((DEPTH, PLANE, 32, 512), BF16),
+        V((DEPTH, PLANE, 32, 384), BF16),
+        V((DEPTH, 32, width), BF16),
+        V((128, width), BF16),
+        V((PLANE, 32, 512), BF16),
+        V((PLANE, 32, 384), BF16),
+        V((32, width), BF16),
         V((PLANE, 32, 512), BF16),
         V((PLANE, 32, 384), BF16),
         V((PLANE, 32, 512), BF16),
@@ -949,27 +1184,36 @@
         V((PLANE - 1, 16, 128), F32),
         V((16, 128), F32),
         V((3, 16, 128), F32),
-        dma((4, 4)), dma((4, 4)), dma((4, 4)), dma((4, 4)),
+        dma((6,)), dma((6,)),
+        dma((4, 2, 2)), dma((4, 2, 2)), dma((4, 2)), dma((4, 2)), dma((4, 4)), dma((4, 4)),
         dma((4, 7)), dma((4, 7)), dma((2, 7)), dma((2, 7)),
-        dma((10, 3)), dma((10, 3)),
+        dma((2, 3)), dma((2, 3)), dma((9, 4)), dma((9, 4)), dma((4,)),
         dma((4, 4)), dma((4, 4)), dma((4, 4)), dma((4, 4)),
     ]
     results = pl.pallas_call(
         plane_kernel,
         out_shape=out_shape,
-        in_specs=[pl.BlockSpec(memory_space=pltpu.SMEM)] + [vmem] * 7,
-        out_specs=tuple([vmem] * 7),
+        in_specs=[pl.BlockSpec(memory_space=pltpu.SMEM)] + [vmem] * 5 + [anywhere] * 6,
+        out_specs=tuple([anywhere] * 6 + [vmem] * 4),
         scratch_shapes=scratch,
         compiler_params=pltpu.CompilerParams(
             collective_id=0, has_side_effects=True, vmem_limit_bytes=63 * 2**20
         ),
-    )(lead_steps, tokens[0], cotangent[0], w_qkv, w_out, w_up, w_down, vectors)
-    output, input_grad, g_qkv, g_out, g_up, g_down, vec = results
-    rows = lax.dynamic_slice(vec, (0, s * 32), (10, 32))
-    g_bias = lax.dynamic_slice(vec, (11 + s, 0), (1, 128))[0]
+    )(
+        lead_steps, norm_gains, shift_rows, lead_weight, up_bias[None], valid_cells,
+        tokens[0], cotangent[0], w_qkv, w_out, w_up, w_down,
+    )
+    results = pl.pallas_call(
+        hand_over,
+        out_shape=out_shape,
+        in_specs=[vmem] * len(out_shape),
+        out_specs=tuple([anywhere] * len(out_shape)),
+        scratch_shapes=[dma((len(out_shape),))],
+    )(*results)
+    output, input_grad, g_qkv, g_out, g_up, g_down, g_gains, g_shifts, g_lead, g_bias = results
     return (
-        output[None], input_grad[None], g_qkv, g_out, g_up, g_down, g_bias,
-        rows[0:2], rows[2:8], rows[8:10],
+        output[None], input_grad[None], g_qkv, g_out, g_up, g_down, g_bias[0],
+        g_gains, g_shifts, g_lead,
     )
 
 

time: 177 us -> 133 us (0.75)
  Pallas kernels: 163 us -> 132 us
  local copies, waits for them, and re-layouts: 11.3 us -> 0 us
    pallas_call x1, Pallas kernels: 163 us -> 129 us  [plane_body(): pl.pallas_call(plane_kernel, out_shape=out_shape, in_specs=[pl.BlockSpec(...]
    unnamed x28 -> x0, local copies, waits for them, and re-layouts: 8.41 us -> none
    pallas_call x0 -> x1, Pallas kernels: none -> 2.96 us  [plane_body(): pl.pallas_call(hand_over, out_shape=out_shape, in_specs=[vmem] * len(out_...]
where the time goes in v2:
time: 133 us
  Pallas kernels  132 us (99%)
    pallas_call x1, Pallas kernels, plane_body(): pl.pallas_call(plane_kernel, out_shape=out_shape, in_specs=[pl.BlockSpec(...  129 us
    pallas_call x1, Pallas kernels, plane_body(): pl.pallas_call(hand_over, out_shape=out_shape, in_specs=[vmem] * len(out_...  2.96 us

profile of v2, /device:TPU:0, one launch (start us, length us, event | category | flops | bytes accessed | tf_op | source)
XLA Modules:
  0.0 133.2 jit_solution(1714257565155158188)
XLA Ops:
  1.3 129.0 %shard_map.195 = (bf16[128,1024]{1,0:T(8,128)(2,1)}, bf16[128,1024]{1,0:T(8,128)(2,1)}, f32[32,3072]{1,0:T(8,128)}, f32[32,1024]{1,0:T(8,128)}, f32[32,4096]{1,0...) custom-call(s32[1]{0:T(128)S(6)} %copy.22.lead_ref, ...), custom_call_target="tpu_custom_call" | custom-call | tf_op jit(solution)/shard_map/pallas_call | solution.py:1193
  130.3 3.0 %shard_map.196 = (bf16[128,1024]{1,0:T(8,128)(2,1)}, bf16[128,1024]{1,0:T(8,128)(2,1)}, f32[32,3072]{1,0:T(8,128)}, f32[32,1024]{1,0:T(8,128)}, f32[32,4096]{1,0...) custom-call(bf16[128,1024]{1,0:T(8,128)(2,1)} %get-tuple-element.30., ...), custom_call_target="tpu_custom_call" | custom-call | tf_op jit(solution)/shard_map/pallas_call | solution.py:1206

commit v3 on v2

--- a/solution.py
+++ b/solution.py
@@ -267,7 +267,6 @@
 ROWS = 128
 HALF = 64
 BLOCK = 256
-CHIPS = 4
 NN = (((1,), (0,)), ((), ()))
 NT = (((1,), (1,)), ((), ()))
 TN = (((0,), (0,)), ((), ()))
@@ -281,17 +280,17 @@
 def plane_kernel(
     lead_ref, gain_in, shift_in, leadw_in, bias_in, valid_in,
     tok_in, cot_in, wqkv_in, wout_in, wup_in, wdown_in,
-    out_h, ig_h, gqkv_h, gout_h, gup_h, gdown_h, gain_o, shift_o, lead_o, bias_o,
-    out_o, ig_o, gqkv_o, gout_o, gup_o, gdown_o,
+    out_h, ig_h, gqkv_h, gout_h, gup_h, gdown_h, gain_h, shift_h, lead_h, bias_h,
+    out_o, ig_o, gqkv_o, gout_o, gup_o, gdown_o, gain_o, shift_o, lead_o, bias_o,
     wqkv, wup, vcol, vec_in,
     agf, wq, wo, wu, wd, sq, su, ztr, vt, vecf, vrow,
-    normed, qaug, kaug, kt, vv, vt2, pst, ot, invl, att, gproj, dk, dv,
+    normed, qaug, kaug, kt, vv, vt2, pst, ot, invl, att, aown, dsend, dob, gproj, dk, dv,
     hid, gder, gpre, mid, gmid,
-    part, pr, cs, rr,
-    gds, gus, gqs, gos, gdr, gur, gqr, gor_, gda, guc, gqc, goc, gu2, gq2, gua, gqa, goa,
+    part, pr, cs, au, rr,
+    gds, gus, gqs, gos, gdr, gur, gqr, gor_, gda, guc, gqc, gu2, gq2, gua, gqa, goa,
     acc, gub, vs, vsr, vz, vzr,
     in_s, out_s, ag_s, ag_r, ac_s, ac_r, fw_s, fw_r, aq_s, aq_r, v_s, v_r, y_s, y_r, z_s, z_r, za_r,
-    p_s, p_r, c_s, c_r,
+    p_s, p_r, f_s, f_r, n_s, n_r, wg_s, wg_r, h_s, h_r, g_s, g_r,
 ):
     b = lax.axis_index("band")
     s = lax.axis_index("samp")
@@ -299,14 +298,14 @@
     x = (b // 2) % 2
     y = b // 4
     mate = b + 1 - 2 * c
-    own = b // 2
 
     def chip(r):
-        dx = r % 2
-        dy = r // 2
-        xx = x + dx * (1 - 2 * x)
-        yy = y + dy * (1 - 2 * y)
+        xx = x + (r % 2) * (1 - 2 * x)
+        yy = y + (r // 2) * (1 - 2 * y)
         return yy * 2 + xx
+
+    def near(r):
+        return chip(r) * 2 + c
 
     def peer(k):
         return (b + k) % PLANE
@@ -324,8 +323,12 @@
     fetches = [
         pltpu.make_async_copy(src, dst, in_s.at[n])
         for n, (src, dst) in enumerate((
-            (wqkv_in, wqkv), (wout_in, wo.at[s]), (tok_in, agf.at[0, b]),
-            (wup_in, wup), (wdown_in, wd.at[s]), (cot_in, agf.at[1, b]),
+            (wqkv_in, wqkv), (wout_in, wo.at[b, pl.ds(pl.multiple_of(s * 32, 32), 32)]),
+            (tok_in.at[pl.ds(0, HALF)], agf.at[0, 0, 0, c]),
+            (tok_in.at[pl.ds(HALF, HALF)], agf.at[0, 0, 1, c]),
+            (wup_in, wup), (wdown_in, wd.at[s]),
+            (cot_in.at[pl.ds(0, HALF)], agf.at[1, 0, 0, c]),
+            (cot_in.at[pl.ds(HALF, HALF)], agf.at[1, 0, 1, c]),
         ))
     ]
     for fetch in fetches:
@@ -344,10 +347,15 @@
     ends = (s == 0) | (s == DEPTH - 1)
     inner = (s > 0) & (s < DEPTH - 1)
 
-    @pl.when(ends)
+    @pl.when(s == 0)
     def _():
-        for kept in (gdr, gur, gqr, gor_):
-            kept[DEPTH - 1 - s] = jnp.zeros(kept.shape[1:], BF16)
+        for kept in (gdr, gur, gqr):
+            kept[0] = jnp.zeros(kept.shape[1:], BF16)
+
+    @pl.when(s == DEPTH - 1)
+    def _():
+        for kept in (gda, guc, gqc):
+            kept[...] = jnp.zeros(kept.shape, BF16)
 
     fetches[0].wait()
     for d in range(PLANE):
@@ -424,131 +432,212 @@
         def _():
             weight_hand(kind, region).wait_send()
 
-    def grad_copy(kind, stage, got, role, to):
-        return rc(stage(to), got(s), z_s.at[kind, role], z_r.at[kind, s], b, to)
-
-    def grad_via(kind, stage, via):
-        return rc(stage(DEPTH - 1 - s), via, z_s.at[kind, 3], za_r.at[kind - 5], b, 1 + s // 3)
+    def grad_up(kind, stage, got, via, t):
+        return rc(stage(t), got(t), z_s.at[kind, t], z_r.at[kind, t], b, s + 1)
+
+    def grad_down_to(kind, stage, got, via, t):
+        return rc(stage(t), got(t), z_s.at[kind, t], z_r.at[kind, t], b, s - 1)
+
+    def grad_down_last(kind, stage, got, via):
+        return rc(stage(s - 1), via, z_s.at[kind, s - 1], za_r.at[kind - 5], b, s - 1)
 
     def grad_start(kind, stage, got, via):
-        @pl.when(ends)
-        def _():
-            grad_via(kind, stage, via).start()
-            grad_copy(kind, stage, got, 0, far).start()
+        @pl.when(s == 0)
+        def _():
+            for t in (3, 2, 1):
+                grad_up(kind, stage, got, via, t).start()
+
+        @pl.when(s == DEPTH - 1)
+        def _():
+            for t in (0, 1):
+                grad_down_to(kind, stage, got, via, t).start()
+            grad_down_last(kind, stage, got, via).start()
+
+    def add_in(kind, stage, got, via, t):
+        rc(got(t), got(t), z_s.at[kind, t], z_r.at[kind, t], b, s).wait_recv()
+        term, more = stage(t), got(t)
+        if len(via.shape) == 3:
+            def add(j, _):
+                term[j] = (term[j].astype(F32) + more[j].astype(F32)).astype(BF16)
+                return 0
+
+            lax.fori_loop(0, via.shape[0], add, 0)
+        else:
+            def add_rows(j, _):
+                rows = pl.ds(pl.multiple_of(j * INNER, INNER), INNER)
+                term[rows, :] = (term[rows, :].astype(F32) + more[rows, :].astype(F32)).astype(BF16)
+                return 0
+
+            lax.fori_loop(0, via.shape[0] // INNER, add_rows, 0)
+
+    def grad_pass(*moved):
+        @pl.when(s == 1)
+        def _():
+            add_in(*moved, 3)
+            grad_up(*moved, 3).start()
+
+        @pl.when(s == 2)
+        def _():
+            add_in(*moved, 0)
+            grad_down_to(*moved, 0).start()
+
+    def grad_pass_on(*moved):
+        @pl.when(s == 1)
+        def _():
+            add_in(*moved, 2)
+            grad_up(*moved, 2).start()
+            add_in(*moved, 0)
+            grad_down_last(*moved).start()
+
+        @pl.when(s == 2)
+        def _():
+            add_in(*moved, 1)
+            grad_down_last(*moved).start()
+            add_in(*moved, 3)
+            grad_up(*moved, 3).start()
+
+    def grad_finish(kind, stage, got, via):
+        @pl.when(s > 0)
+        def _():
+            rc(got(s), got(s), z_s.at[kind, 0], z_r.at[kind, s], b, s).wait_recv()
 
         @pl.when(s < DEPTH - 1)
         def _():
-            grad_copy(kind, stage, got, 1, s + 1).start()
-
-        @pl.when(s > 0)
-        def _():
-            grad_copy(kind, stage, got, 2, s - 1).start()
-
-    def grad_pass(kind, stage, got, via):
-        @pl.when(inner)
-        def _():
-            rc(via, via, z_s.at[kind, 3], za_r.at[kind - 5], b, far).wait_recv()
-            term = stage(far)
-            count = via.shape[0]
-
-            def add(j, _):
-                term[j] = (term[j].astype(F32) + via[j].astype(F32)).astype(BF16)
-                return 0
-
-            if len(via.shape) == 3:
-                lax.fori_loop(0, count, add, 0)
-            else:
-                def add_rows(j, _):
-                    rows = pl.ds(pl.multiple_of(j * INNER, INNER), INNER)
-                    term[rows, :] = (term[rows, :].astype(F32) + via[rows, :].astype(F32)).astype(BF16)
-                    return 0
-
-                lax.fori_loop(0, count // INNER, add_rows, 0)
-            grad_copy(kind, stage, got, 0, far).start()
-
-    def grad_finish(kind, stage, got, via):
-        rc(got(far), got(far), z_s.at[kind, 0], z_r.at[kind, far], b, far).wait_recv()
-
-        @pl.when(s < DEPTH - 1)
-        def _():
-            rc(got(s + 1), got(s + 1), z_s.at[kind, 1], z_r.at[kind, s + 1], b, s + 1).wait_recv()
-
-        @pl.when(s > 0)
-        def _():
-            rc(got(s - 1), got(s - 1), z_s.at[kind, 2], z_r.at[kind, s - 1], b, s - 1).wait_recv()
+            rc(via, via, z_s.at[kind, 0], za_r.at[kind - 5], b, s).wait_recv()
 
     def grad_sent(kind, stage, got, via):
-        grad_copy(kind, stage, got, 0, far).wait_send()
-
-        @pl.when(s < DEPTH - 1)
-        def _():
-            grad_copy(kind, stage, got, 1, s + 1).wait_send()
-
-        @pl.when(s > 0)
-        def _():
-            grad_copy(kind, stage, got, 2, s - 1).wait_send()
-
-        @pl.when(ends)
-        def _():
-            grad_via(kind, stage, via).wait_send()
-
-    results = ((out_o, out_h), (ig_o, ig_h), (gqkv_o, gqkv_h), (gout_o, gout_h), (gup_o, gup_h), (gdown_o, gdown_h))
+        for k in range(1, DEPTH):
+            t = level(k)
+            rc(stage(t), got(t), z_s.at[kind, t], z_r.at[kind, t], b, s).wait_send()
+
+    def direct_copy(kind, stage, got, t):
+        return rc(stage(t), got(s), z_s.at[kind, t], z_r.at[kind, s], b, t)
+
+    def direct_start(kind, stage, got):
+        for t in (3, 2, 1, 0):
+            @pl.when((s != t) & (s < 2))
+            def _():
+                direct_copy(kind, stage, got, t).start()
+
+        for t in (0, 1, 2, 3):
+            @pl.when((s != t) & (s >= 2))
+            def _():
+                direct_copy(kind, stage, got, t).start()
+
+    def direct_finish(kind, stage, got):
+        for k in range(1, DEPTH):
+            t = level(k)
+            rc(got(t), got(t), z_s.at[kind, t], z_r.at[kind, t], b, t).wait_recv()
+
+    def direct_sent(kind, stage, got):
+        for k in range(1, DEPTH):
+            direct_copy(kind, stage, got, level(k)).wait_send()
+
+    results = ((out_o, out_h), (ig_o, ig_h), (gqkv_o, gqkv_h), (gout_o, gout_h), (gup_o, gup_h), (gdown_o, gdown_h),
+               (gain_o, gain_h), (shift_o, shift_h), (lead_o, lead_h), (bias_o, bias_h))
 
     def deliver(n):
         return pltpu.make_async_copy(results[n][0], results[n][1], out_s.at[n])
 
-    w_out_z = (1, lambda t: wo.at[t])
+    w_out_z = (1, lambda t: wo.at[b, pl.ds(pl.multiple_of(t * 32, 32), 32)])
     w_qkv_z = (2, lambda t: wq.at[:, t])
     w_up_z = (3, lambda t: wu.at[:, t])
     w_down_z = (4, lambda t: wd.at[t])
     g_down_z = (5, lambda t: gds.at[t], lambda t: gdr.at[t], gda)
     g_up_z = (6, lambda t: gus.at[:, t], lambda t: gur.at[t], guc)
     g_qkv_z = (7, lambda t: gqs.at[:, t], lambda t: gqr.at[t], gqc)
-    g_out_z = (8, lambda t: gos.at[t], lambda t: gor_.at[t], goc)
-
-    def gather(op, r, half):
-        dst = chip(r) * 2 + c
-        rows = pl.ds(HALF * ((half + r) % 2), HALF)
+    g_out_z = (8, lambda t: gos.at[t], lambda t: gor_.at[t])
+
+    def gather(op, r, turn):
         return rc(
-            agf.at[op, b, rows], agf.at[op, b, rows],
-            ag_s.at[op, r - 1, half], ag_r.at[op, r - 1, half], dst, s,
+            agf.at[op, 0, (turn + r) % 2, c], agf.at[op, 1 + turn, r - 1, c],
+            ag_s.at[op, r - 1, turn], ag_r.at[op, r - 1, turn], near(r), s,
         )
 
     def across(op, r):
-        blk = chip(r) * 2 + c
-        rows = pl.ds(HALF * (r % 2), HALF)
         return rc(
-            agf.at[op, blk, rows], agf.at[op, blk, rows],
-            ac_s.at[op, r - 1], ac_r.at[op, r - 1], chip(3 - r) * 2 + c, s,
-        )
-
-    def share(op, r):
-        blk = chip(r) * 2 + c
-        return rc(agf.at[op, blk], agf.at[op, blk], fw_s.at[op, r], fw_r.at[op, r], mate, s)
+            agf.at[op, 1, r - 1, c], agf.at[op, 3, r % 2, c],
+            ac_s.at[op, r - 1], ac_r.at[op, r - 1], near(3 - r), s,
+        )
+
+    def share(op, blk):
+        return rc(
+            agf.at[op, blk, :, c], agf.at[op, blk, :, c],
+            fw_s.at[op, blk], fw_r.at[op, blk], mate, s,
+        )
 
     def start_gather(op):
-        for half in (0, 1):
+        for turn in (0, 1):
             for r in (1, 2):
-                gather(op, r, half).start()
+                gather(op, r, turn).start()
         share(op, 0).start()
 
-    def pass_first(op):
-        for r in (1, 2):
-            gather(op, r, 0).wait_recv()
-            across(op, r).start()
-
-    def pass_second(op):
-        for r in (1, 2):
-            gather(op, r, 1).wait_recv()
-            share(op, r).start()
-
-    def pass_far(op):
-        across(op, 1).wait_recv()
-        across(op, 2).wait_recv()
-        share(op, 3).start()
-
-    def block(op, q):
-        return agf[op, pl.ds(2 * q, 2)].reshape(BLOCK, -1)
+    def arrive(op, blk):
+        if blk in (1, 2):
+            for r in (1, 2):
+                gather(op, r, blk - 1).wait_recv()
+                if blk == 1:
+                    across(op, r).start()
+        if blk == 3:
+            across(op, 1).wait_recv()
+            across(op, 2).wait_recv()
+        if blk:
+            share(op, blk).start()
+
+    def block(op, i):
+        return agf[op, i].reshape(BLOCK, -1)
+
+    def rows_half(dev, h):
+        return wo.at[dev, pl.ds(h * HALF, HALF)]
+
+    def rows_copy(r, turn):
+        part_ = rows_half(b, (turn + r) % 2)
+        return rc(part_, part_, wg_s.at[r - 1, turn], wg_r.at[r - 1, turn], near(r), s)
+
+    def rows_across(r):
+        part_ = rows_half(near(r), r % 2)
+        return rc(part_, part_, wg_s.at[2, r - 1], wg_r.at[2, r - 1], near(3 - r), s)
+
+    def rows_share(r):
+        dev = near(r) if r else b
+        return rc(wo.at[dev], wo.at[dev], wg_s.at[3, r], wg_r.at[3, r], mate, s)
+
+    def rows_start():
+        for turn in (0, 1):
+            for r in (1, 2):
+                rows_copy(r, turn).start()
+        rows_share(0).start()
+
+    def granule(i, a):
+        return (i, a) if i in (0, 3) else (a + 1, 1 - a if i == 1 else a)
+
+    GRANULES = [(i, a) for i in (3, 2, 1, 0) for a in (0, 1)]
+
+    def heads_copy(i, a, k):
+        r, h = granule(i, a)
+        rows = pl.ds(pl.multiple_of((a * 2 + k) * HALF, HALF), HALF)
+        return rc(
+            att.at[i, rows], aown.at[b, pl.ds(h * HALF, HALF)],
+            h_s.at[i, a, k], h_r.at[r, h, c], chip(r) * 2 + k, s,
+        )
+
+    def heads_from(r, h, k):
+        dst = aown.at[chip(r) * 2 + k, pl.ds(h * HALF, HALF)]
+        return rc(dst, dst, h_s.at[0, 0, 0], h_r.at[r, h, k], mate, s)
+
+    def cores(i):
+        return (1 - c,) if i == 0 else (0, 1)
+
+    def back_copy(i, a, k):
+        r, h = granule(i, a)
+        dev = chip(r) * 2 + k
+        return rc(
+            dsend.at[dev, pl.ds(h * HALF, HALF)], dob.at[i, a, c],
+            g_s.at[i, a, k], g_r.at[i, a, c], dev, s,
+        )
+
+    def back_from(i, a, k):
+        return rc(dob.at[i, a, k], dob.at[i, a, k], g_s.at[0, 0, 0], g_r.at[i, a, k], mate, s)
 
     def swap(kind, k, src, dst):
         return rc(src, dst, aq_s.at[kind, k - 1], aq_r.at[kind, k - 1], peer(k), s)
@@ -559,10 +648,11 @@
         swap(0, k, sq.at[peer(k)], wq.at[b, s]).start()
     weight_start(*w_out_z)
     fetches[2].wait()
+    fetches[3].wait()
     for r in (1, 2):
         gather(0, r, 0).start()
     wq[b, s] = sq[b]
-    fetches[3].wait()
+    fetches[4].wait()
     for d in range(PLANE):
         su[d] = wup[:, d * 512:(d + 1) * 512]
     wu[b, s] = su[b]
@@ -588,7 +678,12 @@
     weight_start(*w_qkv_z)
     for k in range(1, PLANE):
         swap(1, k, su.at[peer(k)], wu.at[b, s]).start()
-    pass_first(0)
+    arrive(0, 1)
+    fetches[6].wait()
+    fetches[7].wait()
+    for r in (1, 2):
+        gather(1, r, 0).start()
+    share(1, 0).start()
     for k in range(1, PLANE):
         spread(k).wait_recv()
     for d in range(PLANE):
@@ -610,49 +705,55 @@
         rstd = lax.rsqrt(variance + eps)
         return centered * rstd, rstd
 
-    for d in range(PLANE):
-        row = jnp.broadcast_to(vecf[d].astype(F32)[10:11, :], (128, 128))
-        column = row.T - 1.0
-        kaug[d * 128:(d + 1) * 128, 128:256] = (column * ends_lane).astype(BF16)
+    for r in range(4):
+        for k in range(2):
+            row = jnp.broadcast_to(vecf[chip(r) * 2 + k].astype(F32)[10:11, :], (128, 128))
+            column = ((row.T - 1.0) * ends_lane).astype(BF16)
+            for h in range(2):
+                if r in (0, 3):
+                    blk, a = r, h
+                else:
+                    blk, a = (1 if h == r % 2 else 2), r - 1
+                top = blk * BLOCK + (a * 2 + k) * HALF
+                kaug[top:top + HALF, 128:256] = column[h * HALF:(h + 1) * HALF]
     for h in range(2):
-        for q in range(CHIPS):
-            qaug[h, q, :, 128:256] = jnp.broadcast_to(ones_lane, (BLOCK, 128)).astype(BF16)
-
-    def norm_block(d):
+        for i in range(4):
+            qaug[h, i, :, 128:256] = jnp.broadcast_to(ones_lane, (BLOCK, 128)).astype(BF16)
+
+    def norm_block(i):
         def chunk(j, _):
-            rows = pl.ds(pl.multiple_of(j * INNER, INNER), INNER)
-            ent = agf[0, d, rows, :].astype(F32) + lead_row
+            rows = pl.ds(pl.multiple_of((j % 2) * INNER, INNER), INNER)
+            ent = agf[0, i, j // 4, (j // 2) % 2, rows, :].astype(F32) + lead_row
             xhat = stats(ent)[0]
-            normed[d, rows, :] = (xhat * gain1 + shift1).astype(BF16)
+            put = pl.ds(pl.multiple_of(j * INNER, INNER), INNER)
+            normed[i, put, :] = (xhat * gain1 + shift1).astype(BF16)
             return 0
 
-        lax.fori_loop(0, ROWS // INNER, chunk, 0)
-
-    norm_block(b)
+        lax.fori_loop(0, BLOCK // INNER, chunk, 0)
+
     share(0, 0).wait_recv()
-    norm_block(mate)
-    pass_second(0)
-    for r in (1, 2):
-        norm_block(chip(r) * 2 + c)
-        share(0, r).wait_recv()
-        norm_block(chip(r) * 2 + 1 - c)
+    norm_block(0)
+    share(0, 1).wait_recv()
+    arrive(0, 2)
+    norm_block(1)
+    weight_pass(*w_out_z)
     weight_pass(*w_qkv_z)
-    pass_far(0)
-    fetches[5].wait()
-    start_gather(1)
-    norm_block(chip(3) * 2 + c)
+    share(0, 2).wait_recv()
+    norm_block(2)
+    weight_finish(*w_out_z)
+    rows_start()
+    arrive(0, 3)
     share(0, 3).wait_recv()
-    norm_block(chip(3) * 2 + 1 - c)
+    norm_block(3)
 
     for k in range(1, PLANE):
         swap(1, k, su.at[peer(k)], wu.at[b, s]).wait_recv()
-    weight_pass(*w_out_z)
     weight_finish(*w_qkv_z)
     weight_start(*w_up_z)
 
     def project_block(q, _):
         rows = pl.ds(pl.multiple_of(q * BLOCK, BLOCK), BLOCK)
-        pj = mm(normed[pl.ds(2 * q, 2)].reshape(BLOCK, width), wq[...].reshape(width, 384))
+        pj = mm(normed[q], wq[...].reshape(width, 384))
         qv = (pj[:, 0:128] + mine[3:4, :]).astype(BF16).astype(F32) * 0.125
         for h in range(2):
             qaug[h, q, :, 0:128] = (qv * head_lane[h]).astype(BF16)
@@ -664,144 +765,202 @@
         vt2[:, rows] = vb.T
         return 0
 
-    lax.fori_loop(0, CHIPS, project_block, 0)
-    weight_finish(*w_out_z)
-
-    def mate_copy(op, slot, r):
-        return rc(part.at[slot, r, 1 - c], pr.at[op, r], p_s.at[op, r], p_r.at[op, r], mate, s)
-
-    def chip_copy(op, slot, r):
-        return rc(cs.at[slot, r], rr.at[op, r], c_s.at[op, r], c_r.at[op, r], chip(r) * 2 + c, s)
-
-    def put_part(op, slot, r, blk):
-        part[slot, r] = blk.astype(BF16).reshape(2, ROWS, width)
-        mate_copy(op, slot, r).start()
-
-    def fold(op, slot, r, send=True):
-        mate_copy(op, slot, r).wait_recv()
+    lax.fori_loop(0, 4, project_block, 0)
+
+    def mate_copy(op, i):
+        return rc(part.at[op, i, :, 1 - c], pr.at[op, i], p_s.at[op, i], p_r.at[op, i], mate, s)
+
+    def far_copy(op, h):
+        return rc(cs.at[op, 3, h], au.at[op, 1 - h], f_s.at[op, h], f_r.at[op, 1 - h], near(h + 1), s)
+
+    def near_copy(op, i, a):
+        h = a if i == 2 else 1 - a
+        return rc(cs.at[op, i, a], rr.at[op, a, h], n_s.at[op, a, h], n_r.at[op, a, h], near(a + 1), s)
+
+    def put_part(op, i, blk):
+        part[op, i] = blk.astype(BF16).reshape(2, 2, HALF, width)
+        mate_copy(op, i).start()
+
+    def fold(op, i):
+        mate_copy(op, i).wait_recv()
 
         def chunk(j, _):
-            rows = pl.ds(pl.multiple_of(j * INNER, INNER), INNER)
-            cs[slot, r, rows, :] = (
-                part[slot, r, c, rows, :].astype(F32) + pr[op, r, rows, :].astype(F32)
+            a = j // 2
+            rows = pl.ds(pl.multiple_of((j % 2) * INNER, INNER), INNER)
+            cs[op, i, a, rows, :] = (
+                part[op, i, a, c, rows, :].astype(F32) + pr[op, i, a, rows, :].astype(F32)
             ).astype(BF16)
             return 0
 
         lax.fori_loop(0, ROWS // INNER, chunk, 0)
 
-        if send:
-            @pl.when(r > 0)
+    def fold_before(op, i, near_too=True):
+        @pl.when(i < 3)
+        def _():
+            fold(op, i + 1)
+
+        @pl.when(i == 2)
+        def _():
+            send_far(op)
+
+        if near_too:
+            @pl.when(i == 1)
             def _():
-                chip_copy(op, slot, r).start()
-
-    def plane_total(op, slot, rows):
-        total = cs[slot, 0, rows, :].astype(F32)
-        for r in (1, 2, 3):
-            total = total + rr[op, r, rows, :].astype(F32)
-        return total
-
-    def end_sums(op, slot):
-        for r in range(CHIPS):
-            mate_copy(op, slot, r).wait_send()
-        for r in (1, 2, 3):
-            chip_copy(op, slot, r).wait_send()
-
-    def attend_block(i, _):
-        r = 3 - i
-        q = chip(r)
-
-        @pl.when(i == 1)
-        def _():
-            pass_first(1)
-            pass_second(1)
-
-        def head(h, _):
-            top = pl.ds(pl.multiple_of(h * 64, 64), 64)
-            st = mm(kaug[...], qaug[h, q], NT)
+                send_near(op, 2)
+
+    def send_far(op):
+        for h in (0, 1):
+            far_copy(op, h).start()
+
+    def send_near(op, i):
+        for a in (0, 1):
+            near_copy(op, i, a).start()
+
+    def send_last(op):
+        for a in (0, 1):
+            far_copy(op, 1 - a).wait_recv()
+
+            def chunk(j, _):
+                rows = pl.ds(pl.multiple_of(j * INNER, INNER), INNER)
+                cs[op, 1, a, rows, :] = (
+                    cs[op, 1, a, rows, :].astype(F32) + au[op, a, rows, :].astype(F32)
+                ).astype(BF16)
+                return 0
+
+            lax.fori_loop(0, HALF // INNER, chunk, 0)
+            near_copy(op, 1, a).start()
+
+    def wait_sums(op):
+        for i in (2, 1):
+            for a in (0, 1):
+                near_copy(op, i, a).wait_recv()
+
+    def place(j):
+        return j // 2, pl.ds(pl.multiple_of((j % 2) * INNER, INNER), INNER)
+
+    def plane_total(op, j):
+        h, rows = place(j)
+        total = cs[op, 0, h, rows, :].astype(F32)
+        return total + rr[op, 0, h, rows, :].astype(F32) + rr[op, 1, h, rows, :].astype(F32)
+
+    def own_rows(op, j):
+        h, rows = place(j)
+        return agf[op, 0, h, c, rows, :].astype(F32)
+
+    def set_rows(op, j, v):
+        h, rows = place(j)
+        agf[op, 0, h, c, rows, :] = v
+
+    def end_sums(op):
+        for i in range(4):
+            mate_copy(op, i).wait_send()
+        for h in (0, 1):
+            far_copy(op, h).wait_send()
+        for i in (2, 1):
+            for a in (0, 1):
+                near_copy(op, i, a).wait_send()
+
+    def attend_block(n, _):
+        i = 3 - n
+
+        @pl.when(n == 3)
+        def _():
+            for r in (1, 2):
+                rows_copy(r, 1).wait_recv()
+                rows_share(r).start()
+
+        for h in range(2):
+            st = mm(kaug[...], qaug[h, i], NT)
             p = jnp.exp(st - jnp.max(st, axis=0, keepdims=True))
             inverse = 1.0 / jnp.sum(p, axis=0, keepdims=True)
             pb = p.astype(BF16)
-            pst[h, q] = pb
-            ot[q, top, :] = mm(vt2[top, :], pb) * inverse
-            invl[q, h] = jnp.broadcast_to(inverse, (8, BLOCK))
-            return 0
-
-        lax.fori_loop(0, 2, head, 0)
-        low = ot[q].T.astype(BF16)
-        att[q] = low
-        put_part(0, 0, r, mm(low, wo[...].reshape(128, width)))
-
-        @pl.when(i > 0)
-        def _():
-            fold(0, 0, r + 1)
+            pst[h, i] = pb
+            ot[i, h * 64:(h + 1) * 64, :] = mm(vt2[h * 64:(h + 1) * 64, :], pb) * inverse
+            invl[i, h] = jnp.broadcast_to(inverse, (8, BLOCK))
+        att[i] = ot[i].T.astype(BF16)
+        for blk in range(4):
+            @pl.when(i == blk)
+            def _():
+                for a in (0, 1):
+                    for k in cores(blk):
+                        heads_copy(blk, a, k).start()
 
         return 0
 
-    lax.fori_loop(0, CHIPS, attend_block, 0)
-    fold(0, 0, 0)
+    arrive(1, 1)
+    for r in (1, 2):
+        rows_copy(r, 0).wait_recv()
+        rows_across(r).start()
+    lax.fori_loop(0, 4, attend_block, 0)
+    for r in (1, 2):
+        gather(1, r, 1).start()
+    for h in (0, 1):
+        top = pl.multiple_of((h * 2 + c) * HALF, HALF)
+        aown[b, h * HALF:(h + 1) * HALF] = att[0, pl.ds(top, HALF), :]
     weight_pass(*w_up_z)
-    fetches[4].wait()
-    weight_start(*w_down_z)
-    for r in (1, 2, 3):
-        chip_copy(0, 0, r).wait_recv()
+    fetches[5].wait()
+
+    @pl.when(inner)
+    def _():
+        weight_start(*w_down_z)
+
+    arrive(1, 3)
+    for r in (1, 2):
+        rows_across(r).wait_recv()
+    rows_share(3).start()
+    for r in range(4):
+        rows_share(r).wait_recv()
+    for r in (3, 2, 1, 0):
+        for h in (0, 1):
+            for k in cores(r):
+                heads_from(r, h, k).wait_recv()
+    heads = jnp.concatenate([aown[d] for d in range(PLANE)], axis=1)
+    mid[...] = mm(heads, wo[...].reshape(1024, width))
 
     def middle_chunk(j, _):
         rows = pl.ds(pl.multiple_of(j * INNER, INNER), INNER)
-        ent = agf[0, b, rows, :].astype(F32) + lead_row
-        m = ent + plane_total(0, 0, rows) + shift_out
+        m = own_rows(0, j) + lead_row + mid[rows, :] + shift_out
         mid[rows, :] = m
-        agf[2, b, rows, :] = (stats(m)[0] * gain2 + shift2).astype(BF16)
+        set_rows(2, j, (stats(m)[0] * gain2 + shift2).astype(BF16))
         return 0
 
     lax.fori_loop(0, ROWS // INNER, middle_chunk, 0)
     start_gather(2)
-    pass_far(1)
-    end_sums(0, 0)
 
     weight_finish(*w_up_z)
+
+    @pl.when(ends)
+    def _():
+        weight_start(*w_down_z)
+
     bias = jnp.concatenate([mine[11 + j:12 + j, :] for j in range(4)], axis=1)
 
     def arrivals(op, i):
-        @pl.when(i == 0)
-        def _():
-            share(op, 0).wait_recv()
-
-        @pl.when(i == 1)
-        def _():
-            pass_first(op)
-            pass_second(op)
-            share(op, 1).wait_recv()
-
-        @pl.when(i == 2)
-        def _():
-            share(op, 2).wait_recv()
-
-        @pl.when(i == 3)
-        def _():
-            pass_far(op)
-            share(op, 3).wait_recv()
+        for blk in range(4):
+            @pl.when(i == blk)
+            def _():
+                arrive(op, blk)
+                share(op, blk).wait_recv()
 
     def up_block(i, _):
         arrivals(2, i)
-        q = chip(i)
-
-        @pl.when(i == 2)
-        def _():
-            weight_pass(*w_down_z)
-
-        hp = mm(block(2, q), wu[...].reshape(width, 512)) + bias
+
+
+        hp = mm(block(2, i), wu[...].reshape(width, 512)) + bias
         phi = 0.5 + 0.5 * lax.erf(hp * 0.7071067811865476)
-        hid[pl.ds(pl.multiple_of(q * BLOCK, BLOCK), BLOCK), :] = (hp * phi).astype(BF16)
-        gder[q] = phi + hp * jnp.exp(hp * hp * -0.5) * 0.3989422804014327
+        hid[pl.ds(pl.multiple_of(i * BLOCK, BLOCK), BLOCK), :] = (hp * phi).astype(BF16)
+        gder[i] = phi + hp * jnp.exp(hp * hp * -0.5) * 0.3989422804014327
         return 0
 
-    lax.fori_loop(0, CHIPS, up_block, 0)
-    for r in range(CHIPS):
-        share(1, r).wait_recv()
+    lax.fori_loop(0, 4, up_block, 0)
+    weight_pass(*w_down_z)
+    arrive(1, 2)
+    for i in range(4):
+        share(1, i).wait_recv()
 
     def down_grad(f, _):
         cols = pl.ds(pl.multiple_of(f * BLOCK, BLOCK), BLOCK)
-        g = mm(hid[:, cols], agf[1].reshape(PLANE * ROWS, width), TN)
+        g = mm(hid[:, cols], agf[1].reshape(1024, width), TN)
         gds[pl.ds(2 * f, 2)] = g.astype(BF16).reshape(2, 128, width)
         return 0
 
@@ -810,52 +969,42 @@
     weight_finish(*w_down_z)
     gub[...] = jnp.zeros_like(gub)
 
-    def back_block(i, _):
-        r = 3 - i
-        q = chip(r)
-        rows = pl.ds(pl.multiple_of(q * BLOCK, BLOCK), BLOCK)
-        gh = mm(block(1, q), wd[...].reshape(512, width), NT)
-        gp = (gder[q] * gh).astype(BF16)
+    def back_block(n, _):
+        i = 3 - n
+        rows = pl.ds(pl.multiple_of(i * BLOCK, BLOCK), BLOCK)
+        gh = mm(block(1, i), wd[...].reshape(512, width), NT)
+        gp = (gder[i] * gh).astype(BF16)
         gpre[rows, :] = gp
         gub[...] += jnp.sum(gp.astype(F32).reshape(BLOCK // 8, 8, 512), axis=0)
-        put_part(1, 1, r, mm(gp, wu[...].reshape(width, 512), NT))
-
-        @pl.when(i > 0)
-        def _():
-            fold(1, 1, r + 1)
-
+        put_part(0, i, mm(gp, wu[...].reshape(width, 512), NT))
+        fold_before(0, i)
         return 0
 
-    lax.fori_loop(0, CHIPS, back_block, 0)
-    fold(1, 1, 0)
+    lax.fori_loop(0, 4, back_block, 0)
+    fold(0, 0)
 
     def up_grad(f, _):
         cols = pl.ds(pl.multiple_of(f * BLOCK, BLOCK), BLOCK)
-        g = mm(agf[2, :, :, cols].reshape(PLANE * ROWS, BLOCK), gpre[...], TN)
+        g = mm(agf[2, :, :, :, :, cols].reshape(1024, BLOCK), gpre[...], TN)
         gus[pl.ds(2 * f, 2)] = g.astype(BF16).reshape(2, 4, 32, 512)
         return 0
 
-    lax.fori_loop(0, CHIPS, up_grad, 0)
+    grad_pass(*g_down_z)
+    lax.fori_loop(0, 4, up_grad, 0)
     grad_start(*g_up_z)
 
-    def out_block(i, _):
-        r = 3 - i
-        q = chip(r)
-        rows = pl.ds(pl.multiple_of(q * BLOCK, BLOCK), BLOCK)
-        put_part(2, 2, r, mm(hid[rows, :], wd[...].reshape(512, width)))
-
-        @pl.when(i > 0)
-        def _():
-            fold(2, 2, r + 1, send=False)
-
+    def out_block(n, _):
+        i = 3 - n
+        rows = pl.ds(pl.multiple_of(i * BLOCK, BLOCK), BLOCK)
+        put_part(1, i, mm(hid[rows, :], wd[...].reshape(512, width)))
+        fold_before(1, i, near_too=False)
         return 0
 
-    lax.fori_loop(0, CHIPS, out_block, 0)
-    fold(2, 2, 0, send=False)
-
-    grad_pass(*g_down_z)
-    for r in (1, 2, 3):
-        chip_copy(1, 1, r).wait_recv()
+    send_last(0)
+    lax.fori_loop(0, 4, out_block, 0)
+    fold(1, 0)
+
+    wait_sums(0)
     acc[...] = jnp.zeros_like(acc)
 
     def add_row(n, v):
@@ -870,20 +1019,30 @@
 
     def second_chunk(j, _):
         rows = pl.ds(pl.multiple_of(j * INNER, INNER), INNER)
-        gs = plane_total(1, 1, rows)
+        gs = plane_total(0, j)
         g, xhat = norm_back(mid[rows, :], gs, gain2)
-        ct = agf[1, b, rows, :].astype(F32)
+        ct = own_rows(1, j)
         gm = ct + g
         gmid[rows, :] = gm
         gb = gm.astype(BF16)
-        agf[3, b, rows, :] = gb
+        set_rows(3, j, gb)
         add_row(1, gs * xhat)
         add_row(6, gs)
         add_row(5, gb.astype(F32))
         add_row(7, ct)
         return 0
 
+    grad_pass_on(*g_down_z)
     lax.fori_loop(0, ROWS // INNER, second_chunk, 0)
+    gbo = agf[3, 0, :, c].reshape(ROWS, width)
+    gha = mm(gbo, wo[...].reshape(1024, width), NT).astype(BF16)
+    for d in range(PLANE):
+        dsend[d] = gha[:, d * 128:(d + 1) * 128]
+    for i, a in GRANULES:
+        for k in cores(i):
+            back_copy(i, a, k).start()
+    for h in (0, 1):
+        dob[0, h, c] = dsend[b, h * HALF:(h + 1) * HALF, :]
     start_gather(3)
 
     dk[...] = jnp.zeros_like(dk)
@@ -891,26 +1050,29 @@
     goa[...] = jnp.zeros_like(goa)
 
     def attend_back(i, _):
-        arrivals(3, i)
+        for blk in range(4):
+            @pl.when(i == blk)
+            def _():
+                for a in (0, 1):
+                    for k in cores(blk):
+                        back_from(blk, a, k).wait_recv()
 
         @pl.when(i == 2)
         def _():
-            for r in (3, 2, 1):
-                chip_copy(2, 2, r).start()
+            send_near(1, 2)
+            send_last(1)
 
         @pl.when(i == 3)
         def _():
+            arrive(3, 1)
             grad_pass(*g_up_z)
 
-        q = chip(i)
-        gbk = block(3, q)
-        wo_all = wo[...].reshape(128, width)
-        dot_t = mm(wo_all, gbk, NT)
+        dot_t = dob[i].reshape(BLOCK, 128).astype(F32).T
         inv = jnp.concatenate(
-            [jnp.broadcast_to(invl[q, h, 0:1, :], (64, BLOCK)) for h in range(2)], axis=0
+            [jnp.broadcast_to(invl[i, h, 0:1, :], (64, BLOCK)) for h in range(2)], axis=0
         )
         dos = dot_t * inv
-        prod = dos * ot[q]
+        prod = dos * ot[i]
         deltas = [jnp.sum(prod[h * 64:(h + 1) * 64], axis=0, keepdims=True) for h in range(2)]
         do_rows = dos.T
         zero = jnp.zeros((64, BLOCK), F32)
@@ -918,80 +1080,76 @@
         for h in range(2):
             halves = [dos[0:64], zero] if h == 0 else [zero, dos[64:128]]
             dp = mm(vv[...], jnp.concatenate(halves, axis=0).astype(BF16))
-            pb = pst[h, q]
+            pb = pst[h, i]
             ds = (pb.astype(F32) * (dp - deltas[h])).astype(BF16)
             dv[...] += mm(pb, (do_rows * head_lane[h]).astype(BF16))
-            dk[...] += mm(ds, qaug[h, q, :, 0:128])
+            dk[...] += mm(ds, qaug[h, i, :, 0:128])
             dq_parts.append(mm(kt[h * 64:(h + 1) * 64, :], ds))
         dq = jnp.concatenate(dq_parts, axis=0).T * 0.125
-        gproj[pl.ds(pl.multiple_of(q * BLOCK, BLOCK), BLOCK), 0:128] = dq.astype(BF16)
-        goa[...] += mm(att[q], gbk, TN)
+        gproj[pl.ds(pl.multiple_of(i * BLOCK, BLOCK), BLOCK), 0:128] = dq.astype(BF16)
         return 0
 
-    lax.fori_loop(0, CHIPS, attend_back, 0)
+    lax.fori_loop(0, 4, attend_back, 0)
     gproj[:, 128:256] = dk[...].astype(BF16)
     gproj[:, 256:384] = dv[...].astype(BF16)
 
     def qkv_grad(f, _):
         cols = pl.ds(pl.multiple_of(f * BLOCK, BLOCK), BLOCK)
-        g = mm(normed[:, :, cols].reshape(PLANE * ROWS, BLOCK), gproj[...], TN)
+        g = mm(normed[:, :, cols].reshape(1024, BLOCK), gproj[...], TN)
         gqs[pl.ds(2 * f, 2)] = g.astype(BF16).reshape(2, 4, 32, 384)
         return 0
 
-    lax.fori_loop(0, CHIPS, qkv_grad, 0)
+    lax.fori_loop(0, 4, qkv_grad, 0)
+    grad_start(*g_qkv_z)
+
+    def project_back(n, _):
+        i = 3 - n
+        rows = pl.ds(pl.multiple_of(i * BLOCK, BLOCK), BLOCK)
+        put_part(2, i, mm(gproj[rows, :], wq[...].reshape(width, 384), NT))
+        fold_before(2, i)
+        return 0
+
+    arrive(3, 2)
+    lax.fori_loop(0, 4, project_back, 0)
+    fold(2, 0)
+
+    grad_pass_on(*g_up_z)
+    share(3, 0).wait_recv()
+    arrive(3, 3)
+
+    def out_grad(i, _):
+        for blk in (1, 2, 3):
+            @pl.when(i == blk)
+            def _():
+                share(3, blk).wait_recv()
+
+        goa[...] += mm(att[i], block(3, i), TN)
+        return 0
+
+    lax.fori_loop(0, 4, out_grad, 0)
     gos[...] = goa[...].astype(BF16).reshape(4, 32, width)
-    grad_start(*g_out_z)
-    grad_start(*g_qkv_z)
-
-    def project_back(i, _):
-        r = 3 - i
-        q = chip(r)
-        rows = pl.ds(pl.multiple_of(q * BLOCK, BLOCK), BLOCK)
-        put_part(3, 0, r, mm(gproj[rows, :], wq[...].reshape(width, 384), NT))
-
-        @pl.when(i > 0)
-        def _():
-            fold(3, 0, r + 1)
-
-        return 0
-
-    lax.fori_loop(0, CHIPS, project_back, 0)
-    fold(3, 0, 0)
-
-    def others(got):
+
+    @pl.when(ends)
+    def _():
+        direct_start(*g_out_z)
+
+    send_last(2)
+    def others(kind, stage, got, via):
+        return [got(s), via]
+
+    def from_planes(got):
         return [got(level(k)) for k in range(1, DEPTH)]
 
     grad_finish(*g_down_z)
-    gdown_o[...] = sum([t[...].astype(F32) for t in others(g_down_z[2])], gds[s].astype(F32))
+    gdown_o[...] = sum([t[...].astype(F32) for t in others(*g_down_z)], gds[s].astype(F32))
     deliver(5).start()
-    for r in (1, 2, 3):
-        chip_copy(2, 2, r).wait_recv()
-
-    def output_chunk(j, _):
-        rows = pl.ds(pl.multiple_of(j * INNER, INNER), INNER)
-        out_o[rows, :] = (mid[rows, :] + plane_total(2, 2, rows) + shift_down).astype(BF16)
-        return 0
-
-    lax.fori_loop(0, ROWS // INNER, output_chunk, 0)
-    deliver(0).start()
-
-    grad_pass(*g_out_z)
     grad_pass(*g_qkv_z)
-    grad_finish(*g_up_z)
-    for d in range(PLANE):
-        gu2[d] = sum(
-            [t[d].astype(F32) for t in others(g_up_z[2])], gus[d, s].astype(F32)
-        ).astype(BF16)
-    for k in range(1, PLANE):
-        swap(2, k, gu2.at[peer(k)], gua.at[b]).start()
-    gua[b] = gu2[b]
-    for r in (1, 2, 3):
-        chip_copy(3, 0, r).wait_recv()
+    wait_sums(2)
 
     def first_chunk(j, _):
         rows = pl.ds(pl.multiple_of(j * INNER, INNER), INNER)
-        gn = plane_total(3, 0, rows)
-        g, xhat = norm_back(agf[0, b, rows, :].astype(F32) + lead_row, gn, gain1)
+        gn = plane_total(2, j)
+        g, xhat = norm_back(own_rows(0, j) + lead_row, gn, gain1)
         ge = gmid[rows, :] + g
         ig_o[rows, :] = ge.astype(BF16)
         add_row(0, gn * xhat)
@@ -1022,6 +1180,30 @@
         + [jnp.zeros((1, 128), F32)],
         axis=0,
     )
+    wait_sums(1)
+
+    def output_chunk(j, _):
+        rows = pl.ds(pl.multiple_of(j * INNER, INNER), INNER)
+        out_o[rows, :] = (mid[rows, :] + plane_total(1, j) + shift_down).astype(BF16)
+        return 0
+
+    lax.fori_loop(0, ROWS // INNER, output_chunk, 0)
+    deliver(0).start()
+
+    grad_finish(*g_up_z)
+    for d in range(PLANE):
+        gu2[d] = sum(
+            [t[d].astype(F32) for t in others(*g_up_z)], gus[d, s].astype(F32)
+        ).astype(BF16)
+    for k in range(1, PLANE):
+        swap(2, k, gu2.at[peer(k)], gua.at[b]).start()
+    gua[b] = gu2[b]
+    grad_pass_on(*g_qkv_z)
+
+    @pl.when(inner)
+    def _():
+        direct_start(*g_out_z)
+
     for k in range(1, PLANE):
         vec_swap(k).wait_recv()
     total = vs[b] + extra
@@ -1031,17 +1213,17 @@
     for k in range(1, DEPTH):
         yc(1, k, vz, vzr.at[k - 1]).start()
 
-    grad_finish(*g_out_z)
-    gout_o[...] = sum([t[...].astype(F32) for t in others(g_out_z[2])], gos[s].astype(F32))
-    deliver(3).start()
     grad_finish(*g_qkv_z)
     for d in range(PLANE):
         gq2[d] = sum(
-            [t[d].astype(F32) for t in others(g_qkv_z[2])], gqs[d, s].astype(F32)
+            [t[d].astype(F32) for t in others(*g_qkv_z)], gqs[d, s].astype(F32)
         ).astype(BF16)
     for k in range(1, PLANE):
         swap(3, k, gq2.at[peer(k)], gqa.at[b]).start()
     gqa[b] = gq2[b]
+    direct_finish(*g_out_z)
+    gout_o[...] = sum([t[...].astype(F32) for t in from_planes(g_out_z[2])], gos[s].astype(F32))
+    deliver(3).start()
     for k in range(1, PLANE):
         swap(2, k, gu2.at[peer(k)], gua.at[b]).wait_recv()
     for d in range(PLANE):
@@ -1055,6 +1237,8 @@
     shift_o[...] = columns[2:8, 0:32]
     lead_o[...] = columns[8:10, 0:32]
     bias_o[...] = jnp.sum(jnp.where(line == 11 + s, vz_sum, 0.0), axis=0, keepdims=True)
+    for n in range(6, 10):
+        deliver(n).start()
     for k in range(1, PLANE):
         swap(3, k, gq2.at[peer(k)], gqa.at[b]).wait_recv()
     for d in range(PLANE):
@@ -1069,10 +1253,20 @@
             gather(op, r, 0).wait_send()
             gather(op, r, 1).wait_send()
             across(op, r).wait_send()
-        for r in range(CHIPS):
-            share(op, r).wait_send()
-    for op, slot in ((1, 1), (2, 2), (3, 0)):
-        end_sums(op, slot)
+        for i in range(4):
+            share(op, i).wait_send()
+    for op in range(3):
+        end_sums(op)
+    for r in (1, 2):
+        rows_copy(r, 0).wait_send()
+        rows_copy(r, 1).wait_send()
+        rows_across(r).wait_send()
+    for r in range(4):
+        rows_share(r).wait_send()
+    for i, a in GRANULES:
+        for k in cores(i):
+            heads_copy(i, a, k).wait_send()
+            back_copy(i, a, k).wait_send()
     for k in range(1, PLANE):
         swap(0, k, sq.at[peer(k)], wq.at[b, s]).wait_send()
         swap(1, k, su.at[peer(k)], wu.at[b, s]).wait_send()
@@ -1085,19 +1279,24 @@
         yc(1, k, vz, vzr.at[k - 1]).wait_send()
     for moved in (w_out_z, w_qkv_z, w_up_z, w_down_z):
         weight_sent(*moved)
-    for moved in (g_down_z, g_up_z, g_qkv_z, g_out_z):
+    for moved in (g_down_z, g_up_z, g_qkv_z):
         grad_sent(*moved)
-    for n in range(6):
+    direct_sent(*g_out_z)
+    for n in range(10):
         deliver(n).wait()
 
 
 def hand_over(*refs):
-    count = len(refs) // 2
-    sems = refs[-1]
-    copies = [pltpu.make_async_copy(refs[n], refs[count + n], sems.at[n]) for n in range(count)]
-    for copy in copies:
+    count = len(refs) // 3
+    given, taken, held, sems = refs[:count], refs[count:2 * count], refs[2 * count:3 * count], refs[-1]
+    into = [pltpu.make_async_copy(given[n], held[n], sems.at[0, n]) for n in range(count)]
+    out = [pltpu.make_async_copy(held[n], taken[n], sems.at[1, n]) for n in range(count)]
+    for copy in into:
         copy.start()
-    for copy in copies:
+    for n in range(count):
+        into[n].wait()
+        out[n].start()
+    for copy in out:
         copy.wait()
 
 
@@ -1126,11 +1325,12 @@
         V((ROWS, width), BF16), V((ROWS, width), BF16),
         V((32, 3 * width), F32), V((32, width), F32),
         V((32, 4 * width), F32), V((128, width), F32),
+        V((2, 32), F32), V((6, 32), F32), V((2, 32), F32), V((1, 128), F32),
         V((32, 3 * width), BF16), V((32, 4 * width), BF16),
         V((16, 128), F32), V((2, 16, 128), BF16),
-        V((4, PLANE, ROWS, width), BF16),
+        V((4, 4, 2, 2, HALF, width), BF16),
         V((PLANE, DEPTH, 32, 384), BF16),
-        V((DEPTH, 32, width), BF16),
+        V((PLANE, 128, width), BF16),
         V((PLANE, DEPTH, 32, 512), BF16),
         V((DEPTH, 128, width), BF16),
         V((PLANE, 32, 384), BF16),
@@ -1139,28 +1339,32 @@
         V((16, 128), BF16),
         V((PLANE, 16, 128), BF16),
         V((16, width), F32),
-        V((PLANE, ROWS, width), BF16),
-        V((2, CHIPS, BLOCK, 256), BF16),
+        V((4, BLOCK, width), BF16),
+        V((2, 4, BLOCK, 256), BF16),
         V((1024, 256), BF16),
         V((128, 1024), BF16),
         V((1024, 128), BF16),
         V((128, 1024), BF16),
-        V((2, CHIPS, 1024, BLOCK), BF16),
-        V((CHIPS, 128, BLOCK), F32),
-        V((CHIPS, 2, 8, BLOCK), F32),
-        V((CHIPS, BLOCK, 128), BF16),
+        V((2, 4, 1024, BLOCK), BF16),
+        V((4, 128, BLOCK), F32),
+        V((4, 2, 8, BLOCK), F32),
+        V((4, BLOCK, 128), BF16),
+        V((PLANE, ROWS, 128), BF16),
+        V((PLANE, ROWS, 128), BF16),
+        V((4, 2, 2, HALF, 128), BF16),
         V((1024, 384), BF16),
         V((1024, 128), F32),
         V((1024, 128), F32),
         V((1024, 512), BF16),
-        V((CHIPS, BLOCK, 512), F32),
+        V((4, BLOCK, 512), F32),
         V((1024, 512), BF16),
         V((ROWS, width), F32),
         V((ROWS, width), F32),
-        V((3, CHIPS, 2, ROWS, width), BF16),
-        V((4, CHIPS, ROWS, width), BF16),
-        V((3, CHIPS, ROWS, width), BF16),
-        V((4, CHIPS, ROWS, width), BF16),
+        V((3, 4, 2, 2, HALF, width), BF16),
+        V((3, 4, 2, HALF, width), BF16),
+        V((3, 4, 2, HALF, width), BF16),
+        V((3, 2, HALF, width), BF16),
+        V((3, 2, 2, HALF, width), BF16),
         V((DEPTH, 128, width), BF16),
         V((PLANE, DEPTH, 32, 512), BF16),
         V((PLANE, DEPTH, 32, 384), BF16),
@@ -1172,7 +1376,6 @@
         V((128, width), BF16),
         V((PLANE, 32, 512), BF16),
         V((PLANE, 32, 384), BF16),
-        V((32, width), BF16),
         V((PLANE, 32, 512), BF16),
         V((PLANE, 32, 384), BF16),
         V((PLANE, 32, 512), BF16),
@@ -1184,17 +1387,18 @@
         V((PLANE - 1, 16, 128), F32),
         V((16, 128), F32),
         V((3, 16, 128), F32),
-        dma((6,)), dma((6,)),
+        dma((8,)), dma((10,)),
         dma((4, 2, 2)), dma((4, 2, 2)), dma((4, 2)), dma((4, 2)), dma((4, 4)), dma((4, 4)),
         dma((4, 7)), dma((4, 7)), dma((2, 7)), dma((2, 7)),
-        dma((2, 3)), dma((2, 3)), dma((9, 4)), dma((9, 4)), dma((4,)),
-        dma((4, 4)), dma((4, 4)), dma((4, 4)), dma((4, 4)),
+        dma((2, 3)), dma((2, 3)), dma((9, 4)), dma((9, 4)), dma((3,)),
+        dma((3, 4)), dma((3, 4)), dma((3, 2)), dma((3, 2)), dma((3, 2, 2)), dma((3, 2, 2)),
+        dma((4, 4)), dma((4, 4)), dma((4, 2, 2)), dma((4, 2, 2)), dma((4, 2, 2)), dma((4, 2, 2)),
     ]
     results = pl.pallas_call(
         plane_kernel,
         out_shape=out_shape,
         in_specs=[pl.BlockSpec(memory_space=pltpu.SMEM)] + [vmem] * 5 + [anywhere] * 6,
-        out_specs=tuple([anywhere] * 6 + [vmem] * 4),
+        out_specs=tuple([anywhere] * 10),
         scratch_shapes=scratch,
         compiler_params=pltpu.CompilerParams(
             collective_id=0, has_side_effects=True, vmem_limit_bytes=63 * 2**20
@@ -1206,9 +1410,9 @@
     results = pl.pallas_call(
         hand_over,
         out_shape=out_shape,
-        in_specs=[vmem] * len(out_shape),
+        in_specs=[anywhere] * len(out_shape),
         out_specs=tuple([anywhere] * len(out_shape)),
-        scratch_shapes=[dma((len(out_shape),))],
+        scratch_shapes=[V(o.shape, o.dtype) for o in out_shape] + [dma((2, len(out_shape)))],
     )(*results)
     output, input_grad, g_qkv, g_out, g_up, g_down, g_gains, g_shifts, g_lead, g_bias = results
     return (

time: 133 us -> 124 us (0.932)
  Pallas kernels: 132 us -> 123 us
    pallas_call x1, Pallas kernels: 129 us -> 120 us  [plane_body(): pl.pallas_call(plane_kernel, out_shape=out_shape, in_specs=[pl.BlockSpec(...]
where the time goes in v3:
time: 124 us
  Pallas kernels  123 us (99%)
  between operations  1.3 us (1%)
    pallas_call x1, Pallas kernels, plane_body(): pl.pallas_call(plane_kernel, out_shape=out_shape, in_specs=[pl.BlockSpec(...  120 us
    pallas_call x1, Pallas kernels, plane_body(): pl.pallas_call(hand_over, out_shape=out_shape, in_specs=[anywhere] * len(...  2.52 us

profile of v3, /device:TPU:0, one launch (start us, length us, event | category | flops | bytes accessed | tf_op | source)
XLA Modules:
  0.0 124.3 jit_solution(5121226366432978850)
XLA Ops:
  1.3 120.5 %shard_map.195 = (bf16[128,1024]{1,0:T(8,128)(2,1)}, bf16[128,1024]{1,0:T(8,128)(2,1)}, f32[32,3072]{1,0:T(8,128)}, f32[32,1024]{1,0:T(8,128)}, f32[32,4096]{1,0...) custom-call(s32[1]{0:T(128)S(6)} %copy.22.lead_ref, ...), custom_call_target="tpu_custom_call" | custom-call | tf_op jit(solution)/shard_map/pallas_call | solution.py:1397
  121.8 2.5 %shard_map.196 = (bf16[128,1024]{1,0:T(8,128)(2,1)}, bf16[128,1024]{1,0:T(8,128)(2,1)}, f32[32,3072]{1,0:T(8,128)}, f32[32,1024]{1,0:T(8,128)}, f32[32,4096]{1,0...) custom-call(bf16[128,1024]{1,0:T(8,128)(2,1)} %get-tuple-element.30., ...), custom_call_target="tpu_custom_call" | custom-call | tf_op jit(solution)/shard_map/pallas_call | solution.py:1410

commit v4 on v3

--- a/solution.py
+++ b/solution.py
@@ -285,12 +285,12 @@
     wqkv, wup, vcol, vec_in,
     agf, wq, wo, wu, wd, sq, su, ztr, vt, vecf, vrow,
     normed, qaug, kaug, kt, vv, vt2, pst, ot, invl, att, aown, dsend, dob, gproj, dk, dv,
-    hid, gder, gpre, mid, gmid,
+    hid, gder, gpre, mid, gmid, gdf,
     part, pr, cs, au, rr,
-    gds, gus, gqs, gos, gdr, gur, gqr, gor_, gda, guc, gqc, gu2, gq2, gua, gqa, goa,
+    gds, gus, gqs, gos, gdr, gur, gqr, gor_, gda, guc, gqc, goc, gu2, gq2, gua, gqa, goa,
     acc, gub, vs, vsr, vz, vzr,
-    in_s, out_s, ag_s, ag_r, ac_s, ac_r, fw_s, fw_r, aq_s, aq_r, v_s, v_r, y_s, y_r, z_s, z_r, za_r,
-    p_s, p_r, f_s, f_r, n_s, n_r, wg_s, wg_r, h_s, h_r, g_s, g_r,
+    in_s, out_s, ag_s, ag_r, ac_r, fw_s, fw_r, aq_s, aq_r, v_s, v_r, y_s, y_r, w_s, w_r, z_s, z_r,
+    p_s, p_r, f_r, n_s, n_r, wg_s, wg_r, h_s, h_r, g_s, g_r,
 ):
     b = lax.axis_index("band")
     s = lax.axis_index("samp")
@@ -349,12 +349,12 @@
 
     @pl.when(s == 0)
     def _():
-        for kept in (gdr, gur, gqr):
+        for kept in (gdr, gur, gqr, gor_):
             kept[0] = jnp.zeros(kept.shape[1:], BF16)
 
     @pl.when(s == DEPTH - 1)
     def _():
-        for kept in (gda, guc, gqc):
+        for kept in (gda, guc, gqc, goc):
             kept[...] = jnp.zeros(kept.shape, BF16)
 
     fetches[0].wait()
@@ -370,91 +370,96 @@
             device_id=(band, samp), device_id_type=MESH,
         )
 
+    def landed(ref, sem):
+        rc(ref, ref, aq_s.at[0], sem, mate, s).wait_recv()
+
+    def left(ref, sem):
+        rc(ref, ref, sem, aq_r.at[0], mate, s).wait_send()
+
     def yc(kind, k, src, dst):
-        return rc(src, dst, y_s.at[kind, k - 1], y_r.at[kind, k - 1], b, level(k))
-
-    def weight_copy(kind, region, role, to):
-        return rc(region(s), region(s), z_s.at[kind, role], z_r.at[kind, s], b, to)
-
-    def weight_hand(kind, region):
-        return rc(region(far), region(far), z_s.at[kind, 3], z_r.at[kind, far], b, 3 * (s - 1))
-
-    def weight_from(kind, region, t):
-        rc(region(t), region(t), z_s.at[kind, 3], z_r.at[kind, t], b, t).wait_recv()
-
-    def weight_start(kind, region):
+        return rc(src, dst, y_s.at[kind], y_r.at[kind], b, level(k))
+
+    def weight_copy(kind, region, pieces, role, to):
+        return rc(region(s), region(s), w_s.at[kind], w_r.at[kind, role], b, to)
+
+    def weight_hand(kind, region, pieces):
+        return rc(region(far), region(far), w_s.at[kind], w_r.at[kind, 1], b, 3 * (s - 1))
+
+    def weight_start(*moved):
         @pl.when(s == 1)
         def _():
-            weight_copy(kind, region, 2, s - 1).start()
-
-        weight_copy(kind, region, 0, far).start()
+            weight_copy(*moved, 1, s - 1).start()
+
+        weight_copy(*moved, 0, far).start()
 
         @pl.when(s < DEPTH - 1)
         def _():
-            weight_copy(kind, region, 1, s + 1).start()
+            weight_copy(*moved, 1, s + 1).start()
 
         @pl.when(s > 1)
         def _():
-            weight_copy(kind, region, 2, s - 1).start()
-
-    def weight_pass(kind, region):
+            weight_copy(*moved, 1, s - 1).start()
+
+    def weight_pass(kind, region, pieces):
         @pl.when(inner)
         def _():
-            weight_from(kind, region, far)
-            weight_hand(kind, region).start()
-
-    def weight_finish(kind, region):
-        @pl.when(s < DEPTH - 1)
-        def _():
-            weight_from(kind, region, s + 1)
-
-        @pl.when(s > 0)
-        def _():
-            weight_from(kind, region, s - 1)
+            landed(region(far), w_r.at[kind, 0])
+            weight_hand(kind, region, pieces).start()
+
+    def weight_finish(kind, region, pieces):
+        landed(pieces(2), w_r.at[kind, 1])
 
         @pl.when(ends)
         def _():
-            weight_from(kind, region, far)
-            weight_from(kind, region, DEPTH - 1 - s)
-
-    def weight_sent(kind, region):
-        weight_copy(kind, region, 0, far).wait_send()
-
-        @pl.when(s < DEPTH - 1)
-        def _():
-            weight_copy(kind, region, 1, s + 1).wait_send()
-
-        @pl.when(s > 0)
-        def _():
-            weight_copy(kind, region, 2, s - 1).wait_send()
+            landed(region(far), w_r.at[kind, 0])
+
+    def weight_sent(kind, region, pieces):
+        @pl.when(ends)
+        def _():
+            left(pieces(2), w_s.at[kind])
 
         @pl.when(inner)
         def _():
-            weight_hand(kind, region).wait_send()
-
-    def grad_up(kind, stage, got, via, t):
-        return rc(stage(t), got(t), z_s.at[kind, t], z_r.at[kind, t], b, s + 1)
-
-    def grad_down_to(kind, stage, got, via, t):
-        return rc(stage(t), got(t), z_s.at[kind, t], z_r.at[kind, t], b, s - 1)
-
-    def grad_down_last(kind, stage, got, via):
-        return rc(stage(s - 1), via, z_s.at[kind, s - 1], za_r.at[kind - 5], b, s - 1)
-
-    def grad_start(kind, stage, got, via):
+            left(pieces(4), w_s.at[kind])
+
+    def grad_up(kind, stage, got, via, pieces, t):
+        return rc(stage(t), got(t), z_s.at[kind], z_r.at[kind, t], b, s + 1)
+
+    def grad_down_to(kind, stage, got, via, pieces, t):
+        return rc(stage(t), got(t), z_s.at[kind], z_r.at[kind, t], b, s - 1)
+
+    def grad_down_last(kind, stage, got, via, pieces):
+        return rc(stage(s - 1), via, z_s.at[kind], z_r.at[kind, DEPTH], b, s - 1)
+
+    def grad_start(*moved):
+        for hops in (3, 2, 1):
+            grad_start_some(*moved, hops)
+
+    def grad_start_some(kind, stage, got, via, pieces, hops):
         @pl.when(s == 0)
         def _():
-            for t in (3, 2, 1):
-                grad_up(kind, stage, got, via, t).start()
+            grad_up(kind, stage, got, via, pieces, hops).start()
 
         @pl.when(s == DEPTH - 1)
         def _():
-            for t in (0, 1):
-                grad_down_to(kind, stage, got, via, t).start()
-            grad_down_last(kind, stage, got, via).start()
-
-    def add_in(kind, stage, got, via, t):
-        rc(got(t), got(t), z_s.at[kind, t], z_r.at[kind, t], b, s).wait_recv()
+            if hops == 1:
+                grad_down_last(kind, stage, got, via, pieces).start()
+            else:
+                grad_down_to(kind, stage, got, via, pieces, DEPTH - 1 - hops).start()
+
+    def down_half(half):
+        rows = pl.ds(half * HALF, HALF)
+
+        @pl.when(s == 0)
+        def _():
+            rc(gds.at[1, rows], gdr.at[1, rows], z_s.at[0], z_r.at[0, 1], b, 1).start()
+
+        @pl.when(s == DEPTH - 1)
+        def _():
+            rc(gds.at[2, rows], gda.at[rows], z_s.at[0], z_r.at[0, DEPTH], b, DEPTH - 2).start()
+
+    def add_in(kind, stage, got, via, pieces, t):
+        landed(got(t), z_r.at[kind, t])
         term, more = stage(t), got(t)
         if len(via.shape) == 3:
             def add(j, _):
@@ -496,42 +501,17 @@
             add_in(*moved, 3)
             grad_up(*moved, 3).start()
 
-    def grad_finish(kind, stage, got, via):
+    def grad_finish(kind, stage, got, via, pieces):
         @pl.when(s > 0)
         def _():
-            rc(got(s), got(s), z_s.at[kind, 0], z_r.at[kind, s], b, s).wait_recv()
+            landed(got(s), z_r.at[kind, s])
 
         @pl.when(s < DEPTH - 1)
         def _():
-            rc(via, via, z_s.at[kind, 0], za_r.at[kind - 5], b, s).wait_recv()
-
-    def grad_sent(kind, stage, got, via):
-        for k in range(1, DEPTH):
-            t = level(k)
-            rc(stage(t), got(t), z_s.at[kind, t], z_r.at[kind, t], b, s).wait_send()
-
-    def direct_copy(kind, stage, got, t):
-        return rc(stage(t), got(s), z_s.at[kind, t], z_r.at[kind, s], b, t)
-
-    def direct_start(kind, stage, got):
-        for t in (3, 2, 1, 0):
-            @pl.when((s != t) & (s < 2))
-            def _():
-                direct_copy(kind, stage, got, t).start()
-
-        for t in (0, 1, 2, 3):
-            @pl.when((s != t) & (s >= 2))
-            def _():
-                direct_copy(kind, stage, got, t).start()
-
-    def direct_finish(kind, stage, got):
-        for k in range(1, DEPTH):
-            t = level(k)
-            rc(got(t), got(t), z_s.at[kind, t], z_r.at[kind, t], b, t).wait_recv()
-
-    def direct_sent(kind, stage, got):
-        for k in range(1, DEPTH):
-            direct_copy(kind, stage, got, level(k)).wait_send()
+            landed(via, z_r.at[kind, DEPTH])
+
+    def grad_sent(kind, stage, got, via, pieces):
+        left(pieces(3), z_s.at[kind])
 
     results = ((out_o, out_h), (ig_o, ig_h), (gqkv_o, gqkv_h), (gout_o, gout_h), (gup_o, gup_h), (gdown_o, gdown_h),
                (gain_o, gain_h), (shift_o, shift_h), (lead_o, lead_h), (bias_o, bias_h))
@@ -539,31 +519,34 @@
     def deliver(n):
         return pltpu.make_async_copy(results[n][0], results[n][1], out_s.at[n])
 
-    w_out_z = (1, lambda t: wo.at[b, pl.ds(pl.multiple_of(t * 32, 32), 32)])
-    w_qkv_z = (2, lambda t: wq.at[:, t])
-    w_up_z = (3, lambda t: wu.at[:, t])
-    w_down_z = (4, lambda t: wd.at[t])
-    g_down_z = (5, lambda t: gds.at[t], lambda t: gdr.at[t], gda)
-    g_up_z = (6, lambda t: gus.at[:, t], lambda t: gur.at[t], guc)
-    g_qkv_z = (7, lambda t: gqs.at[:, t], lambda t: gqr.at[t], gqc)
-    g_out_z = (8, lambda t: gos.at[t], lambda t: gor_.at[t])
+    w_out_z = (
+        0, lambda t: wo.at[b, pl.ds(pl.multiple_of(t * 32, 32), 32)],
+        lambda n: wo.at[b, pl.ds(0, n * 32)],
+    )
+    w_qkv_z = (1, lambda t: wq.at[:, t], lambda n: wq.at[:, pl.ds(0, n)])
+    w_up_z = (2, lambda t: wu.at[:, t], lambda n: wu.at[:, pl.ds(0, n)])
+    w_down_z = (3, lambda t: wd.at[t], lambda n: wd.at[pl.ds(0, n)])
+    g_down_z = (0, lambda t: gds.at[t], lambda t: gdr.at[t], gda, lambda n: gds.at[pl.ds(0, n)])
+    g_up_z = (1, lambda t: gus.at[:, t], lambda t: gur.at[t], guc, lambda n: gus.at[:, pl.ds(0, n)])
+    g_qkv_z = (2, lambda t: gqs.at[:, t], lambda t: gqr.at[t], gqc, lambda n: gqs.at[:, pl.ds(0, n)])
+    g_out_z = (3, lambda t: gos.at[t], lambda t: gor_.at[t], goc, lambda n: gos.at[pl.ds(0, n)])
 
     def gather(op, r, turn):
         return rc(
             agf.at[op, 0, (turn + r) % 2, c], agf.at[op, 1 + turn, r - 1, c],
-            ag_s.at[op, r - 1, turn], ag_r.at[op, r - 1, turn], near(r), s,
+            ag_s.at[op], ag_r.at[op, turn], near(r), s,
         )
 
     def across(op, r):
         return rc(
             agf.at[op, 1, r - 1, c], agf.at[op, 3, r % 2, c],
-            ac_s.at[op, r - 1], ac_r.at[op, r - 1], near(3 - r), s,
+            ag_s.at[op], ac_r.at[op], near(3 - r), s,
         )
 
     def share(op, blk):
         return rc(
             agf.at[op, blk, :, c], agf.at[op, blk, :, c],
-            fw_s.at[op, blk], fw_r.at[op, blk], mate, s,
+            fw_s.at[op], fw_r.at[op, blk], mate, s,
         )
 
     def start_gather(op):
@@ -574,13 +557,12 @@
 
     def arrive(op, blk):
         if blk in (1, 2):
+            landed(agf.at[op, blk, :, c], ag_r.at[op, blk - 1])
+        if blk == 1:
             for r in (1, 2):
-                gather(op, r, blk - 1).wait_recv()
-                if blk == 1:
-                    across(op, r).start()
+                across(op, r).start()
         if blk == 3:
-            across(op, 1).wait_recv()
-            across(op, 2).wait_recv()
+            landed(agf.at[op, 3, :, c], ac_r.at[op])
         if blk:
             share(op, blk).start()
 
@@ -592,15 +574,15 @@
 
     def rows_copy(r, turn):
         part_ = rows_half(b, (turn + r) % 2)
-        return rc(part_, part_, wg_s.at[r - 1, turn], wg_r.at[r - 1, turn], near(r), s)
+        return rc(part_, part_, wg_s.at[0], wg_r.at[turn], near(r), s)
 
     def rows_across(r):
         part_ = rows_half(near(r), r % 2)
-        return rc(part_, part_, wg_s.at[2, r - 1], wg_r.at[2, r - 1], near(3 - r), s)
+        return rc(part_, part_, wg_s.at[0], wg_r.at[2], near(3 - r), s)
 
     def rows_share(r):
         dev = near(r) if r else b
-        return rc(wo.at[dev], wo.at[dev], wg_s.at[3, r], wg_r.at[3, r], mate, s)
+        return rc(wo.at[dev], wo.at[dev], wg_s.at[1], wg_r.at[3], mate, s)
 
     def rows_start():
         for turn in (0, 1):
@@ -611,19 +593,15 @@
     def granule(i, a):
         return (i, a) if i in (0, 3) else (a + 1, 1 - a if i == 1 else a)
 
-    GRANULES = [(i, a) for i in (3, 2, 1, 0) for a in (0, 1)]
+    GRANULES = [(i, a) for i in (1, 0, 2, 3) for a in (0, 1)]
 
     def heads_copy(i, a, k):
         r, h = granule(i, a)
         rows = pl.ds(pl.multiple_of((a * 2 + k) * HALF, HALF), HALF)
         return rc(
             att.at[i, rows], aown.at[b, pl.ds(h * HALF, HALF)],
-            h_s.at[i, a, k], h_r.at[r, h, c], chip(r) * 2 + k, s,
-        )
-
-    def heads_from(r, h, k):
-        dst = aown.at[chip(r) * 2 + k, pl.ds(h * HALF, HALF)]
-        return rc(dst, dst, h_s.at[0, 0, 0], h_r.at[r, h, k], mate, s)
+            h_s.at[0], h_r.at[0], chip(r) * 2 + k, s,
+        )
 
     def cores(i):
         return (1 - c,) if i == 0 else (0, 1)
@@ -633,14 +611,11 @@
         dev = chip(r) * 2 + k
         return rc(
             dsend.at[dev, pl.ds(h * HALF, HALF)], dob.at[i, a, c],
-            g_s.at[i, a, k], g_r.at[i, a, c], dev, s,
-        )
-
-    def back_from(i, a, k):
-        return rc(dob.at[i, a, k], dob.at[i, a, k], g_s.at[0, 0, 0], g_r.at[i, a, k], mate, s)
+            g_s.at[0], g_r.at[i], dev, s,
+        )
 
     def swap(kind, k, src, dst):
-        return rc(src, dst, aq_s.at[kind, k - 1], aq_r.at[kind, k - 1], peer(k), s)
+        return rc(src, dst, aq_s.at[kind], aq_r.at[kind], peer(k), s)
 
     for k in range(1, DEPTH):
         yc(0, k, vec_in.at[0], ztr.at[k - 1]).start()
@@ -657,15 +632,14 @@
         su[d] = wup[:, d * 512:(d + 1) * 512]
     wu[b, s] = su[b]
 
-    for k in range(1, DEPTH):
-        yc(0, k, vec_in.at[0], ztr.at[k - 1]).wait_recv()
+    landed(ztr, y_r.at[0])
     vt[...] = (
         vec_in[0].astype(F32) + vec_in[1].astype(F32)
         + ztr[0].astype(F32) + ztr[1].astype(F32) + ztr[2].astype(F32)
     ).astype(BF16)
 
     def spread(k):
-        return rc(vt, vecf.at[b], v_s.at[0, k - 1], v_r.at[0, k - 1], peer(k), s)
+        return rc(vt, vecf.at[b], v_s.at[0], v_r.at[0], peer(k), s)
 
     for k in range(1, PLANE):
         spread(k).start()
@@ -673,8 +647,7 @@
         gather(0, r, 1).start()
     share(0, 0).start()
     vecf[b] = vt[...]
-    for k in range(1, PLANE):
-        swap(0, k, sq.at[peer(k)], wq.at[b, s]).wait_recv()
+    landed(sq.at[pl.ds(0, 7)], aq_r.at[0])
     weight_start(*w_qkv_z)
     for k in range(1, PLANE):
         swap(1, k, su.at[peer(k)], wu.at[b, s]).start()
@@ -684,8 +657,7 @@
     for r in (1, 2):
         gather(1, r, 0).start()
     share(1, 0).start()
-    for k in range(1, PLANE):
-        spread(k).wait_recv()
+    landed(vecf.at[pl.ds(0, 7)], v_r.at[0])
     for d in range(PLANE):
         vrow[:, d * 128:(d + 1) * 128] = vecf[d].astype(F32)
     lead_days = lead_ref[0].astype(F32) * 0.25
@@ -718,7 +690,7 @@
                 kaug[top:top + HALF, 128:256] = column[h * HALF:(h + 1) * HALF]
     for h in range(2):
         for i in range(4):
-            qaug[h, i, :, 128:256] = jnp.broadcast_to(ones_lane, (BLOCK, 128)).astype(BF16)
+            qaug[i, h * BLOCK:(h + 1) * BLOCK, 128:256] = jnp.broadcast_to(ones_lane, (BLOCK, 128)).astype(BF16)
 
     def norm_block(i):
         def chunk(j, _):
@@ -746,8 +718,7 @@
     share(0, 3).wait_recv()
     norm_block(3)
 
-    for k in range(1, PLANE):
-        swap(1, k, su.at[peer(k)], wu.at[b, s]).wait_recv()
+    landed(su.at[pl.ds(0, 7)], aq_r.at[1])
     weight_finish(*w_qkv_z)
     weight_start(*w_up_z)
 
@@ -756,7 +727,7 @@
         pj = mm(normed[q], wq[...].reshape(width, 384))
         qv = (pj[:, 0:128] + mine[3:4, :]).astype(BF16).astype(F32) * 0.125
         for h in range(2):
-            qaug[h, q, :, 0:128] = (qv * head_lane[h]).astype(BF16)
+            qaug[q, h * BLOCK:(h + 1) * BLOCK, 0:128] = (qv * head_lane[h]).astype(BF16)
         kv = pj[:, 128:256].astype(BF16)
         kaug[rows, 0:128] = kv
         kt[:, rows] = kv.T
@@ -768,14 +739,14 @@
     lax.fori_loop(0, 4, project_block, 0)
 
     def mate_copy(op, i):
-        return rc(part.at[op, i, :, 1 - c], pr.at[op, i], p_s.at[op, i], p_r.at[op, i], mate, s)
+        return rc(part.at[op, i, :, 1 - c], pr.at[op, i], p_s.at[op], p_r.at[op, i], mate, s)
 
     def far_copy(op, h):
-        return rc(cs.at[op, 3, h], au.at[op, 1 - h], f_s.at[op, h], f_r.at[op, 1 - h], near(h + 1), s)
+        return rc(cs.at[op, 3, h], au.at[op, 1 - h], n_s.at[op], f_r.at[op], near(h + 1), s)
 
     def near_copy(op, i, a):
         h = a if i == 2 else 1 - a
-        return rc(cs.at[op, i, a], rr.at[op, a, h], n_s.at[op, a, h], n_r.at[op, a, h], near(a + 1), s)
+        return rc(cs.at[op, i, a], rr.at[op, a, h], n_s.at[op], n_r.at[op], near(a + 1), s)
 
     def put_part(op, i, blk):
         part[op, i] = blk.astype(BF16).reshape(2, 2, HALF, width)
@@ -817,9 +788,8 @@
             near_copy(op, i, a).start()
 
     def send_last(op):
+        landed(au.at[op], f_r.at[op])
         for a in (0, 1):
-            far_copy(op, 1 - a).wait_recv()
-
             def chunk(j, _):
                 rows = pl.ds(pl.multiple_of(j * INNER, INNER), INNER)
                 cs[op, 1, a, rows, :] = (
@@ -831,9 +801,7 @@
             near_copy(op, 1, a).start()
 
     def wait_sums(op):
-        for i in (2, 1):
-            for a in (0, 1):
-                near_copy(op, i, a).wait_recv()
+        landed(rr.at[op], n_r.at[op])
 
     def place(j):
         return j // 2, pl.ds(pl.multiple_of((j % 2) * INNER, INNER), INNER)
@@ -852,31 +820,27 @@
         agf[op, 0, h, c, rows, :] = v
 
     def end_sums(op):
-        for i in range(4):
-            mate_copy(op, i).wait_send()
-        for h in (0, 1):
-            far_copy(op, h).wait_send()
-        for i in (2, 1):
-            for a in (0, 1):
-                near_copy(op, i, a).wait_send()
+        left(part.at[op, :, :, 0], p_s.at[op])
+        left(cs.at[op, pl.ds(0, 3)], n_s.at[op])
 
     def attend_block(n, _):
         i = 3 - n
 
         @pl.when(n == 3)
         def _():
+            landed(wo.at[0], wg_r.at[1])
             for r in (1, 2):
-                rows_copy(r, 1).wait_recv()
                 rows_share(r).start()
 
-        for h in range(2):
-            st = mm(kaug[...], qaug[h, i], NT)
-            p = jnp.exp(st - jnp.max(st, axis=0, keepdims=True))
-            inverse = 1.0 / jnp.sum(p, axis=0, keepdims=True)
-            pb = p.astype(BF16)
-            pst[h, i] = pb
-            ot[i, h * 64:(h + 1) * 64, :] = mm(vt2[h * 64:(h + 1) * 64, :], pb) * inverse
-            invl[i, h] = jnp.broadcast_to(inverse, (8, BLOCK))
+        st = mm(kaug[...], qaug[i], NT)
+        p = jnp.exp(st - jnp.max(st, axis=0, keepdims=True))
+        inverse = 1.0 / jnp.sum(p, axis=0, keepdims=True)
+        pb = p.astype(BF16)
+        pst[i] = pb
+        out = mm(vt2[...], pb) * inverse
+        ot[i, 0:64, :] = out[0:64, 0:BLOCK]
+        ot[i, 64:128, :] = out[64:128, BLOCK:]
+        invl[i] = jnp.broadcast_to(inverse, (8, 2 * BLOCK))
         att[i] = ot[i].T.astype(BF16)
         for blk in range(4):
             @pl.when(i == blk)
@@ -887,11 +851,13 @@
 
         return 0
 
-    arrive(1, 1)
+    landed(wo.at[0], wg_r.at[0])
     for r in (1, 2):
-        rows_copy(r, 0).wait_recv()
         rows_across(r).start()
     lax.fori_loop(0, 4, attend_block, 0)
+    landed(wo.at[0], wg_r.at[2])
+    rows_share(3).start()
+    arrive(1, 1)
     for r in (1, 2):
         gather(1, r, 1).start()
     for h in (0, 1):
@@ -904,16 +870,8 @@
     def _():
         weight_start(*w_down_z)
 
-    arrive(1, 3)
-    for r in (1, 2):
-        rows_across(r).wait_recv()
-    rows_share(3).start()
-    for r in range(4):
-        rows_share(r).wait_recv()
-    for r in (3, 2, 1, 0):
-        for h in (0, 1):
-            for k in cores(r):
-                heads_from(r, h, k).wait_recv()
+    landed(wo.at[pl.ds(0, 4)], wg_r.at[3])
+    landed(aown.at[pl.ds(0, 7)], h_r.at[0])
     heads = jnp.concatenate([aown[d] for d in range(PLANE)], axis=1)
     mid[...] = mm(heads, wo[...].reshape(1024, width))
 
@@ -926,6 +884,8 @@
 
     lax.fori_loop(0, ROWS // INNER, middle_chunk, 0)
     start_gather(2)
+    arrive(1, 2)
+    arrive(1, 3)
 
     weight_finish(*w_up_z)
 
@@ -942,7 +902,20 @@
                 arrive(op, blk)
                 share(op, blk).wait_recv()
 
+    def down_grad_first(f, _):
+        cols = pl.ds(pl.multiple_of(f * BLOCK, BLOCK), BLOCK)
+        gdf[pl.ds(pl.multiple_of(f * BLOCK, BLOCK), BLOCK), :] = mm(
+            hid[:3 * BLOCK, cols], agf[1, 0:3].reshape(3 * BLOCK, width), TN
+        )
+        return 0
+
     def up_block(i, _):
+        @pl.when(i == 3)
+        def _():
+            for blk in range(3):
+                share(1, blk).wait_recv()
+            lax.fori_loop(0, 2, down_grad_first, 0)
+
         arrivals(2, i)
 
 
@@ -954,18 +927,24 @@
 
     lax.fori_loop(0, 4, up_block, 0)
     weight_pass(*w_down_z)
-    arrive(1, 2)
-    for i in range(4):
-        share(1, i).wait_recv()
+    share(1, 3).wait_recv()
 
     def down_grad(f, _):
         cols = pl.ds(pl.multiple_of(f * BLOCK, BLOCK), BLOCK)
-        g = mm(hid[:, cols], agf[1].reshape(1024, width), TN)
+        g = gdf[pl.ds(pl.multiple_of(f * BLOCK, BLOCK), BLOCK), :] + mm(hid[3 * BLOCK:, cols], block(1, 3), TN)
         gds[pl.ds(2 * f, 2)] = g.astype(BF16).reshape(2, 128, width)
         return 0
 
     lax.fori_loop(0, 2, down_grad, 0)
-    grad_start(*g_down_z)
+    grad_start_some(*g_down_z, 3)
+    grad_start_some(*g_down_z, 2)
+    down_half(0)
+    for i in range(4):
+        for j in range(i + 1):
+            upper = normed[j, :, i * BLOCK:(i + 1) * BLOCK].T
+            if i != j:
+                normed[j, :, i * BLOCK:(i + 1) * BLOCK] = normed[i, :, j * BLOCK:(j + 1) * BLOCK].T
+            normed[i, :, j * BLOCK:(j + 1) * BLOCK] = upper
     weight_finish(*w_down_z)
     gub[...] = jnp.zeros_like(gub)
 
@@ -1045,6 +1024,7 @@
         dob[0, h, c] = dsend[b, h * HALF:(h + 1) * HALF, :]
     start_gather(3)
 
+    grad_pass(*g_up_z)
     dk[...] = jnp.zeros_like(dk)
     dv[...] = jnp.zeros_like(dv)
     goa[...] = jnp.zeros_like(goa)
@@ -1053,23 +1033,11 @@
         for blk in range(4):
             @pl.when(i == blk)
             def _():
-                for a in (0, 1):
-                    for k in cores(blk):
-                        back_from(blk, a, k).wait_recv()
-
-        @pl.when(i == 2)
-        def _():
-            send_near(1, 2)
-            send_last(1)
-
-        @pl.when(i == 3)
-        def _():
-            arrive(3, 1)
-            grad_pass(*g_up_z)
+                landed(dob.at[blk] if blk else dob.at[0, :, 0], g_r.at[blk])
 
         dot_t = dob[i].reshape(BLOCK, 128).astype(F32).T
         inv = jnp.concatenate(
-            [jnp.broadcast_to(invl[i, h, 0:1, :], (64, BLOCK)) for h in range(2)], axis=0
+            [jnp.broadcast_to(invl[i, 0:1, h * BLOCK:(h + 1) * BLOCK], (64, BLOCK)) for h in range(2)], axis=0
         )
         dos = dot_t * inv
         prod = dos * ot[i]
@@ -1080,27 +1048,25 @@
         for h in range(2):
             halves = [dos[0:64], zero] if h == 0 else [zero, dos[64:128]]
             dp = mm(vv[...], jnp.concatenate(halves, axis=0).astype(BF16))
-            pb = pst[h, i]
+            pb = pst[i, :, h * BLOCK:(h + 1) * BLOCK]
             ds = (pb.astype(F32) * (dp - deltas[h])).astype(BF16)
             dv[...] += mm(pb, (do_rows * head_lane[h]).astype(BF16))
-            dk[...] += mm(ds, qaug[h, i, :, 0:128])
+            dk[...] += mm(ds, qaug[i, h * BLOCK:(h + 1) * BLOCK, 0:128])
             dq_parts.append(mm(kt[h * 64:(h + 1) * 64, :], ds))
         dq = jnp.concatenate(dq_parts, axis=0).T * 0.125
         gproj[pl.ds(pl.multiple_of(i * BLOCK, BLOCK), BLOCK), 0:128] = dq.astype(BF16)
         return 0
 
     lax.fori_loop(0, 4, attend_back, 0)
+    send_near(1, 2)
     gproj[:, 128:256] = dk[...].astype(BF16)
     gproj[:, 256:384] = dv[...].astype(BF16)
 
-    def qkv_grad(f, _):
-        cols = pl.ds(pl.multiple_of(f * BLOCK, BLOCK), BLOCK)
-        g = mm(normed[:, :, cols].reshape(1024, BLOCK), gproj[...], TN)
-        gqs[pl.ds(2 * f, 2)] = g.astype(BF16).reshape(2, 4, 32, 384)
-        return 0
-
-    lax.fori_loop(0, 4, qkv_grad, 0)
-    grad_start(*g_qkv_z)
+    gqs[...] = mm(normed[...].reshape(1024, 1024), gproj[...]).astype(BF16).reshape(8, 4, 32, 384)
+    grad_start_some(*g_qkv_z, 3)
+    grad_start_some(*g_qkv_z, 2)
+    grad_pass_on(*g_up_z)
+    arrive(3, 1)
 
     def project_back(n, _):
         i = 3 - n
@@ -1109,14 +1075,12 @@
         fold_before(2, i)
         return 0
 
-    arrive(3, 2)
     lax.fori_loop(0, 4, project_back, 0)
     fold(2, 0)
-
-    grad_pass_on(*g_up_z)
+    arrive(3, 2)
     share(3, 0).wait_recv()
     arrive(3, 3)
-
+    grad_pass(*g_qkv_z)
     def out_grad(i, _):
         for blk in (1, 2, 3):
             @pl.when(i == blk)
@@ -1128,22 +1092,19 @@
 
     lax.fori_loop(0, 4, out_grad, 0)
     gos[...] = goa[...].astype(BF16).reshape(4, 32, width)
-
-    @pl.when(ends)
-    def _():
-        direct_start(*g_out_z)
-
+    grad_start_some(*g_out_z, 3)
+    grad_start_some(*g_qkv_z, 1)
+    grad_start_some(*g_out_z, 2)
+    grad_start_some(*g_out_z, 1)
+    down_half(1)
     send_last(2)
-    def others(kind, stage, got, via):
+    send_last(1)
+
+    def others(kind, stage, got, via, pieces):
         return [got(s), via]
 
-    def from_planes(got):
-        return [got(level(k)) for k in range(1, DEPTH)]
-
-    grad_finish(*g_down_z)
-    gdown_o[...] = sum([t[...].astype(F32) for t in others(*g_down_z)], gds[s].astype(F32))
-    deliver(5).start()
-    grad_pass(*g_qkv_z)
+    grad_pass(*g_out_z)
+    grad_pass_on(*g_qkv_z)
     wait_sums(2)
 
     def first_chunk(j, _):
@@ -1167,7 +1128,7 @@
         vs[d] = packed[:, d * 128:(d + 1) * 128]
 
     def vec_swap(k):
-        return rc(vs.at[peer(k)], vsr.at[k - 1], v_s.at[1, k - 1], v_r.at[1, k - 1], peer(k), s)
+        return rc(vs.at[peer(k)], vsr.at[k - 1], v_s.at[1], v_r.at[1], peer(k), s)
 
     for k in range(1, PLANE):
         vec_swap(k).start()
@@ -1180,16 +1141,6 @@
         + [jnp.zeros((1, 128), F32)],
         axis=0,
     )
-    wait_sums(1)
-
-    def output_chunk(j, _):
-        rows = pl.ds(pl.multiple_of(j * INNER, INNER), INNER)
-        out_o[rows, :] = (mid[rows, :] + plane_total(1, j) + shift_down).astype(BF16)
-        return 0
-
-    lax.fori_loop(0, ROWS // INNER, output_chunk, 0)
-    deliver(0).start()
-
     grad_finish(*g_up_z)
     for d in range(PLANE):
         gu2[d] = sum(
@@ -1198,14 +1149,18 @@
     for k in range(1, PLANE):
         swap(2, k, gu2.at[peer(k)], gua.at[b]).start()
     gua[b] = gu2[b]
-    grad_pass_on(*g_qkv_z)
-
-    @pl.when(inner)
-    def _():
-        direct_start(*g_out_z)
-
-    for k in range(1, PLANE):
-        vec_swap(k).wait_recv()
+    grad_pass_on(*g_out_z)
+    wait_sums(1)
+
+    def output_chunk(j, _):
+        rows = pl.ds(pl.multiple_of(j * INNER, INNER), INNER)
+        out_o[rows, :] = (mid[rows, :] + plane_total(1, j) + shift_down).astype(BF16)
+        return 0
+
+    lax.fori_loop(0, ROWS // INNER, output_chunk, 0)
+    deliver(0).start()
+
+    landed(vs.at[pl.ds(0, 7)], v_r.at[1])
     total = vs[b] + extra
     for k in range(PLANE - 1):
         total = total + vsr[k]
@@ -1221,16 +1176,17 @@
     for k in range(1, PLANE):
         swap(3, k, gq2.at[peer(k)], gqa.at[b]).start()
     gqa[b] = gq2[b]
-    direct_finish(*g_out_z)
-    gout_o[...] = sum([t[...].astype(F32) for t in from_planes(g_out_z[2])], gos[s].astype(F32))
+    grad_finish(*g_out_z)
+    gout_o[...] = sum([t[...].astype(F32) for t in others(*g_out_z)], gos[s].astype(F32))
     deliver(3).start()
-    for k in range(1, PLANE):
-        swap(2, k, gu2.at[peer(k)], gua.at[b]).wait_recv()
+    grad_finish(*g_down_z)
+    gdown_o[...] = sum([t[...].astype(F32) for t in others(*g_down_z)], gds[s].astype(F32))
+    deliver(5).start()
+    landed(gu2.at[pl.ds(0, 7)], aq_r.at[2])
     for d in range(PLANE):
         gup_o[:, d * 512:(d + 1) * 512] = gua[d].astype(F32)
     deliver(4).start()
-    for k in range(1, DEPTH):
-        yc(1, k, vz, vzr.at[k - 1]).wait_recv()
+    landed(vzr, y_r.at[1])
     vz_sum = vz[...] + vzr[0] + vzr[1] + vzr[2]
     columns = pltpu.roll(vz_sum, (128 - 32 * s) % 128, 1)
     gain_o[...] = columns[0:2, 0:32]
@@ -1239,8 +1195,7 @@
     bias_o[...] = jnp.sum(jnp.where(line == 11 + s, vz_sum, 0.0), axis=0, keepdims=True)
     for n in range(6, 10):
         deliver(n).start()
-    for k in range(1, PLANE):
-        swap(3, k, gq2.at[peer(k)], gqa.at[b]).wait_recv()
+    landed(gq2.at[pl.ds(0, 7)], aq_r.at[3])
     for d in range(PLANE):
         for j in range(3):
             gqkv_o[:, j * width + d * 128:j * width + (d + 1) * 128] = (
@@ -1249,39 +1204,24 @@
 
     deliver(2).start()
     for op in range(4):
-        for r in (1, 2):
-            gather(op, r, 0).wait_send()
-            gather(op, r, 1).wait_send()
-            across(op, r).wait_send()
-        for i in range(4):
-            share(op, i).wait_send()
+        left(agf.at[op, pl.ds(0, 3), :, 0], ag_s.at[op])
+        left(agf.at[op, :, :, 0], fw_s.at[op])
     for op in range(3):
         end_sums(op)
-    for r in (1, 2):
-        rows_copy(r, 0).wait_send()
-        rows_copy(r, 1).wait_send()
-        rows_across(r).wait_send()
-    for r in range(4):
-        rows_share(r).wait_send()
-    for i, a in GRANULES:
-        for k in cores(i):
-            heads_copy(i, a, k).wait_send()
-            back_copy(i, a, k).wait_send()
-    for k in range(1, PLANE):
-        swap(0, k, sq.at[peer(k)], wq.at[b, s]).wait_send()
-        swap(1, k, su.at[peer(k)], wu.at[b, s]).wait_send()
-        swap(2, k, gu2.at[peer(k)], gua.at[b]).wait_send()
-        swap(3, k, gq2.at[peer(k)], gqa.at[b]).wait_send()
-        spread(k).wait_send()
-        vec_swap(k).wait_send()
-    for k in range(1, DEPTH):
-        yc(0, k, vec_in.at[0], ztr.at[k - 1]).wait_send()
-        yc(1, k, vz, vzr.at[k - 1]).wait_send()
+    left(wo.at[pl.ds(0, 3)], wg_s.at[0])
+    left(wo.at[pl.ds(0, 4)], wg_s.at[1])
+    left(aown.at[pl.ds(0, 7)], h_s.at[0])
+    left(dsend.at[pl.ds(0, 7)], g_s.at[0])
+    for kind, sent in enumerate((sq, su, gu2, gq2)):
+        left(sent.at[pl.ds(0, 7)], aq_s.at[kind])
+    left(vecf.at[pl.ds(0, 7)], v_s.at[0])
+    left(vs.at[pl.ds(0, 7)], v_s.at[1])
+    left(ztr, y_s.at[0])
+    left(vzr, y_s.at[1])
     for moved in (w_out_z, w_qkv_z, w_up_z, w_down_z):
         weight_sent(*moved)
-    for moved in (g_down_z, g_up_z, g_qkv_z):
+    for moved in (g_down_z, g_up_z, g_qkv_z, g_out_z):
         grad_sent(*moved)
-    direct_sent(*g_out_z)
     for n in range(10):
         deliver(n).wait()
 
@@ -1340,14 +1280,14 @@
         V((PLANE, 16, 128), BF16),
         V((16, width), F32),
         V((4, BLOCK, width), BF16),
-        V((2, 4, BLOCK, 256), BF16),
+        V((4, 2 * BLOCK, 256), BF16),
         V((1024, 256), BF16),
         V((128, 1024), BF16),
         V((1024, 128), BF16),
         V((128, 1024), BF16),
-        V((2, 4, 1024, BLOCK), BF16),
+        V((4, 1024, 2 * BLOCK), BF16),
         V((4, 128, BLOCK), F32),
-        V((4, 2, 8, BLOCK), F32),
+        V((4, 8, 2 * BLOCK), F32),
         V((4, BLOCK, 128), BF16),
         V((PLANE, ROWS, 128), BF16),
         V((PLANE, ROWS, 128), BF16),
@@ -1360,6 +1300,7 @@
         V((1024, 512), BF16),
         V((ROWS, width), F32),
         V((ROWS, width), F32),
+        V((512, width), F32),
         V((3, 4, 2, 2, HALF, width), BF16),
         V((3, 4, 2, HALF, width), BF16),
         V((3, 4, 2, HALF, width), BF16),
@@ -1376,6 +1317,7 @@
         V((128, width), BF16),
         V((PLANE, 32, 512), BF16),
         V((PLANE, 32, 384), BF16),
+        V((32, width), BF16),
         V((PLANE, 32, 512), BF16),
         V((PLANE, 32, 384), BF16),
         V((PLANE, 32, 512), BF16),
@@ -1388,11 +1330,11 @@
         V((16, 128), F32),
         V((3, 16, 128), F32),
         dma((8,)), dma((10,)),
-        dma((4, 2, 2)), dma((4, 2, 2)), dma((4, 2)), dma((4, 2)), dma((4, 4)), dma((4, 4)),
-        dma((4, 7)), dma((4, 7)), dma((2, 7)), dma((2, 7)),
-        dma((2, 3)), dma((2, 3)), dma((9, 4)), dma((9, 4)), dma((3,)),
-        dma((3, 4)), dma((3, 4)), dma((3, 2)), dma((3, 2)), dma((3, 2, 2)), dma((3, 2, 2)),
-        dma((4, 4)), dma((4, 4)), dma((4, 2, 2)), dma((4, 2, 2)), dma((4, 2, 2)), dma((4, 2, 2)),
+        dma((4,)), dma((4, 2)), dma((4,)), dma((4,)), dma((4, 4)),
+        dma((4,)), dma((4,)), dma((2,)), dma((2,)), dma((2,)), dma((2,)),
+        dma((4,)), dma((4, 2)), dma((4,)), dma((4, 5)),
+        dma((3,)), dma((3, 4)), dma((3,)), dma((3,)), dma((3,)),
+        dma((2,)), dma((4,)), dma((1,)), dma((1,)), dma((1,)), dma((4,)),
     ]
     results = pl.pallas_call(
         plane_kernel,

time: 124 us -> 116 us (0.935)
  Pallas kernels: 123 us -> 115 us
    pallas_call x1, Pallas kernels: 120 us -> 112 us  [plane_body(): pl.pallas_call(plane_kernel, out_shape=out_shape, in_specs=[pl.BlockSpec(...]
where the time goes in v4:
time: 116 us
  Pallas kernels  115 us (99%)
  between operations  1.3 us (1%)
    pallas_call x1, Pallas kernels, plane_body(): pl.pallas_call(plane_kernel, out_shape=out_shape, in_specs=[pl.BlockSpec(...  112 us
    pallas_call x1, Pallas kernels, plane_body(): pl.pallas_call(hand_over, out_shape=out_shape, in_specs=[anywhere] * len(...  2.52 us

profile of v4, /device:TPU:0, one launch (start us, length us, event | category | flops | bytes accessed | tf_op | source)
XLA Modules:
  0.0 116.1 jit_solution(11241042647663733268)
XLA Ops:
  1.3 112.3 %shard_map.195 = (bf16[128,1024]{1,0:T(8,128)(2,1)}, bf16[128,1024]{1,0:T(8,128)(2,1)}, f32[32,3072]{1,0:T(8,128)}, f32[32,1024]{1,0:T(8,128)}, f32[32,4096]{1,0...) custom-call(s32[1]{0:T(128)S(6)} %copy.22.lead_ref, ...), custom_call_target="tpu_custom_call" | custom-call | tf_op jit(solution)/shard_map/pallas_call | solution.py:1339
  113.6 2.5 %shard_map.196 = (bf16[128,1024]{1,0:T(8,128)(2,1)}, bf16[128,1024]{1,0:T(8,128)(2,1)}, f32[32,3072]{1,0:T(8,128)}, f32[32,1024]{1,0:T(8,128)}, f32[32,4096]{1,0...) custom-call(bf16[128,1024]{1,0:T(8,128)(2,1)} %get-tuple-element.30., ...), custom_call_target="tpu_custom_call" | custom-call | tf_op jit(solution)/shard_map/pallas_call | solution.py:1352

commit v5 on v4

--- a/solution.py
+++ b/solution.py
@@ -285,7 +285,7 @@
     wqkv, wup, vcol, vec_in,
     agf, wq, wo, wu, wd, sq, su, ztr, vt, vecf, vrow,
     normed, qaug, kaug, kt, vv, vt2, pst, ot, invl, att, aown, dsend, dob, gproj, dk, dv,
-    hid, gder, gpre, mid, gmid, gdf,
+    hid, gder, gpre, mid, gmid, gdf, sct,
     part, pr, cs, au, rr,
     gds, gus, gqs, gos, gdr, gur, gqr, gor_, gda, guc, gqc, goc, gu2, gq2, gua, gqa, goa,
     acc, gub, vs, vsr, vz, vzr,
@@ -383,7 +383,7 @@
         return rc(region(s), region(s), w_s.at[kind], w_r.at[kind, role], b, to)
 
     def weight_hand(kind, region, pieces):
-        return rc(region(far), region(far), w_s.at[kind], w_r.at[kind, 1], b, 3 * (s - 1))
+        return rc(region(far), region(far), w_s.at[kind], w_r.at[kind, 2], b, 3 * (s - 1))
 
     def weight_start(*moved):
         @pl.when(s == 1)
@@ -392,13 +392,17 @@
 
         weight_copy(*moved, 0, far).start()
 
-        @pl.when(s < DEPTH - 1)
+        @pl.when(ends)
+        def _():
+            weight_copy(*moved, 1, 1 + s // 3).start()
+
+        @pl.when(s == 2)
         def _():
             weight_copy(*moved, 1, s + 1).start()
 
-        @pl.when(s > 1)
-        def _():
-            weight_copy(*moved, 1, s - 1).start()
+        @pl.when(inner)
+        def _():
+            weight_copy(*moved, 2, DEPTH - 1 - s).start()
 
     def weight_pass(kind, region, pieces):
         @pl.when(inner)
@@ -406,12 +410,19 @@
             landed(region(far), w_r.at[kind, 0])
             weight_hand(kind, region, pieces).start()
 
-    def weight_finish(kind, region, pieces):
-        landed(pieces(2), w_r.at[kind, 1])
+    def weight_most(kind, region, pieces):
+        landed(region(DEPTH - 1 - far), w_r.at[kind, 1])
 
         @pl.when(ends)
         def _():
             landed(region(far), w_r.at[kind, 0])
+
+    def weight_last(kind, region, pieces):
+        landed(region(DEPTH - 1 - s), w_r.at[kind, 2])
+
+    def weight_finish(*moved):
+        weight_most(*moved)
+        weight_last(*moved)
 
     def weight_sent(kind, region, pieces):
         @pl.when(ends)
@@ -714,13 +725,26 @@
     norm_block(2)
     weight_finish(*w_out_z)
     rows_start()
+    landed(su.at[pl.ds(0, 7)], aq_r.at[1])
+
+    @pl.when(inner)
+    def _():
+        weight_copy(*w_up_z, 1, 3 * (s - 1)).start()
+
     arrive(0, 3)
     share(0, 3).wait_recv()
+    @pl.when(ends)
+    def _():
+        weight_start(*w_up_z)
+
     norm_block(3)
 
-    landed(su.at[pl.ds(0, 7)], aq_r.at[1])
     weight_finish(*w_qkv_z)
-    weight_start(*w_up_z)
+    @pl.when(inner)
+    def _():
+        weight_copy(*w_up_z, 0, far).start()
+        weight_copy(*w_up_z, 2, DEPTH - 1 - s).start()
+
 
     def project_block(q, _):
         rows = pl.ds(pl.multiple_of(q * BLOCK, BLOCK), BLOCK)
@@ -858,8 +882,6 @@
     landed(wo.at[0], wg_r.at[2])
     rows_share(3).start()
     arrive(1, 1)
-    for r in (1, 2):
-        gather(1, r, 1).start()
     for h in (0, 1):
         top = pl.multiple_of((h * 2 + c) * HALF, HALF)
         aown[b, h * HALF:(h + 1) * HALF] = att[0, pl.ds(top, HALF), :]
@@ -884,14 +906,16 @@
 
     lax.fori_loop(0, ROWS // INNER, middle_chunk, 0)
     start_gather(2)
-    arrive(1, 2)
     arrive(1, 3)
-
-    weight_finish(*w_up_z)
+    arrive(2, 1)
+    for r in (1, 2):
+        gather(1, r, 1).start()
 
     @pl.when(ends)
     def _():
         weight_start(*w_down_z)
+
+    weight_finish(*w_up_z)
 
     bias = jnp.concatenate([mine[11 + j:12 + j, :] for j in range(4)], axis=1)
 
@@ -899,20 +923,21 @@
         for blk in range(4):
             @pl.when(i == blk)
             def _():
-                arrive(op, blk)
+                if blk != 1:
+                    arrive(op, blk)
                 share(op, blk).wait_recv()
 
     def down_grad_first(f, _):
         cols = pl.ds(pl.multiple_of(f * BLOCK, BLOCK), BLOCK)
         gdf[pl.ds(pl.multiple_of(f * BLOCK, BLOCK), BLOCK), :] = mm(
-            hid[:3 * BLOCK, cols], agf[1, 0:3].reshape(3 * BLOCK, width), TN
+            hid[:2 * BLOCK, cols], agf[1, 0:2].reshape(2 * BLOCK, width), TN
         )
         return 0
 
     def up_block(i, _):
         @pl.when(i == 3)
         def _():
-            for blk in range(3):
+            for blk in range(2):
                 share(1, blk).wait_recv()
             lax.fori_loop(0, 2, down_grad_first, 0)
 
@@ -927,11 +952,15 @@
 
     lax.fori_loop(0, 4, up_block, 0)
     weight_pass(*w_down_z)
+    arrive(1, 2)
+    share(1, 2).wait_recv()
     share(1, 3).wait_recv()
 
     def down_grad(f, _):
         cols = pl.ds(pl.multiple_of(f * BLOCK, BLOCK), BLOCK)
-        g = gdf[pl.ds(pl.multiple_of(f * BLOCK, BLOCK), BLOCK), :] + mm(hid[3 * BLOCK:, cols], block(1, 3), TN)
+        g = gdf[pl.ds(pl.multiple_of(f * BLOCK, BLOCK), BLOCK), :] + mm(
+            hid[2 * BLOCK:, cols], agf[1, 2:4].reshape(2 * BLOCK, width), TN
+        )
         gds[pl.ds(2 * f, 2)] = g.astype(BF16).reshape(2, 128, width)
         return 0
 
@@ -945,17 +974,46 @@
             if i != j:
                 normed[j, :, i * BLOCK:(i + 1) * BLOCK] = normed[i, :, j * BLOCK:(j + 1) * BLOCK].T
             normed[i, :, j * BLOCK:(j + 1) * BLOCK] = upper
+    def turn_second(i, _):
+        cols = pl.ds(pl.multiple_of(i * BLOCK, BLOCK), BLOCK)
+        blk = block(2, i)
+        for f in range(4):
+            sct[f, :, cols] = blk[:, f * BLOCK:(f + 1) * BLOCK].T
+        return 0
+
+    lax.fori_loop(0, 4, turn_second, 0)
+
+    def even_out(n, _):
+        i = n // 4
+        rows = pl.ds(pl.multiple_of((n % 4) * BLOCK, BLOCK), BLOCK)
+        pst[i, rows, :] = (pst[i, rows, :].astype(F32) * invl[i, 0:1, :]).astype(BF16)
+        return 0
+
+    lax.fori_loop(0, 16, even_out, 0)
+
+    left(wo.at[pl.ds(0, 3)], wg_s.at[0])
+    left(wo.at[pl.ds(0, 4)], wg_s.at[1])
+    weight_sent(*w_out_z)
+
+    def wo_block(i, j):
+        return wo[2 * i:2 * i + 2, :, j * BLOCK:(j + 1) * BLOCK].reshape(BLOCK, BLOCK)
+
+    for i in range(4):
+        for j in range(i + 1):
+            upper = wo_block(j, i).T.reshape(2, ROWS, BLOCK)
+            if i != j:
+                wo[2 * j:2 * j + 2, :, i * BLOCK:(i + 1) * BLOCK] = wo_block(i, j).T.reshape(2, ROWS, BLOCK)
+            wo[2 * i:2 * i + 2, :, j * BLOCK:(j + 1) * BLOCK] = upper
     weight_finish(*w_down_z)
     gub[...] = jnp.zeros_like(gub)
 
     def back_block(n, _):
         i = 3 - n
         rows = pl.ds(pl.multiple_of(i * BLOCK, BLOCK), BLOCK)
-        gh = mm(block(1, i), wd[...].reshape(512, width), NT)
-        gp = (gder[i] * gh).astype(BF16)
+        gp = (gder[i] * mm(block(1, i), wd[...].reshape(512, width), NT)).astype(BF16)
+        put_part(0, i, mm(gp, wu[...].reshape(width, 512), NT))
         gpre[rows, :] = gp
         gub[...] += jnp.sum(gp.astype(F32).reshape(BLOCK // 8, 8, 512), axis=0)
-        put_part(0, i, mm(gp, wu[...].reshape(width, 512), NT))
         fold_before(0, i)
         return 0
 
@@ -963,20 +1021,19 @@
     fold(0, 0)
 
     def up_grad(f, _):
-        cols = pl.ds(pl.multiple_of(f * BLOCK, BLOCK), BLOCK)
-        g = mm(agf[2, :, :, :, :, cols].reshape(1024, BLOCK), gpre[...], TN)
-        gus[pl.ds(2 * f, 2)] = g.astype(BF16).reshape(2, 4, 32, 512)
+        g = mm(sct[pl.ds(2 * f, 2)].reshape(2 * BLOCK, 1024), gpre[...])
+        gus[pl.ds(4 * f, 4)] = g.astype(BF16).reshape(4, 4, 32, 512)
         return 0
 
     grad_pass(*g_down_z)
-    lax.fori_loop(0, 4, up_grad, 0)
+    lax.fori_loop(0, 2, up_grad, 0)
     grad_start(*g_up_z)
 
     def out_block(n, _):
         i = 3 - n
         rows = pl.ds(pl.multiple_of(i * BLOCK, BLOCK), BLOCK)
         put_part(1, i, mm(hid[rows, :], wd[...].reshape(512, width)))
-        fold_before(1, i, near_too=False)
+        fold_before(1, i)
         return 0
 
     send_last(0)
@@ -1007,14 +1064,12 @@
         set_rows(3, j, gb)
         add_row(1, gs * xhat)
         add_row(6, gs)
-        add_row(5, gb.astype(F32))
-        add_row(7, ct)
         return 0
 
     grad_pass_on(*g_down_z)
     lax.fori_loop(0, ROWS // INNER, second_chunk, 0)
     gbo = agf[3, 0, :, c].reshape(ROWS, width)
-    gha = mm(gbo, wo[...].reshape(1024, width), NT).astype(BF16)
+    gha = mm(gbo, wo[...].reshape(width, 1024)).astype(BF16)
     for d in range(PLANE):
         dsend[d] = gha[:, d * 128:(d + 1) * 128]
     for i, a in GRANULES:
@@ -1035,30 +1090,30 @@
             def _():
                 landed(dob.at[blk] if blk else dob.at[0, :, 0], g_r.at[blk])
 
-        dot_t = dob[i].reshape(BLOCK, 128).astype(F32).T
-        inv = jnp.concatenate(
-            [jnp.broadcast_to(invl[i, 0:1, h * BLOCK:(h + 1) * BLOCK], (64, BLOCK)) for h in range(2)], axis=0
-        )
-        dos = dot_t * inv
-        prod = dos * ot[i]
-        deltas = [jnp.sum(prod[h * 64:(h + 1) * 64], axis=0, keepdims=True) for h in range(2)]
-        do_rows = dos.T
+        do_rows = dob[i].reshape(BLOCK, 128)
+        do_cols = do_rows.T.astype(F32)
+        prod = do_cols * ot[i]
+        delta = jnp.concatenate(
+            [jnp.sum(prod[h * 64:(h + 1) * 64], axis=0, keepdims=True) for h in range(2)], axis=1
+        )
         zero = jnp.zeros((64, BLOCK), F32)
-        dq_parts = []
-        for h in range(2):
-            halves = [dos[0:64], zero] if h == 0 else [zero, dos[64:128]]
-            dp = mm(vv[...], jnp.concatenate(halves, axis=0).astype(BF16))
-            pb = pst[i, :, h * BLOCK:(h + 1) * BLOCK]
-            ds = (pb.astype(F32) * (dp - deltas[h])).astype(BF16)
-            dv[...] += mm(pb, (do_rows * head_lane[h]).astype(BF16))
-            dk[...] += mm(ds, qaug[i, h * BLOCK:(h + 1) * BLOCK, 0:128])
-            dq_parts.append(mm(kt[h * 64:(h + 1) * 64, :], ds))
-        dq = jnp.concatenate(dq_parts, axis=0).T * 0.125
+        spread_cols = jnp.concatenate([
+            jnp.concatenate([do_cols[0:64], zero], axis=0),
+            jnp.concatenate([zero, do_cols[64:128]], axis=0),
+        ], axis=1).astype(BF16)
+        spread_rows = jnp.concatenate(
+            [(do_rows.astype(F32) * head_lane[h]).astype(BF16) for h in range(2)], axis=0
+        )
+        pb = pst[i]
+        ds = (pb.astype(F32) * (mm(vv[...], spread_cols) - delta)).astype(BF16)
+        dv[...] += mm(pb, spread_rows)
+        dk[...] += mm(ds, qaug[i, :, 0:128])
+        dq = mm(kt[...], ds)
+        dq = jnp.concatenate([dq[0:64, 0:BLOCK], dq[64:128, BLOCK:]], axis=0).T * 0.125
         gproj[pl.ds(pl.multiple_of(i * BLOCK, BLOCK), BLOCK), 0:128] = dq.astype(BF16)
         return 0
 
     lax.fori_loop(0, 4, attend_back, 0)
-    send_near(1, 2)
     gproj[:, 128:256] = dk[...].astype(BF16)
     gproj[:, 256:384] = dv[...].astype(BF16)
 
@@ -1072,10 +1127,21 @@
         i = 3 - n
         rows = pl.ds(pl.multiple_of(i * BLOCK, BLOCK), BLOCK)
         put_part(2, i, mm(gproj[rows, :], wq[...].reshape(width, 384), NT))
-        fold_before(2, i)
+
+        @pl.when(n == 2)
+        def _():
+            fold(2, 3)
+            send_far(2)
+
+        @pl.when(n == 3)
+        def _():
+            fold(2, 2)
+            send_near(2, 2)
+
         return 0
 
     lax.fori_loop(0, 4, project_back, 0)
+    fold(2, 1)
     fold(2, 0)
     arrive(3, 2)
     share(3, 0).wait_recv()
@@ -1093,8 +1159,8 @@
     lax.fori_loop(0, 4, out_grad, 0)
     gos[...] = goa[...].astype(BF16).reshape(4, 32, width)
     grad_start_some(*g_out_z, 3)
+    grad_start_some(*g_out_z, 2)
     grad_start_some(*g_qkv_z, 1)
-    grad_start_some(*g_out_z, 2)
     grad_start_some(*g_out_z, 1)
     down_half(1)
     send_last(2)
@@ -1105,6 +1171,12 @@
 
     grad_pass(*g_out_z)
     grad_pass_on(*g_qkv_z)
+    def own_sums(j, _):
+        add_row(5, own_rows(3, j))
+        add_row(7, own_rows(1, j))
+        return 0
+
+    lax.fori_loop(0, ROWS // INNER, own_sums, 0)
     wait_sums(2)
 
     def first_chunk(j, _):
@@ -1150,16 +1222,6 @@
         swap(2, k, gu2.at[peer(k)], gua.at[b]).start()
     gua[b] = gu2[b]
     grad_pass_on(*g_out_z)
-    wait_sums(1)
-
-    def output_chunk(j, _):
-        rows = pl.ds(pl.multiple_of(j * INNER, INNER), INNER)
-        out_o[rows, :] = (mid[rows, :] + plane_total(1, j) + shift_down).astype(BF16)
-        return 0
-
-    lax.fori_loop(0, ROWS // INNER, output_chunk, 0)
-    deliver(0).start()
-
     landed(vs.at[pl.ds(0, 7)], v_r.at[1])
     total = vs[b] + extra
     for k in range(PLANE - 1):
@@ -1167,6 +1229,16 @@
     vz[...] = total
     for k in range(1, DEPTH):
         yc(1, k, vz, vzr.at[k - 1]).start()
+
+    wait_sums(1)
+
+    def output_chunk(j, _):
+        rows = pl.ds(pl.multiple_of(j * INNER, INNER), INNER)
+        out_o[rows, :] = (mid[rows, :] + plane_total(1, j) + shift_down).astype(BF16)
+        return 0
+
+    lax.fori_loop(0, ROWS // INNER, output_chunk, 0)
+    deliver(0).start()
 
     grad_finish(*g_qkv_z)
     for d in range(PLANE):
@@ -1208,8 +1280,6 @@
         left(agf.at[op, :, :, 0], fw_s.at[op])
     for op in range(3):
         end_sums(op)
-    left(wo.at[pl.ds(0, 3)], wg_s.at[0])
-    left(wo.at[pl.ds(0, 4)], wg_s.at[1])
     left(aown.at[pl.ds(0, 7)], h_s.at[0])
     left(dsend.at[pl.ds(0, 7)], g_s.at[0])
     for kind, sent in enumerate((sq, su, gu2, gq2)):
@@ -1218,7 +1288,7 @@
     left(vs.at[pl.ds(0, 7)], v_s.at[1])
     left(ztr, y_s.at[0])
     left(vzr, y_s.at[1])
-    for moved in (w_out_z, w_qkv_z, w_up_z, w_down_z):
+    for moved in (w_qkv_z, w_up_z, w_down_z):
         weight_sent(*moved)
     for moved in (g_down_z, g_up_z, g_qkv_z, g_out_z):
         grad_sent(*moved)
@@ -1301,6 +1371,7 @@
         V((ROWS, width), F32),
         V((ROWS, width), F32),
         V((512, width), F32),
+        V((4, BLOCK, 1024), BF16),
         V((3, 4, 2, 2, HALF, width), BF16),
         V((3, 4, 2, HALF, width), BF16),
         V((3, 4, 2, HALF, width), BF16),
@@ -1332,7 +1403,7 @@
         dma((8,)), dma((10,)),
         dma((4,)), dma((4, 2)), dma((4,)), dma((4,)), dma((4, 4)),
         dma((4,)), dma((4,)), dma((2,)), dma((2,)), dma((2,)), dma((2,)),
-        dma((4,)), dma((4, 2)), dma((4,)), dma((4, 5)),
+        dma((4,)), dma((4, 3)), dma((4,)), dma((4, 5)),
         dma((3,)), dma((3, 4)), dma((3,)), dma((3,)), dma((3,)),
         dma((2,)), dma((4,)), dma((1,)), dma((1,)), dma((1,)), dma((4,)),
     ]

time: 116 us -> 115 us (level)
  Pallas kernels: 115 us -> 113 us
    pallas_call x1, Pallas kernels: 112 us -> 111 us  [plane_body(): pl.pallas_call(plane_kernel, out_shape=out_shape, in_specs=[pl.BlockSpec(...]
where the time goes in v5:
time: 115 us
  Pallas kernels  113 us (98%)
  between operations  1.3 us (1%)
    pallas_call x1, Pallas kernels, plane_body(): pl.pallas_call(plane_kernel, out_shape=out_shape, in_specs=[pl.BlockSpec(...  111 us
    pallas_call x1, Pallas kernels, plane_body(): pl.pallas_call(hand_over, out_shape=out_shape, in_specs=[anywhere] * len(...  2.52 us

profile of v5, /device:TPU:0, one launch (start us, length us, event | category | flops | bytes accessed | tf_op | source)
XLA Modules:
  0.0 114.7 jit_solution(15782676988555414233)
XLA Ops:
  1.3 110.9 %shard_map.195 = (bf16[128,1024]{1,0:T(8,128)(2,1)}, bf16[128,1024]{1,0:T(8,128)(2,1)}, f32[32,3072]{1,0:T(8,128)}, f32[32,1024]{1,0:T(8,128)}, f32[32,4096]{1,0...) custom-call(s32[1]{0:T(128)S(6)} %copy.22.lead_ref, ...), custom_call_target="tpu_custom_call" | custom-call | tf_op jit(solution)/shard_map/pallas_call | solution.py:1410
  112.2 2.5 %shard_map.196 = (bf16[128,1024]{1,0:T(8,128)(2,1)}, bf16[128,1024]{1,0:T(8,128)(2,1)}, f32[32,3072]{1,0:T(8,128)}, f32[32,1024]{1,0:T(8,128)}, f32[32,4096]{1,0...) custom-call(bf16[128,1024]{1,0:T(8,128)(2,1)} %get-tuple-element.30., ...), custom_call_target="tpu_custom_call" | custom-call | tf_op jit(solution)/shard_map/pallas_call | solution.py:1423

commit v6 on v5

--- a/solution.py
+++ b/solution.py
@@ -283,14 +283,14 @@
     out_h, ig_h, gqkv_h, gout_h, gup_h, gdown_h, gain_h, shift_h, lead_h, bias_h,
     out_o, ig_o, gqkv_o, gout_o, gup_o, gdown_o, gain_o, shift_o, lead_o, bias_o,
     wqkv, wup, vcol, vec_in,
-    agf, wq, wo, wu, wd, sq, su, ztr, vt, vecf, vrow,
-    normed, qaug, kaug, kt, vv, vt2, pst, ot, invl, att, aown, dsend, dob, gproj, dk, dv,
+    agf, tokown, gbown, wq, wo, wu, wd, sq, su, ztr, vt, vecf, vrow,
+    normed, qaug, kaug, kt, vv, vt2, pst, ot, invl, att, aown, dsend, dob, gsend, gcol, gproj, dk, dv,
     hid, gder, gpre, mid, gmid, gdf, sct,
     part, pr, cs, au, rr,
-    gds, gus, gqs, gos, gdr, gur, gqr, gor_, gda, guc, gqc, goc, gu2, gq2, gua, gqa, goa,
+    gds, gus, gqs, gos, gdr, gur, gqr, gor_, gda, guc, gqc, goc, go2, go3, gu2, gq2, gua, gqa,
     acc, gub, vs, vsr, vz, vzr,
     in_s, out_s, ag_s, ag_r, ac_r, fw_s, fw_r, aq_s, aq_r, v_s, v_r, y_s, y_r, w_s, w_r, z_s, z_r,
-    p_s, p_r, f_r, n_s, n_r, wg_s, wg_r, h_s, h_r, g_s, g_r,
+    p_s, p_r, f_r, n_s, n_r, wg_s, wg_r, h_s, h_r, g_s, g_r, gc_s, gc_r,
 ):
     b = lax.axis_index("band")
     s = lax.axis_index("samp")
@@ -540,23 +540,23 @@
     g_down_z = (0, lambda t: gds.at[t], lambda t: gdr.at[t], gda, lambda n: gds.at[pl.ds(0, n)])
     g_up_z = (1, lambda t: gus.at[:, t], lambda t: gur.at[t], guc, lambda n: gus.at[:, pl.ds(0, n)])
     g_qkv_z = (2, lambda t: gqs.at[:, t], lambda t: gqr.at[t], gqc, lambda n: gqs.at[:, pl.ds(0, n)])
-    g_out_z = (3, lambda t: gos.at[t], lambda t: gor_.at[t], goc, lambda n: gos.at[pl.ds(0, n)])
+    g_out_z = (3, lambda t: gos.at[:, t], lambda t: gor_.at[t], goc, lambda n: gos.at[:, pl.ds(0, n)])
 
     def gather(op, r, turn):
         return rc(
-            agf.at[op, 0, (turn + r) % 2, c], agf.at[op, 1 + turn, r - 1, c],
+            agf.at[op % 3, 0, (turn + r) % 2, c], agf.at[op % 3, 1 + turn, r - 1, c],
             ag_s.at[op], ag_r.at[op, turn], near(r), s,
         )
 
     def across(op, r):
         return rc(
-            agf.at[op, 1, r - 1, c], agf.at[op, 3, r % 2, c],
+            agf.at[op % 3, 1, r - 1, c], agf.at[op % 3, 3, r % 2, c],
             ag_s.at[op], ac_r.at[op], near(3 - r), s,
         )
 
     def share(op, blk):
         return rc(
-            agf.at[op, blk, :, c], agf.at[op, blk, :, c],
+            agf.at[op % 3, blk, :, c], agf.at[op % 3, blk, :, c],
             fw_s.at[op], fw_r.at[op, blk], mate, s,
         )
 
@@ -568,14 +568,18 @@
 
     def arrive(op, blk):
         if blk in (1, 2):
-            landed(agf.at[op, blk, :, c], ag_r.at[op, blk - 1])
+            landed(agf.at[op % 3, blk, :, c], ag_r.at[op, blk - 1])
         if blk == 1:
             for r in (1, 2):
                 across(op, r).start()
         if blk == 3:
-            landed(agf.at[op, 3, :, c], ac_r.at[op])
+            landed(agf.at[op % 3, 3, :, c], ac_r.at[op])
         if blk:
             share(op, blk).start()
+
+    def gathered(op):
+        left(agf.at[op % 3, pl.ds(0, 3), :, 0], ag_s.at[op])
+        left(agf.at[op % 3, :, :, 0], fw_s.at[op])
 
     def block(op, i):
         return agf[op, i].reshape(BLOCK, -1)
@@ -623,6 +627,14 @@
         return rc(
             dsend.at[dev, pl.ds(h * HALF, HALF)], dob.at[i, a, c],
             g_s.at[0], g_r.at[i], dev, s,
+        )
+
+    def branch_copy(i, a, k):
+        r, h = granule(i, a)
+        dev = chip(r) * 2 + k
+        return rc(
+            gsend.at[dev, pl.ds(h * HALF, HALF)], gcol.at[i, a, c],
+            gc_s.at[0], gc_r.at[0], dev, s,
         )
 
     def swap(kind, k, src, dst):
@@ -837,11 +849,16 @@
 
     def own_rows(op, j):
         h, rows = place(j)
-        return agf[op, 0, h, c, rows, :].astype(F32)
+        kept = {0: tokown, 3: gbown}.get(op)
+        v = agf[op, 0, h, c, rows, :] if kept is None else kept[h, rows, :]
+        return v.astype(F32)
 
     def set_rows(op, j, v):
         h, rows = place(j)
-        agf[op, 0, h, c, rows, :] = v
+        if op == 3:
+            gbown[h, rows, :] = v
+        else:
+            agf[op, 0, h, c, rows, :] = v
 
     def end_sums(op):
         left(part.at[op, :, :, 0], p_s.at[op])
@@ -875,6 +892,8 @@
 
         return 0
 
+    tokown[...] = agf[0, 0, :, c]
+    gathered(0)
     landed(wo.at[0], wg_r.at[0])
     for r in (1, 2):
         rows_across(r).start()
@@ -896,6 +915,7 @@
     landed(aown.at[pl.ds(0, 7)], h_r.at[0])
     heads = jnp.concatenate([aown[d] for d in range(PLANE)], axis=1)
     mid[...] = mm(heads, wo[...].reshape(1024, width))
+    agf[0, 0, :, c] = heads.reshape(2, HALF, width)
 
     def middle_chunk(j, _):
         rows = pl.ds(pl.multiple_of(j * INNER, INNER), INNER)
@@ -910,6 +930,7 @@
     arrive(2, 1)
     for r in (1, 2):
         gather(1, r, 1).start()
+    start_gather(3)
 
     @pl.when(ends)
     def _():
@@ -1004,8 +1025,11 @@
             if i != j:
                 wo[2 * j:2 * j + 2, :, i * BLOCK:(i + 1) * BLOCK] = wo_block(i, j).T.reshape(2, ROWS, BLOCK)
             wo[2 * i:2 * i + 2, :, j * BLOCK:(j + 1) * BLOCK] = upper
+    arrive(3, 1)
+    arrive(3, 2)
     weight_finish(*w_down_z)
     gub[...] = jnp.zeros_like(gub)
+    arrive(3, 3)
 
     def back_block(n, _):
         i = 3 - n
@@ -1017,6 +1041,7 @@
         fold_before(0, i)
         return 0
 
+    grad_pass(*g_down_z)
     lax.fori_loop(0, 4, back_block, 0)
     fold(0, 0)
 
@@ -1025,7 +1050,6 @@
         gus[pl.ds(4 * f, 4)] = g.astype(BF16).reshape(4, 4, 32, 512)
         return 0
 
-    grad_pass(*g_down_z)
     lax.fori_loop(0, 2, up_grad, 0)
     grad_start(*g_up_z)
 
@@ -1033,10 +1057,11 @@
         i = 3 - n
         rows = pl.ds(pl.multiple_of(i * BLOCK, BLOCK), BLOCK)
         put_part(1, i, mm(hid[rows, :], wd[...].reshape(512, width)))
-        fold_before(1, i)
+        fold_before(1, i, near_too=False)
         return 0
 
     send_last(0)
+    grad_pass_on(*g_down_z)
     lax.fori_loop(0, 4, out_block, 0)
     fold(1, 0)
 
@@ -1066,9 +1091,8 @@
         add_row(6, gs)
         return 0
 
-    grad_pass_on(*g_down_z)
     lax.fori_loop(0, ROWS // INNER, second_chunk, 0)
-    gbo = agf[3, 0, :, c].reshape(ROWS, width)
+    gbo = gbown[...].reshape(ROWS, width)
     gha = mm(gbo, wo[...].reshape(width, 1024)).astype(BF16)
     for d in range(PLANE):
         dsend[d] = gha[:, d * 128:(d + 1) * 128]
@@ -1077,12 +1101,17 @@
             back_copy(i, a, k).start()
     for h in (0, 1):
         dob[0, h, c] = dsend[b, h * HALF:(h + 1) * HALF, :]
-    start_gather(3)
+    for d in range(PLANE):
+        gsend[d] = gbo[:, d * 128:(d + 1) * 128]
+    for i, a in GRANULES:
+        for k in cores(i):
+            branch_copy(i, a, k).start()
+    for h in (0, 1):
+        gcol[0, h, c] = gsend[b, h * HALF:(h + 1) * HALF, :]
 
     grad_pass(*g_up_z)
     dk[...] = jnp.zeros_like(dk)
     dv[...] = jnp.zeros_like(dv)
-    goa[...] = jnp.zeros_like(goa)
 
     def attend_back(i, _):
         for blk in range(4):
@@ -1117,53 +1146,42 @@
     gproj[:, 128:256] = dk[...].astype(BF16)
     gproj[:, 256:384] = dv[...].astype(BF16)
 
+    put_part(2, 3, mm(gproj[3 * BLOCK:, :], wq[...].reshape(width, 384), NT))
     gqs[...] = mm(normed[...].reshape(1024, 1024), gproj[...]).astype(BF16).reshape(8, 4, 32, 384)
     grad_start_some(*g_qkv_z, 3)
     grad_start_some(*g_qkv_z, 2)
+    fold(2, 3)
+    send_far(2)
     grad_pass_on(*g_up_z)
-    arrive(3, 1)
 
     def project_back(n, _):
-        i = 3 - n
+        i = 2 - n
         rows = pl.ds(pl.multiple_of(i * BLOCK, BLOCK), BLOCK)
         put_part(2, i, mm(gproj[rows, :], wq[...].reshape(width, 384), NT))
 
-        @pl.when(n == 2)
-        def _():
-            fold(2, 3)
-            send_far(2)
-
-        @pl.when(n == 3)
+        @pl.when(n == 1)
         def _():
             fold(2, 2)
             send_near(2, 2)
 
         return 0
 
-    lax.fori_loop(0, 4, project_back, 0)
+    lax.fori_loop(0, 3, project_back, 0)
     fold(2, 1)
     fold(2, 0)
-    arrive(3, 2)
-    share(3, 0).wait_recv()
-    arrive(3, 3)
     grad_pass(*g_qkv_z)
-    def out_grad(i, _):
-        for blk in (1, 2, 3):
-            @pl.when(i == blk)
-            def _():
-                share(3, blk).wait_recv()
-
-        goa[...] += mm(att[i], block(3, i), TN)
-        return 0
-
-    lax.fori_loop(0, 4, out_grad, 0)
-    gos[...] = goa[...].astype(BF16).reshape(4, 32, width)
+    for i in range(4):
+        share(3, i).wait_recv()
+    landed(aown.at[pl.ds(0, 7)], gc_r.at[0])
+    gos[...] = mm(gcol[...].reshape(1024, 128), agf[0].reshape(1024, width), TN).T.astype(BF16).reshape(
+        PLANE, DEPTH, 32, 128
+    )
     grad_start_some(*g_out_z, 3)
     grad_start_some(*g_out_z, 2)
     grad_start_some(*g_qkv_z, 1)
     grad_start_some(*g_out_z, 1)
-    down_half(1)
     send_last(2)
+    send_near(1, 2)
     send_last(1)
 
     def others(kind, stage, got, via, pieces):
@@ -1229,16 +1247,7 @@
     vz[...] = total
     for k in range(1, DEPTH):
         yc(1, k, vz, vzr.at[k - 1]).start()
-
-    wait_sums(1)
-
-    def output_chunk(j, _):
-        rows = pl.ds(pl.multiple_of(j * INNER, INNER), INNER)
-        out_o[rows, :] = (mid[rows, :] + plane_total(1, j) + shift_down).astype(BF16)
-        return 0
-
-    lax.fori_loop(0, ROWS // INNER, output_chunk, 0)
-    deliver(0).start()
+    down_half(1)
 
     grad_finish(*g_qkv_z)
     for d in range(PLANE):
@@ -1249,8 +1258,23 @@
         swap(3, k, gq2.at[peer(k)], gqa.at[b]).start()
     gqa[b] = gq2[b]
     grad_finish(*g_out_z)
-    gout_o[...] = sum([t[...].astype(F32) for t in others(*g_out_z)], gos[s].astype(F32))
-    deliver(3).start()
+    for d in range(PLANE):
+        go2[d] = sum(
+            [t[d].astype(F32) for t in others(*g_out_z)], gos[d, s].astype(F32)
+        ).astype(BF16)
+    for k in range(1, PLANE):
+        swap(4, k, go2.at[peer(k)], go3.at[b]).start()
+    go3[b] = go2[b]
+    wait_sums(1)
+
+    def output_chunk(j, _):
+        rows = pl.ds(pl.multiple_of(j * INNER, INNER), INNER)
+        out_o[rows, :] = (mid[rows, :] + plane_total(1, j) + shift_down).astype(BF16)
+        return 0
+
+    lax.fori_loop(0, ROWS // INNER, output_chunk, 0)
+    deliver(0).start()
+
     grad_finish(*g_down_z)
     gdown_o[...] = sum([t[...].astype(F32) for t in others(*g_down_z)], gds[s].astype(F32))
     deliver(5).start()
@@ -1267,6 +1291,10 @@
     bias_o[...] = jnp.sum(jnp.where(line == 11 + s, vz_sum, 0.0), axis=0, keepdims=True)
     for n in range(6, 10):
         deliver(n).start()
+    landed(go2.at[pl.ds(0, 7)], aq_r.at[4])
+    for d in range(PLANE):
+        gout_o[:, d * 128:(d + 1) * 128] = go3[d].astype(F32)
+    deliver(3).start()
     landed(gq2.at[pl.ds(0, 7)], aq_r.at[3])
     for d in range(PLANE):
         for j in range(3):
@@ -1275,14 +1303,14 @@
             )
 
     deliver(2).start()
-    for op in range(4):
-        left(agf.at[op, pl.ds(0, 3), :, 0], ag_s.at[op])
-        left(agf.at[op, :, :, 0], fw_s.at[op])
+    for op in (1, 2, 3):
+        gathered(op)
     for op in range(3):
         end_sums(op)
     left(aown.at[pl.ds(0, 7)], h_s.at[0])
     left(dsend.at[pl.ds(0, 7)], g_s.at[0])
-    for kind, sent in enumerate((sq, su, gu2, gq2)):
+    left(gsend.at[pl.ds(0, 7)], gc_s.at[0])
+    for kind, sent in enumerate((sq, su, gu2, gq2, go2)):
         left(sent.at[pl.ds(0, 7)], aq_s.at[kind])
     left(vecf.at[pl.ds(0, 7)], v_s.at[0])
     left(vs.at[pl.ds(0, 7)], v_s.at[1])
@@ -1338,7 +1366,8 @@
         V((2, 32), F32), V((6, 32), F32), V((2, 32), F32), V((1, 128), F32),
         V((32, 3 * width), BF16), V((32, 4 * width), BF16),
         V((16, 128), F32), V((2, 16, 128), BF16),
-        V((4, 4, 2, 2, HALF, width), BF16),
+        V((3, 4, 2, 2, HALF, width), BF16),
+        V((2, HALF, width), BF16), V((2, HALF, width), BF16),
         V((PLANE, DEPTH, 32, 384), BF16),
         V((PLANE, 128, width), BF16),
         V((PLANE, DEPTH, 32, 512), BF16),
@@ -1362,6 +1391,8 @@
         V((PLANE, ROWS, 128), BF16),
         V((PLANE, ROWS, 128), BF16),
         V((4, 2, 2, HALF, 128), BF16),
+        V((PLANE, ROWS, 128), BF16),
+        V((4, 2, 2, HALF, 128), BF16),
         V((1024, 384), BF16),
         V((1024, 128), F32),
         V((1024, 128), F32),
@@ -1380,20 +1411,20 @@
         V((DEPTH, 128, width), BF16),
         V((PLANE, DEPTH, 32, 512), BF16),
         V((PLANE, DEPTH, 32, 384), BF16),
-        V((DEPTH, 32, width), BF16),
+        V((PLANE, DEPTH, 32, 128), BF16),
         V((DEPTH, 128, width), BF16),
         V((DEPTH, PLANE, 32, 512), BF16),
         V((DEPTH, PLANE, 32, 384), BF16),
-        V((DEPTH, 32, width), BF16),
+        V((DEPTH, PLANE, 32, 128), BF16),
         V((128, width), BF16),
         V((PLANE, 32, 512), BF16),
         V((PLANE, 32, 384), BF16),
-        V((32, width), BF16),
+        V((PLANE, 32, 128), BF16),
+        V((PLANE, 32, 128), BF16), V((PLANE, 32, 128), BF16),
         V((PLANE, 32, 512), BF16),
         V((PLANE, 32, 384), BF16),
         V((PLANE, 32, 512), BF16),
         V((PLANE, 32, 384), BF16),
-        V((128, width), F32),
         V((10, 8, width), F32),
         V((8, 512), F32),
         V((PLANE, 16, 128), F32),
@@ -1402,10 +1433,10 @@
         V((3, 16, 128), F32),
         dma((8,)), dma((10,)),
         dma((4,)), dma((4, 2)), dma((4,)), dma((4,)), dma((4, 4)),
-        dma((4,)), dma((4,)), dma((2,)), dma((2,)), dma((2,)), dma((2,)),
+        dma((5,)), dma((5,)), dma((2,)), dma((2,)), dma((2,)), dma((2,)),
         dma((4,)), dma((4, 3)), dma((4,)), dma((4, 5)),
         dma((3,)), dma((3, 4)), dma((3,)), dma((3,)), dma((3,)),
-        dma((2,)), dma((4,)), dma((1,)), dma((1,)), dma((1,)), dma((4,)),
+        dma((2,)), dma((4,)), dma((1,)), dma((1,)), dma((1,)), dma((4,)), dma((1,)), dma((1,)),
     ]
     results = pl.pallas_call(
         plane_kernel,

time: 115 us -> 115 us (level)
  no operation moved by 1% of the time
where the time goes in v6:
time: 115 us; the launch traced here: 114 us
  Pallas kernels  113 us (98%)
  between operations  1.3 us (1%)
    pallas_call x1, Pallas kernels, plane_body(): pl.pallas_call(plane_kernel, out_shape=out_shape, in_specs=[pl.BlockSpec(...  111 us
    pallas_call x1, Pallas kernels, plane_body(): pl.pallas_call(hand_over, out_shape=out_shape, in_specs=[anywhere] * len(...  2.52 us

profile of v6, /device:TPU:0, one launch (start us, length us, event | category | flops | bytes accessed | tf_op | source)
XLA Modules:
  0.0 114.4 jit_solution(709916144310741372)
XLA Ops:
  1.3 110.6 %shard_map.195 = (bf16[128,1024]{1,0:T(8,128)(2,1)}, bf16[128,1024]{1,0:T(8,128)(2,1)}, f32[32,3072]{1,0:T(8,128)}, f32[32,1024]{1,0:T(8,128)}, f32[32,4096]{1,0...) custom-call(s32[1]{0:T(128)S(6)} %copy.22.lead_ref, ...), custom_call_target="tpu_custom_call" | custom-call | tf_op jit(solution)/shard_map/pallas_call | solution.py:1441
  111.9 2.5 %shard_map.196 = (bf16[128,1024]{1,0:T(8,128)(2,1)}, bf16[128,1024]{1,0:T(8,128)(2,1)}, f32[32,3072]{1,0:T(8,128)}, f32[32,1024]{1,0:T(8,128)}, f32[32,4096]{1,0...) custom-call(bf16[128,1024]{1,0:T(8,128)(2,1)} %get-tuple-element.30., ...), custom_call_target="tpu_custom_call" | custom-call | tf_op jit(solution)/shard_map/pallas_call | solution.py:1454

commit v7 on v6

--- a/solution.py
+++ b/solution.py
@@ -655,6 +655,8 @@
         su[d] = wup[:, d * 512:(d + 1) * 512]
     wu[b, s] = su[b]
 
+    landed(sq.at[pl.ds(0, 7)], aq_r.at[0])
+    weight_start(*w_qkv_z)
     landed(ztr, y_r.at[0])
     vt[...] = (
         vec_in[0].astype(F32) + vec_in[1].astype(F32)
@@ -670,8 +672,6 @@
         gather(0, r, 1).start()
     share(0, 0).start()
     vecf[b] = vt[...]
-    landed(sq.at[pl.ds(0, 7)], aq_r.at[0])
-    weight_start(*w_qkv_z)
     for k in range(1, PLANE):
         swap(1, k, su.at[peer(k)], wu.at[b, s]).start()
     arrive(0, 1)

time: 115 us -> 114 us (level)
  no operation moved by 1% of the time
where the time goes in v7:
time: 114 us
  Pallas kernels  113 us (99%)
  between operations  1.3 us (1%)
    pallas_call x1, Pallas kernels, plane_body(): pl.pallas_call(plane_kernel, out_shape=out_shape, in_specs=[pl.BlockSpec(...  110 us
    pallas_call x1, Pallas kernels, plane_body(): pl.pallas_call(hand_over, out_shape=out_shape, in_specs=[anywhere] * len(...  2.52 us

profile of v7, /device:TPU:0, one launch (start us, length us, event | category | flops | bytes accessed | tf_op | source)
XLA Modules:
  0.0 114.1 jit_solution(5861995165920179223)
XLA Ops:
  1.3 110.3 %shard_map.195 = (bf16[128,1024]{1,0:T(8,128)(2,1)}, bf16[128,1024]{1,0:T(8,128)(2,1)}, f32[32,3072]{1,0:T(8,128)}, f32[32,1024]{1,0:T(8,128)}, f32[32,4096]{1,0...) custom-call(s32[1]{0:T(128)S(6)} %copy.22.lead_ref, ...), custom_call_target="tpu_custom_call" | custom-call | tf_op jit(solution)/shard_map/pallas_call | solution.py:1441
  111.6 2.5 %shard_map.196 = (bf16[128,1024]{1,0:T(8,128)(2,1)}, bf16[128,1024]{1,0:T(8,128)(2,1)}, f32[32,3072]{1,0:T(8,128)}, f32[32,1024]{1,0:T(8,128)}, f32[32,4096]{1,0...) custom-call(bf16[128,1024]{1,0:T(8,128)(2,1)} %get-tuple-element.30., ...), custom_call_target="tpu_custom_call" | custom-call | tf_op jit(solution)/shard_map/pallas_call | solution.py:1454

commit v8 on v7

--- a/solution.py
+++ b/solution.py
@@ -528,7 +528,7 @@
                (gain_o, gain_h), (shift_o, shift_h), (lead_o, lead_h), (bias_o, bias_h))
 
     def deliver(n):
-        return pltpu.make_async_copy(results[n][0], results[n][1], out_s.at[n])
+        return pltpu.make_async_copy(results[n][0], results[n][1], (in_s.at[n] if n < 8 else out_s.at[n - 8]))
 
     w_out_z = (
         0, lambda t: wo.at[b, pl.ds(pl.multiple_of(t * 32, 32), 32)],
@@ -1431,7 +1431,7 @@
         V((PLANE - 1, 16, 128), F32),
         V((16, 128), F32),
         V((3, 16, 128), F32),
-        dma((8,)), dma((10,)),
+        dma((8,)), dma((2,)),
         dma((4,)), dma((4, 2)), dma((4,)), dma((4,)), dma((4, 4)),
         dma((5,)), dma((5,)), dma((2,)), dma((2,)), dma((2,)), dma((2,)),
         dma((4,)), dma((4, 3)), dma((4,)), dma((4, 5)),

time: 114 us -> 114 us (level)
  no operation moved by 1% of the time
where the time goes in v8:
time: 114 us
  Pallas kernels  113 us (99%)
  between operations  1.3 us (1%)
    pallas_call x1, Pallas kernels, plane_body(): pl.pallas_call(plane_kernel, out_shape=out_shape, in_specs=[pl.BlockSpec(...  110 us
    pallas_call x1, Pallas kernels, plane_body(): pl.pallas_call(hand_over, out_shape=out_shape, in_specs=[anywhere] * len(...  2.52 us

profile of v8, /device:TPU:0, one launch (start us, length us, event | category | flops | bytes accessed | tf_op | source)
XLA Modules:
  0.0 114.1 jit_solution(10271408328866334678)
XLA Ops:
  1.3 110.2 %shard_map.195 = (bf16[128,1024]{1,0:T(8,128)(2,1)}, bf16[128,1024]{1,0:T(8,128)(2,1)}, f32[32,3072]{1,0:T(8,128)}, f32[32,1024]{1,0:T(8,128)}, f32[32,4096]{1,0...) custom-call(s32[1]{0:T(128)S(6)} %copy.22.lead_ref, ...), custom_call_target="tpu_custom_call" | custom-call | tf_op jit(solution)/shard_map/pallas_call | solution.py:1441
  111.5 2.5 %shard_map.196 = (bf16[128,1024]{1,0:T(8,128)(2,1)}, bf16[128,1024]{1,0:T(8,128)(2,1)}, f32[32,3072]{1,0:T(8,128)}, f32[32,1024]{1,0:T(8,128)}, f32[32,4096]{1,0...) custom-call(bf16[128,1024]{1,0:T(8,128)(2,1)} %get-tuple-element.30., ...), custom_call_target="tpu_custom_call" | custom-call | tf_op jit(solution)/shard_map/pallas_call | solution.py:1454
